TPU v7x, 32 devices: a whole 2x2x4 slice. The times are simulated.
32 devices in a mesh: dp: 8 (over y, x, core), seq: 4 (over z).
Axes of the slice: x: 2, y: 2, z: 4, core: 2. Of those that a mesh axis runs over, the one named last changes fastest.
Arguments:
- image_tokens: bfloat16 [8, 1024, 1536], P('dp', 'seq'), may hold values from -6 to 6
- text_tokens: bfloat16 [8, 308, 1536], P('dp', 'seq'), may hold values from -6 to 6
- text_lengths: int32 [8, 4], P('dp', 'seq'), may hold values from 1 to 77, 154 in all within a row
- conditioning: bfloat16 [8, 1536], P('dp'), may hold values from -6 to 6
- ada_weight: bfloat16 [1536, 2, 9216], P('dp', None, 'seq'), may hold values from -0.15625 to 0.15625
- ada_bias: bfloat16 [2, 9216], P(None, 'seq'), may hold values from -3 to 3
- qkv_weight: bfloat16 [1536, 2, 3, 1536], P('dp', None, None, 'seq'), may hold values from -1 to 1
- qv_bias: bfloat16 [2, 2, 1536], P(None, None, 'seq'), may hold values from -3 to 3
- proj_weight: bfloat16 [1536, 2, 1536], P('seq', None, 'dp'), may hold values from -1.75 to 1.75
- proj_bias: bfloat16 [2, 1536], P(None, 'seq'), may hold values from -3 to 3
- fc1_weight: bfloat16 [1536, 2, 6144], P('dp', None, 'seq'), may hold values from -0.15625 to 0.15625
- fc1_bias: bfloat16 [2, 6144], P(None, 'seq'), may hold values from -3 to 3
- fc2_weight: bfloat16 [6144, 2, 1536], P('seq', None, 'dp'), may hold values from -0.078125 to 0.078125
- fc2_bias: bfloat16 [2, 1536], P(None, 'seq'), may hold values from -3 to 3
- image_cotangent: bfloat16 [8, 1024, 1536], P('dp', 'seq'), may hold values from -6 to 6
- text_cotangent: bfloat16 [8, 308, 1536], P('dp', 'seq'), may hold values from -6 to 6
Outputs:
- image_out: bfloat16 [8, 1024, 1536], P('dp', 'seq')
- text_out: bfloat16 [8, 308, 1536], P('dp', 'seq')
- image_grad: float32 [8, 1024, 1536], P('dp', 'seq')
- text_grad: float32 [8, 308, 1536], P('dp', 'seq')
- cond_grad: float32 [8, 1536], P('dp')
- ada_weight_grad: float32 [1536, 2, 9216], P('dp', None, 'seq')
- ada_bias_grad: float32 [2, 9216], P(None, 'seq')
- qkv_weight_grad: float32 [1536, 2, 3, 1536], P('dp', None, None, 'seq')
- qv_bias_grad: float32 [2, 2, 1536], P(None, None, 'seq')
- proj_weight_grad: float32 [1536, 2, 1536], P('seq', None, 'dp')
- proj_bias_grad: float32 [2, 1536], P(None, 'seq')
- fc1_weight_grad: float32 [1536, 2, 6144], P('dp', None, 'seq')
- fc1_bias_grad: float32 [2, 6144], P(None, 'seq')
- fc2_weight_grad: float32 [6144, 2, 1536], P('seq', None, 'dp')
- fc2_bias_grad: float32 [2, 1536], P(None, 'seq')
Inputs may be any that keep to these rules, and one draw needn't show every extreme that they name: The first text_lengths slots of a device's 77 are live; the live slots of one sequence add up to 154, and in each sequence some device has all 77 live.
All inputs are finite; a program needn't handle non-finite values.
Results may differ from a plain program's by a relative error of at most 0.025.
The roundings to bfloat16 on the way count: a program that leaves them out, or rounds other values in their place, can miss the bound.
Values may be sent and summed in bfloat16 or wider, within the bound.
A program may use at most 320 MiB of HBM per device.

v0:
```python
import math

import jax
import jax.numpy as jnp
from jax import lax
from jax.sharding import PartitionSpec as P

HD = 64


EPSILON = 1e-06
GELU_ROOT = math.sqrt(2.0 / math.pi)
GELU_CUBE = 0.044715
MASKED = -1e30
SINGLE = jnp.float32
HALF = jnp.bfloat16


def layer_norm(values):
    center = values - jnp.mean(values, axis=-1, keepdims=True)
    inv_std = lax.rsqrt(jnp.mean(center * center, axis=-1, keepdims=True) + EPSILON)
    return (center * inv_std, inv_std)


def norm_back(normed, inv_std, upstream):
    first = jnp.mean(upstream, axis=-1, keepdims=True)
    second = jnp.mean(upstream * normed, axis=-1, keepdims=True)
    return inv_std * (upstream - first - normed * second)


def gelu_tanh(values):
    inner = GELU_ROOT * (values + GELU_CUBE * values * values * values)
    return 0.5 * values * (1.0 + jnp.tanh(inner))


def gelu_slope(values):
    inner = GELU_ROOT * (values + GELU_CUBE * values * values * values)
    tangent = jnp.tanh(inner)
    return 0.5 * (1.0 + tangent) + 0.5 * values * (1.0 - tangent * tangent) * GELU_ROOT * (
        1.0 + 3.0 * GELU_CUBE * values * values
    )


def silu_slope(values):
    sigma = jax.nn.sigmoid(values)
    return sigma + values * sigma * (1.0 - sigma)


def column(shifts, position):
    return shifts[:, position][:, None, :]


def attend(queries, key_rows, value_rows, live_keys):
    score_scale = 1.0 / math.sqrt(queries.shape[-1])
    scores = (
        jnp.einsum("qhd,khd->hqk", queries, key_rows, preferred_element_type=SINGLE) * score_scale
    )
    scores = jnp.where(live_keys[None, None, :], scores, MASKED)
    maxima = jnp.max(scores, axis=-1, keepdims=True)
    raised = jnp.exp(scores - maxima)
    totals = jnp.sum(raised, axis=-1, keepdims=True)
    weights = (raised / totals).astype(HALF)
    mixture = jnp.einsum("hqk,khd->qhd", weights, value_rows, preferred_element_type=SINGLE).astype(
        HALF
    )
    return (mixture, (maxima + jnp.log(totals))[..., 0])


def attend_back(queries, key_rows, value_rows, mixture, grad_mix, log_total, live_keys):
    score_scale = 1.0 / math.sqrt(queries.shape[-1])
    scores = (
        jnp.einsum("qhd,khd->hqk", queries, key_rows, preferred_element_type=SINGLE) * score_scale
    )
    scores = jnp.where(live_keys[None, None, :], scores, MASKED)
    probs = jnp.exp(scores - log_total[..., None])
    prob_half = probs.astype(HALF)
    grad_prob = jnp.einsum("qhd,khd->hqk", grad_mix, value_rows, preferred_element_type=SINGLE)
    offset = jnp.sum(grad_mix.astype(SINGLE) * mixture.astype(SINGLE), axis=-1).T
    grad_score = (probs * (grad_prob - offset[:, :, None]) * score_scale).astype(HALF)
    grad_query = jnp.einsum("hqk,khd->qhd", grad_score, key_rows, preferred_element_type=SINGLE)
    grad_key = jnp.einsum("hqk,qhd->khd", grad_score, queries, preferred_element_type=SINGLE)
    grad_value = jnp.einsum("hqk,qhd->khd", prob_half, grad_mix, preferred_element_type=SINGLE)
    return (grad_query, grad_key, grad_value)


def gather_rows(pair):
    return (
        lax.all_gather(pair[0], "seq", axis=1, tiled=True),
        lax.all_gather(pair[1], "seq", axis=1, tiled=True),
    )


def sum_rows(pair):
    return (
        lax.psum_scatter(pair[0], "seq", scatter_dimension=1, tiled=True),
        lax.psum_scatter(pair[1], "seq", scatter_dimension=1, tiled=True),
    )


def gather_grads(pair):
    return (
        lax.all_gather(pair[0], "seq", axis=1, tiled=True),
        lax.all_gather(pair[1], "seq", axis=1, tiled=True),
    )


def sum_grads(pair):
    return (
        lax.psum_scatter(pair[0], "seq", scatter_dimension=1, tiled=True),
        lax.psum_scatter(pair[1], "seq", scatter_dimension=1, tiled=True),
    )


def body(
    image_tokens,
    text_tokens,
    text_lengths,
    conditioning,
    ada_weight,
    ada_bias,
    qkv_weight,
    qv_bias,
    proj_weight,
    proj_bias,
    fc1_weight,
    fc1_bias,
    fc2_weight,
    fc2_bias,
    image_cotangent,
    text_cotangent,
):
    groups = image_tokens.shape[0]
    slots = text_tokens.shape[1]
    width = image_tokens.shape[2]
    seq_count = lax.axis_size("seq")
    image_all = image_tokens.shape[1] * seq_count
    local_width = qkv_weight.shape[3]
    head_local = local_width // HD
    gathered = (
        lax.all_gather(ada_weight, "dp", axis=0, tiled=True),
        lax.all_gather(qkv_weight, "dp", axis=0, tiled=True),
        lax.all_gather(proj_weight, "dp", axis=2, tiled=True),
        lax.all_gather(fc1_weight, "dp", axis=0, tiled=True),
        lax.all_gather(fc2_weight, "dp", axis=2, tiled=True),
    )
    ada_full, qkv_full, proj_full, fc1_full, fc2_full = gathered
    cond_float = conditioning.astype(SINGLE)
    cond_act = jax.nn.silu(cond_float).astype(HALF)
    mod_local = (
        jnp.einsum("gd,dtc->gtc", cond_act, ada_full, preferred_element_type=SINGLE)
        + ada_bias.astype(SINGLE)[None]
    )
    mod_all, proj_shift, fc2_shift, lengths_all = (
        lax.all_gather(mod_local, "seq", axis=2, tiled=True),
        lax.all_gather(proj_bias.astype(SINGLE), "seq", axis=1, tiled=True),
        lax.all_gather(fc2_bias.astype(SINGLE), "seq", axis=1, tiled=True),
        lax.all_gather(text_lengths.astype(SINGLE), "seq", axis=1, tiled=True),
    )
    mod_all = mod_all.reshape(groups, 2, 6, width)
    slot_iota = jnp.arange(slots, dtype=jnp.int32)
    live_local = (slot_iota[None, :] < text_lengths).astype(SINGLE)[:, :, None]
    slot_float = jnp.arange(slots, dtype=SINGLE)
    live_text = (slot_float[None, None, :] < lengths_all[:, :, None]).reshape(
        groups, seq_count * slots
    )
    live_keys = jnp.concatenate([jnp.ones((groups, image_all), jnp.bool_), live_text], axis=1)
    residual_in = (image_tokens.astype(SINGLE), text_tokens.astype(SINGLE))
    row_masks = (jnp.ones((1, 1, 1), SINGLE), live_local)
    cotangents = (image_cotangent, text_cotangent)
    first_norm = []
    attn_local = []
    for stream in range(2):
        shifts = mod_all[:, stream]
        normed, inv_std = layer_norm(residual_in[stream])
        first_norm.append((normed, inv_std))
        attn_local.append((normed * (1.0 + column(shifts, 1)) + column(shifts, 0)).astype(HALF))
    attn_inputs = gather_rows((attn_local[0], attn_local[1]))
    qkv_rows = []
    for stream in range(2):
        projected = jnp.einsum(
            "grd,dch->grch", attn_inputs[stream], qkv_full[:, stream], preferred_element_type=SINGLE
        )
        bias_rows = jnp.stack(
            [
                qv_bias[stream, 0].astype(SINGLE),
                jnp.zeros((local_width,), SINGLE),
                qv_bias[stream, 1].astype(SINGLE),
            ]
        )
        qkv_rows.append((projected + bias_rows).astype(HALF))
    joint_rows = jnp.concatenate(qkv_rows, axis=1).reshape(groups, -1, 3, head_local, HD)
    mixture, log_total = lax.map(
        lambda packed: attend(packed[0][:, 0], packed[0][:, 1], packed[0][:, 2], packed[1]),
        (joint_rows, live_keys),
    )
    mixture_rows = mixture.reshape(groups, -1, local_width)
    mix_parts = (mixture_rows[:, :image_all], mixture_rows[:, image_all:])
    attn_partial = []
    for stream in range(2):
        attn_partial.append(
            jnp.einsum(
                "grc,ce->gre",
                mix_parts[stream],
                proj_full[:, stream],
                preferred_element_type=SINGLE,
            )
        )
    attn_sums = sum_rows((attn_partial[0], attn_partial[1]))
    attn_outs = []
    middles = []
    second_norm = []
    mlp_local = []
    for stream in range(2):
        shifts = mod_all[:, stream]
        attn_out = attn_sums[stream] + proj_shift[stream]
        middle = residual_in[stream] + column(shifts, 2) * attn_out
        normed_two, inv_two = layer_norm(middle)
        attn_outs.append(attn_out)
        middles.append(middle)
        second_norm.append((normed_two, inv_two))
        mlp_local.append((normed_two * (1.0 + column(shifts, 4)) + column(shifts, 3)).astype(HALF))
    mlp_inputs = gather_rows((mlp_local[0], mlp_local[1]))
    pre_acts = []
    hiddens = []
    mlp_partial = []
    for stream in range(2):
        pre_act = jnp.einsum(
            "grd,dh->grh", mlp_inputs[stream], fc1_full[:, stream], preferred_element_type=SINGLE
        ) + fc1_bias[stream].astype(SINGLE)
        hidden = gelu_tanh(pre_act).astype(HALF)
        pre_acts.append(pre_act)
        hiddens.append(hidden)
        mlp_partial.append(
            jnp.einsum("grh,he->gre", hidden, fc2_full[:, stream], preferred_element_type=SINGLE)
        )
    mlp_sums = sum_rows((mlp_partial[0], mlp_partial[1]))
    block_outs = []
    mlp_outs = []
    for stream in range(2):
        shifts = mod_all[:, stream]
        mlp_out = mlp_sums[stream] + fc2_shift[stream]
        mlp_outs.append(mlp_out)
        block_outs.append(
            ((middles[stream] + column(shifts, 5) * mlp_out) * row_masks[stream]).astype(HALF)
        )
    regathered = (
        lax.all_gather(ada_weight, "dp", axis=0, tiled=True),
        lax.all_gather(qkv_weight, "dp", axis=0, tiled=True),
        lax.all_gather(proj_weight, "dp", axis=2, tiled=True),
        lax.all_gather(fc1_weight, "dp", axis=0, tiled=True),
        lax.all_gather(fc2_weight, "dp", axis=2, tiled=True),
    )
    ada_back, qkv_back, proj_back, fc1_back, fc2_back = regathered
    upstreams = []
    gate_twos = []
    fc2_bias_parts = []
    grad_mlp_local = []
    for stream in range(2):
        shifts = mod_all[:, stream]
        upstream = cotangents[stream].astype(SINGLE) * row_masks[stream]
        grad_mlp_full = column(shifts, 5) * upstream
        upstreams.append(upstream)
        gate_twos.append(jnp.sum(upstream * mlp_outs[stream], axis=1))
        fc2_bias_parts.append(jnp.sum(grad_mlp_full, axis=(0, 1)))
        grad_mlp_local.append(grad_mlp_full.astype(HALF))
    grad_mlp_all = gather_grads((grad_mlp_local[0], grad_mlp_local[1]))
    fc2_grads = []
    fc1_grads = []
    fc1_bias_grads = []
    mlp_in_partial = []
    for stream in range(2):
        fc2_grads.append(
            jnp.einsum(
                "grh,gre->he", hiddens[stream], grad_mlp_all[stream], preferred_element_type=SINGLE
            )
        )
        grad_hidden = jnp.einsum(
            "gre,he->grh", grad_mlp_all[stream], fc2_back[:, stream], preferred_element_type=SINGLE
        ) * gelu_slope(pre_acts[stream])
        fc1_bias_grads.append(jnp.sum(grad_hidden, axis=(0, 1)))
        grad_hidden_half = grad_hidden.astype(HALF)
        fc1_grads.append(
            jnp.einsum(
                "grd,grh->dh", mlp_inputs[stream], grad_hidden_half, preferred_element_type=SINGLE
            )
        )
        mlp_in_partial.append(
            jnp.einsum(
                "grh,dh->grd", grad_hidden_half, fc1_back[:, stream], preferred_element_type=SINGLE
            )
        )
    fc1_stack = jnp.stack(fc1_grads, axis=1)
    fc2_stack = jnp.stack(fc2_grads, axis=1)
    grad_mlp_in = sum_grads((mlp_in_partial[0], mlp_in_partial[1]))
    scale_twos = []
    shift_twos = []
    grad_middles = []
    gate_ones = []
    proj_bias_parts = []
    grad_attn_local = []
    for stream in range(2):
        shifts = mod_all[:, stream]
        normed_two, inv_two = second_norm[stream]
        scale_twos.append(jnp.sum(grad_mlp_in[stream] * normed_two, axis=1))
        shift_twos.append(jnp.sum(grad_mlp_in[stream], axis=1))
        grad_middle = upstreams[stream] + norm_back(
            normed_two, inv_two, grad_mlp_in[stream] * (1.0 + column(shifts, 4))
        )
        grad_middles.append(grad_middle)
        grad_attn_full = column(shifts, 2) * grad_middle
        gate_ones.append(jnp.sum(grad_middle * attn_outs[stream], axis=1))
        proj_bias_parts.append(jnp.sum(grad_attn_full, axis=(0, 1)))
        grad_attn_local.append(grad_attn_full.astype(HALF))
    grad_attn_all = gather_grads((grad_attn_local[0], grad_attn_local[1]))
    proj_grads = []
    grad_mix_parts = []
    for stream in range(2):
        proj_grads.append(
            jnp.einsum(
                "grc,gre->ce",
                mix_parts[stream],
                grad_attn_all[stream],
                preferred_element_type=SINGLE,
            )
        )
        grad_mix_parts.append(
            jnp.einsum(
                "gre,ce->grc",
                grad_attn_all[stream],
                proj_back[:, stream],
                preferred_element_type=SINGLE,
            ).astype(HALF)
        )
    grad_mix = jnp.concatenate(grad_mix_parts, axis=1).reshape(groups, -1, head_local, HD)
    grad_query, grad_key, grad_value = lax.map(
        lambda packed: attend_back(
            packed[0][:, 0],
            packed[0][:, 1],
            packed[0][:, 2],
            packed[1],
            packed[2],
            packed[3],
            packed[4],
        ),
        (joint_rows, mixture, grad_mix, log_total, live_keys),
    )
    grad_joint = jnp.stack([grad_query, grad_key, grad_value], axis=2).reshape(
        groups, -1, 3, local_width
    )
    joint_parts = (grad_joint[:, :image_all], grad_joint[:, image_all:])
    qv_grads = []
    qkv_grads = []
    attn_in_partial = []
    for stream in range(2):
        rows_grad = joint_parts[stream]
        qv_grads.append(
            jnp.stack(
                [jnp.sum(rows_grad[:, :, 0], axis=(0, 1)), jnp.sum(rows_grad[:, :, 2], axis=(0, 1))]
            )
        )
        rows_half = rows_grad.astype(HALF)
        qkv_grads.append(
            jnp.einsum(
                "grd,grch->dch", attn_inputs[stream], rows_half, preferred_element_type=SINGLE
            )
        )
        attn_in_partial.append(
            jnp.einsum(
                "grch,dch->grd", rows_half, qkv_back[:, stream], preferred_element_type=SINGLE
            )
        )
    grad_attn_in = sum_grads((attn_in_partial[0], attn_in_partial[1]))
    input_grads = []
    mod_parts = []
    for stream in range(2):
        shifts = mod_all[:, stream]
        normed, inv_std = first_norm[stream]
        scale_one = jnp.sum(grad_attn_in[stream] * normed, axis=1)
        shift_one = jnp.sum(grad_attn_in[stream], axis=1)
        input_grads.append(
            (
                grad_middles[stream]
                + norm_back(normed, inv_std, grad_attn_in[stream] * (1.0 + column(shifts, 1)))
            )
            * row_masks[stream]
        )
        mod_parts.append(
            jnp.stack(
                [
                    shift_one,
                    scale_one,
                    gate_ones[stream],
                    shift_twos[stream],
                    scale_twos[stream],
                    gate_twos[stream],
                ],
                axis=1,
            )
        )
    mod_grad_part = jnp.stack(mod_parts, axis=1).reshape(groups, 2, 6 * width)
    mod_grad, proj_bias_grad, fc2_bias_grad = (
        lax.psum_scatter(
            mod_grad_part.astype(jnp.bfloat16), "seq", scatter_dimension=2, tiled=True
        ).astype(jnp.float32),
        lax.psum_scatter(
            jnp.stack(proj_bias_parts).astype(jnp.bfloat16), "seq", scatter_dimension=1, tiled=True
        ).astype(jnp.float32),
        lax.psum_scatter(
            jnp.stack(fc2_bias_parts).astype(jnp.bfloat16), "seq", scatter_dimension=1, tiled=True
        ).astype(jnp.float32),
    )
    mod_half = mod_grad.astype(HALF)
    ada_grad_part = jnp.einsum("gd,gtc->dtc", cond_act, mod_half, preferred_element_type=SINGLE)
    ada_bias_part = jnp.sum(mod_grad, axis=0)
    cond_part = jnp.einsum("gtc,dtc->gd", mod_half, ada_back, preferred_element_type=SINGLE)
    cond_grad = lax.psum(cond_part, "seq") * silu_slope(cond_float)
    qkv_stack = jnp.stack(qkv_grads, axis=1)
    proj_stack = jnp.stack(proj_grads, axis=1)
    weight_grads = (
        lax.psum_scatter(
            ada_grad_part.astype(jnp.bfloat16), "dp", scatter_dimension=0, tiled=True
        ).astype(jnp.float32),
        lax.psum_scatter(
            qkv_stack.astype(jnp.bfloat16), "dp", scatter_dimension=0, tiled=True
        ).astype(jnp.float32),
        lax.psum_scatter(
            proj_stack.astype(jnp.bfloat16), "dp", scatter_dimension=2, tiled=True
        ).astype(jnp.float32),
        lax.psum_scatter(
            fc1_stack.astype(jnp.bfloat16), "dp", scatter_dimension=0, tiled=True
        ).astype(jnp.float32),
        lax.psum_scatter(
            fc2_stack.astype(jnp.bfloat16), "dp", scatter_dimension=2, tiled=True
        ).astype(jnp.float32),
    )
    bias_grads = lax.psum(
        (
            ada_bias_part,
            jnp.stack(qv_grads),
            proj_bias_grad,
            jnp.stack(fc1_bias_grads),
            fc2_bias_grad,
        ),
        "dp",
    )
    return (
        block_outs[0],
        block_outs[1],
        input_grads[0],
        input_grads[1],
        cond_grad,
        weight_grads[0],
        bias_grads[0],
        weight_grads[1],
        bias_grads[1],
        weight_grads[2],
        bias_grads[2],
        weight_grads[3],
        bias_grads[3],
        weight_grads[4],
        bias_grads[4],
    )


def solution(mesh):
    in_specs = (
        P("dp", "seq", None),
        P("dp", "seq", None),
        P("dp", "seq"),
        P("dp", None),
        P("dp", None, "seq"),
        P(None, "seq"),
        P("dp", None, None, "seq"),
        P(None, None, "seq"),
        P("seq", None, "dp"),
        P(None, "seq"),
        P("dp", None, "seq"),
        P(None, "seq"),
        P("seq", None, "dp"),
        P(None, "seq"),
        P("dp", "seq", None),
        P("dp", "seq", None),
    )
    out_specs = (
        P("dp", "seq", None),
        P("dp", "seq", None),
        P("dp", "seq", None),
        P("dp", "seq", None),
        P("dp", None),
        P("dp", None, "seq"),
        P(None, "seq"),
        P("dp", None, None, "seq"),
        P(None, None, "seq"),
        P("seq", None, "dp"),
        P(None, "seq"),
        P("dp", None, "seq"),
        P(None, "seq"),
        P("seq", None, "dp"),
        P(None, "seq"),
    )
    return jax.shard_map(body, mesh=mesh, in_specs=in_specs, out_specs=out_specs, check_vma=False)
```

profile of v0, /device:TPU:0, one launch (start us, length us, event | category | flops | bytes accessed | tf_op | source)
XLA Modules:
  0.0 2153.2 jit_solution(7594980608853862414)
XLA Ops:
  10.0 81.5 %all-gather.11.cloned.1.call-done = bf16[1536,2,2304]{2,1,0:T(2,128)(2,1)} async-done(((bf16[192,2,2304]{2,1,0:T(2,128)(2,1)}), bf16[1536,2,2304]{2,1,0:T(2,128)(2,1)}) %all-gather.11.cloned.1.call-update) | async-done | bytes 14155792 | tf_op jit(solution)/shard_map/all_gather | solution.py:140
  91.4 35.1 %copy.137 = bf16[1536,2,2304]{0,2,1:T(8,128)(2,1)} copy(bf16[1536,2,2304]{2,1,0:T(2,128)(2,1)} %all-gather.11.cloned.1.call-done) | data formatting | bytes 28311552 | tf_op jit(solution)/shard_map/all_gather | solution.py:140
  167.3 15.3 fusion.130
  182.6 16.9 copy.151
  201.7 42.3 %all_gather.62 = bf16[1,308,1536]{2,0,1:T(2,128)(2,1)S(1)} all-gather(bf16[1,77,1536]{2,0,1:T(2,128)(2,1)S(1)} %get-tuple-element.181), channel_id=1, replica_groups=mesh['dp'=8,'seq'=4] {'seq'}, dimensions={1}, use_global_device_ids=true | all-gather | bytes 1182720 | tf_op jit(solution)/shard_map/all_gather | solution.py:89
  259.0 17.0 fusion.132
  276.0 17.9 fusion
  294.0 18.8 fusion.43
  335.7 92.6 %reduce-scatter.16.cloned.1.call-done = f32[1,256,1536]{2,1,0:T(8,128)} async-done(((f32[1,1024,1536]{2,1,0:T(8,128)}), f32[1,256,1536]{2,1,0:T(8,128)}) %reduce-scatter.16.cloned.1.call-update) | async-done | bytes 1572880 | tf_op jit(solution)/shard_map/reduce_scatter | solution.py:95
  441.8 48.2 %all-gather.21.cloned.1.call-done = bf16[1536,2,1536]{2,0,1:T(8,128)(2,1)} async-done(((bf16[192,2,1536]{2,0,1:T(8,128)(2,1)}), bf16[1536,2,1536]{2,0,1:T(8,128)(2,1)}) %all-gather.21.cloned.1.call-update) | async-done | bytes 9437200 | tf_op jit(solution)/shard_map/all_gather | solution.py:143
  490.0 65.7 %all-gather.19.cloned.1.call-done = bf16[1,1024,1536]{2,1,0:T(8,128)(2,1)} async-done(((bf16[1,256,1536]{2,1,0:T(8,128)(2,1)}), bf16[1,1024,1536]{2,1,0:T(8,128)(2,1)}) %all-gather.19.cloned.1.call-update) | async-done | bytes 3145744 | tf_op jit(solution)/shard_map/all_gather | solution.py:88
  565.5 49.6 %all-gather.23.cloned.1.call-done = bf16[1536,2,1536]{0,2,1:T(8,128)(2,1)} async-done(((bf16[1536,2,192]{0,2,1:T(8,128)(2,1)}), bf16[1536,2,1536]{0,2,1:T(8,128)(2,1)}) %all-gather.23.cloned.1.call-update) | async-done | bytes 9437200 | tf_op jit(solution)/shard_map/all_gather | solution.py:144
  615.1 65.7 %all-gather.25.cloned.1.call-done = bf16[1,1024,1536]{2,1,0:T(8,128)(2,1)} async-done(((bf16[1,256,1536]{2,1,0:T(8,128)(2,1)}), bf16[1,1024,1536]{2,1,0:T(8,128)(2,1)}) %all-gather.25.cloned.1.call-update) | async-done | bytes 3145744 | tf_op jit(solution)/shard_map/all_gather | solution.py:102
  716.8 54.7 %all_gather.74 = bf16[1,308,1536]{2,0,1:T(2,128)(2,1)} all-gather(bf16[1,77,1536]{2,0,1:T(2,128)(2,1)S(1)} %get-tuple-element.173), channel_id=1, replica_groups=mesh['dp'=8,'seq'=4] {'seq'}, dimensions={1}, use_global_device_ids=true | all-gather | bytes 1182720 | tf_op jit(solution)/shard_map/all_gather | solution.py:103
  787.9 65.7 %all_gather.71 = bf16[1,308,1536]{2,0,1:T(2,128)(2,1)S(1)} all-gather(bf16[1,77,1536]{2,0,1:T(2,128)(2,1)S(1)} %get-tuple-element.175), channel_id=1, replica_groups=mesh['dp'=8,'seq'=4] {'seq'}, dimensions={1}, use_global_device_ids=true | all-gather | bytes 1182720 | tf_op jit(solution)/shard_map/all_gather | solution.py:89
  869.9 17.4 all_gather.70
  887.9 36.7 %reduce-scatter.20.cloned.1.call-done = f32[1,256,1536]{2,1,0:T(8,128)} async-done(((f32[1,1024,1536]{2,1,0:T(8,128)}), f32[1,256,1536]{2,1,0:T(8,128)}) %reduce-scatter.20.cloned.1.call-update) | async-done | bytes 1572880 | tf_op jit(solution)/shard_map/reduce_scatter | solution.py:109
  927.7 110.9 %reduce-scatter.18.cloned.1.call-done = f32[1,256,1536]{2,1,0:T(8,128)} async-done(((f32[1,1024,1536]{2,1,0:T(8,128)}), f32[1,256,1536]{2,1,0:T(8,128)}) %reduce-scatter.18.cloned.1.call-update) | async-done | bytes 1572880 | tf_op jit(solution)/shard_map/reduce_scatter | solution.py:95
  1055.4 66.1 %all-reduce.19.cloned.1.call-done = f32[1,308,1536]{2,0,1:T(1,128)} async-done(((f32[1,308,1536]{2,0,1:T(1,128)}), f32[1,308,1536]{2,0,1:T(1,128)}) %all-reduce.19.cloned.1.call-update) | async-done | bytes 1892368
  1129.0 64.5 %all_gather.75 = bf16[1,308,1536]{2,0,1:T(2,128)(2,1)S(1)} all-gather(bf16[1,77,1536]{2,0,1:T(2,128)(2,1)S(1)} %multiply_convert_fusion.6), channel_id=1, replica_groups=mesh['dp'=8,'seq'=4] {'seq'}, dimensions={1}, use_global_device_ids=true | all-gather | bytes 1182720 | tf_op jit(solution)/shard_map/all_gather | solution.py:103
  1196.3 17.5 all-gather.27.cloned.1.call-done
  1218.9 18.7 fusion.2
  1237.6 26.9 %multiply_convert_fusion = bf16[6,1332,1332]{1,2,0:T(8,128)(2,1)} fusion(f32[6,1332,1332]{1,2,0:T(8,128)} %get-tuple-element.204, f32[6,1332]{1,0:T(8,128)S(1)} %bitcast.273, f32[6,1332]{1,0:T(8,128)S(1)} %log_add_fusion, bf16[308,6,64]{0,2,1:T(8,128)(2,1)} %bitcast.267, bf16[1024,6,64]{0,2,1:T(8,128)(2,1)} %bitcast.264, ...), kind=kOutput, calls=%fused_computation | convolution fusion | flops 1419922816 | bytes 68027904 | tf_op jit(solution)/shard_map/while/body/eval_jaxpr/qhd,khd->hqk/dot_general | solution.py:77
  1328.1 118.1 %all-reduce.21.cloned.1.call-done = (f32[1,308,1536]{2,0,1:T(1,128)}, f32[1,308,1536]{2,0,1:T(1,128)}) async-done(((f32[1,308,1536]{2,0,1:T(1,128)}, f32[1,308,1536]{2,0,1:T(1,128)}), (f32[1,308,1536]{2,0,1:T(1,128)}, f32[1,308,1536]{2,0,1:T(1,128)})) %all-reduce.21.cloned.1.call-update) | async-done | bytes 3784720
  1453.7 104.5 %reduce-scatter.22.cloned.1.call-done = f32[1,256,1536]{2,1,0:T(8,128)} async-done(((f32[1,1024,1536]{2,1,0:T(8,128)}), f32[1,256,1536]{2,1,0:T(8,128)}) %reduce-scatter.22.cloned.1.call-update) | async-done | bytes 1572880 | tf_op jit(solution)/shard_map/reduce_scatter | solution.py:109
  1631.7 24.2 %copy.122 = bf16[1536,2,1536]{0,1,2:T(2,128)(2,1)} copy(bf16[1536,2,1536]{2,0,1:T(8,128)(2,1)} %pad_maximum_fusion.1) | data formatting | bytes 18874368 | tf_op jit(solution)/shard_map/stack | solution.py:293
  1668.1 14.5 multiply_convert_fusion.1
  1685.7 36.3 %reduce-scatter.26.cloned.1.call-done = bf16[192,2,1536]{2,0,1:T(8,128)(2,1)} async-done(((bf16[1536,2,1536]{2,0,1:T(8,128)(2,1)}), bf16[192,2,1536]{2,0,1:T(8,128)(2,1)}) %reduce-scatter.26.cloned.1.call-update) | async-done | bytes 1179664 | tf_op jit(solution)/shard_map/reduce_scatter | solution.py:429
  1728.6 16.2 reduce-scatter.32.cloned.1.call-done
  1745.8 66.4 %reduce-scatter.24.cloned.1.call-done = bf16[192,2,3,384]{3,0,2,1:T(8,128)(2,1)} async-done(((bf16[1536,2,3,384]{3,0,2,1:T(8,128)(2,1)}), bf16[192,2,3,384]{3,0,2,1:T(8,128)(2,1)}) %reduce-scatter.24.cloned.1.call-update) | async-done | bytes 884752 | tf_op jit(solution)/shard_map/reduce_scatter | solution.py:423
  1836.1 25.6 %all-reduce.9 = (f32[2,2304]{1,0:T(2,128)}, f32[2,2,384]{2,1,0:T(2,128)}, f32[2,384]{1,0:T(2,128)}, f32[2,1536]{1,0:T(2,128)}, f32[2,384]{1,0:T(2,128)}) all-reduce(f32[2,2304]{1,0:T(2,128)S(1)} %bitcast_convert_fusion, f32[2,2,384]{2,1,0:T(2,128)S(1)} %pad_maximum_fusion.12, ...), channel_id=1, replica_groups=mesh['dp'=8,'seq'=4] {'dp'}, use_global_device_ids=true, to_apply=%region_42.43 | all-reduce | flops 10752 | bytes 82944 | tf_op jit(solution)/shard_map/psum | solution.py:436
  1862.3 273.4 %all-reduce.23.cloned.1.call-done = (bf16[1536,2,2304]{2,1,0:T(2,128)(2,1)}, bf16[384,2,1536]{0,1,2:T(2,128)(2,1)}, bf16[1536,2,1536]{0,1,2:T(2,128)(2,1)}) async-done(((bf16[1536,2,2304]{2,1,0:T(2,128)(2,1)}, bf16[384,2,1536]{0,1,2:T(2,128)(2,1)}, bf16[1536,2,1536]{0,1,2:T(2,128)(2,1)}), (bf16[1536,2,2304]{2,1,0:T(2,128)(2,1)}, bf16[384,2,1536]{0,1,2:T(2,128)(2,1)}, ...) | async-done | bytes 25952272
  (417 shorter events, 410.1 us)
Async XLA Ops:
  7.2 84.2 %all-gather.11.cloned.1.call-start = ((), (), s32[]{:S(2)}) async-start(), calls=%async_computation.9 | async-start | bytes 15925248 | tf_op jit(solution)/shard_map/all_gather | solution.py:140
  7.9 159.4 %all-gather.15.cloned.1.call-start = ((), (), s32[]{:S(2)}) async-start(), calls=%async_computation.11 | async-start | bytes 7962624 | tf_op jit(solution)/shard_map/all_gather | solution.py:141
  8.7 243.4 %all-gather.13.cloned.1.call-start = ((), (), s32[]{:S(2)}) async-start(), calls=%async_computation.10 | async-start | bytes 3932160 | tf_op jit(solution)/shard_map/all_gather | solution.py:88
  8.9 140.2 %copy-start.57 = (f32[256]{0:T(256)}, f32[256]{0:T(256)S(1)}, u32[]{:S(2)}) copy-start(f32[256]{0:T(256)S(1)} %broadcast_multiply_fusion.8) | copy-start | bytes 3076
  9.3 139.8 %copy-start.64 = (f32[256]{0:T(256)}, f32[256]{0:T(256)S(1)}, u32[]{:S(2)}) copy-start(f32[256]{0:T(256)S(1)} %add_rsqrt_fusion.1) | copy-start | bytes 3076
  149.1 284.3 %copy-start.50 = (f32[1536]{0:T(1024)}, f32[1536]{0:T(1024)S(1)}, u32[]{:S(2)}) copy-start(f32[1536]{0:T(1024)S(1)} %get-tuple-element.147) | copy-start | bytes 18436
  150.4 162.4 %all-gather.17.cloned.1.call-start = ((), (), s32[]{:S(2)}) async-start(), calls=%async_computation.12 | async-start | bytes 2654208 | tf_op jit(solution)/shard_map/all_gather | solution.py:142
  151.0 277.3 %reduce-scatter.16.cloned.1.call-start = ((), (), s32[]{:S(2)}) async-start(), calls=%async_computation.13 | async-start | bytes 7864320 | tf_op jit(solution)/shard_map/reduce_scatter | solution.py:95
  318.8 171.2 %all-gather.21.cloned.1.call-start = ((), (), s32[]{:S(2)}) async-start(), calls=%async_computation.15 | async-start | bytes 10616832 | tf_op jit(solution)/shard_map/all_gather | solution.py:143
  321.3 234.4 %all-gather.19.cloned.1.call-start = ((), (), s32[]{:S(2)}) async-start(), calls=%async_computation.14 | async-start | bytes 3932160 | tf_op jit(solution)/shard_map/all_gather | solution.py:88
  432.7 182.4 %all-gather.23.cloned.1.call-start = ((), (), s32[]{:S(2)}) async-start(), calls=%async_computation.16 | async-start | bytes 10616832 | tf_op jit(solution)/shard_map/all_gather | solution.py:144
  433.4 247.3 %all-gather.25.cloned.1.call-start = ((), (), s32[]{:S(2)}) async-start(), calls=%async_computation.18 | async-start | bytes 3932160 | tf_op jit(solution)/shard_map/all_gather | solution.py:102
  435.7 346.8 %all-reduce.17.cloned.1.call-start = ((), (), s32[]{:S(2)}) async-start(), calls=%async_computation.27 | async-start | bytes 3784704
  436.3 265.8 %copy-start.73 = (f32[1536]{0:T(1024)}, f32[1536]{0:T(1024)S(1)}, u32[]{:S(2)}) copy-start(f32[1536]{0:T(1024)S(1)} %get-tuple-element.158) | copy-start | bytes 18436
  441.7 482.9 %reduce-scatter.20.cloned.1.call-start = ((), (), s32[]{:S(2)}) async-start(), calls=%async_computation.19 | async-start | bytes 7864320 | tf_op jit(solution)/shard_map/reduce_scatter | solution.py:109
  701.9 336.8 %reduce-scatter.18.cloned.1.call-start = ((), (), s32[]{:S(2)}) async-start(), calls=%async_computation.17 | async-start | bytes 7864320 | tf_op jit(solution)/shard_map/reduce_scatter | solution.py:95
  713.0 408.4 %all-reduce.19.cloned.1.call-start = ((), (), s32[]{:S(2)}) async-start(), calls=%async_computation.28 | async-start | bytes 3784704
  869.8 168.9 %copy-start.48 = (f32[1536]{0:T(1024)S(1)}, f32[1536]{0:T(1024)}, u32[]{:S(2)}) copy-start(f32[1536]{0:T(1024)} %copy-done.47) | copy-start | bytes 18436
  869.8 168.9 %copy-start.51 = (f32[1536]{0:T(1024)S(1)}, f32[1536]{0:T(1024)}, u32[]{:S(2)}) copy-start(f32[1536]{0:T(1024)} %copy-done.50) | copy-start | bytes 18436
  869.8 344.1 %all-gather.27.cloned.1.call-start = ((), (), s32[]{:S(2)}) async-start(), calls=%async_computation.20 | async-start | bytes 3932160 | tf_op jit(solution)/shard_map/all_gather | solution.py:102
  1047.1 399.1 %all-reduce.21.cloned.1.call-start = ((), (), s32[]{:S(2)}) async-start(), calls=%async_computation.29 | async-start | bytes 7569408
  1304.1 254.1 %reduce-scatter.22.cloned.1.call-start = ((), (), s32[]{:S(2)}) async-start(), calls=%async_computation.21 | async-start | bytes 7864320 | tf_op jit(solution)/shard_map/reduce_scatter | solution.py:109
  1314.9 349.6 %reduce-scatter.28.cloned.1.call-start = ((), (), s32[]{:S(2)}) async-start(), calls=%async_computation.24 | async-start | bytes 2949120
  1321.1 127.9 %copy-start.11 = (f32[1,77,1536]{2,0,1:T(1,128)S(1)}, f32[1,77,1536]{2,0,1:T(1,128)}, u32[]{:S(2)}) copy-start(f32[1,77,1536]{2,0,1:T(1,128)} %copy-done.10) | copy-start | bytes 1419268
  1321.1 127.9 %copy-start.18 = (f32[1,77,1536]{2,0,1:T(1,128)S(1)}, f32[1,77,1536]{2,0,1:T(1,128)}, u32[]{:S(2)}) copy-start(f32[1,77,1536]{2,0,1:T(1,128)} %get-tuple-element.174) | copy-start | bytes 1419268
  1321.1 127.9 %copy-start.20 = (f32[1,77,1536]{2,0,1:T(1,128)S(1)}, f32[1,77,1536]{2,0,1:T(1,128)}, u32[]{:S(2)}) copy-start(f32[1,77,1536]{2,0,1:T(1,128)} %copy-done.19) | copy-start | bytes 1419268
  1321.1 127.9 %copy-start.49 = (f32[1536]{0:T(1024)S(1)}, f32[1536]{0:T(1024)}, u32[]{:S(2)}) copy-start(f32[1536]{0:T(1024)} %get-tuple-element.143) | copy-start | bytes 18436
  1572.3 112.4 %reduce-scatter.30.cloned.1.call-start = ((), (), s32[]{:S(2)}) async-start(), calls=%async_computation.25 | async-start | bytes 491520
  1573.4 148.6 %reduce-scatter.26.cloned.1.call-start = ((), (), s32[]{:S(2)}) async-start(), calls=%async_computation.23 | async-start | bytes 10616832 | tf_op jit(solution)/shard_map/reduce_scatter | solution.py:429
  1581.7 163.1 %reduce-scatter.32.cloned.1.call-start = ((), (), s32[]{:S(2)}) async-start(), calls=%async_computation.26 | async-start | bytes 491520
  1594.2 217.9 %reduce-scatter.24.cloned.1.call-start = ((), (), s32[]{:S(2)}) async-start(), calls=%async_computation.22 | async-start | bytes 7962624 | tf_op jit(solution)/shard_map/reduce_scatter | solution.py:423
  1601.1 534.6 %all-reduce.23.cloned.1.call-start = ((), (), s32[]{:S(2)}) async-start(), calls=%async_computation.30 | async-start | bytes 51904512
  (88 other events, 2392.7 us)
Sparse Core Ops, SparseCore 0:
  9.9 81.4 all-gather.10
  93.3 48.8 all-gather.14
  150.6 78.3 all-gather.12
  230.7 27.1 all-gather.16
  318.9 109.3 reduce-scatter.15
  430.7 59.3 all-gather.20
  492.2 63.4 all-gather.18
  557.6 57.4 all-gather.22
  617.3 63.4 all-gather.24
  683.6 98.8 all-reduce.16
  784.9 139.6 reduce-scatter.19
  926.9 111.7 reduce-scatter.17
  1041.2 80.2 all-reduce.18
  1123.4 90.4 all-gather.26
  1304.3 141.9 all-reduce.20
  1448.4 109.7 reduce-scatter.21
  1572.4 48.5 reduce-scatter.27
  1623.2 20.0 reduce-scatter.29
  1647.2 74.7 reduce-scatter.25
  1724.2 20.5 reduce-scatter.31
  1748.3 63.7 reduce-scatter.23
  1817.6 318.0 all-reduce.22
where the time goes:
time: 2160 us; the launch traced here: 2150 us
  waiting for transfers between devices  1260 us (58%)
  blocking collectives  321 us (15%)
  matrix products  259 us (12%)
  local copies, waits for them, and re-layouts  172 us (8%)
  other arithmetic  117 us (5%)
    unnamed x29, waiting for transfers between devices  488 us
    reduce_scatter x2, waiting for transfers between devices, sum_rows(): lax.psum_scatter(pair[0], 'seq', scatter_dimension=1, tiled=True)  204 us
    reduce_scatter x2, waiting for transfers between devices, sum_grads(): lax.psum_scatter(pair[0], 'seq', scatter_dimension=1, tiled=True)  141 us
    all_gather x2, blocking collectives, gather_grads(): lax.all_gather(pair[1], 'seq', axis=1, tiled=True)  119 us
    all_gather x2, blocking collectives, gather_rows(): lax.all_gather(pair[1], 'seq', axis=1, tiled=True)  108 us
    all_gather x2, waiting for transfers between devices, gather_grads(): lax.all_gather(pair[0], 'seq', axis=1, tiled=True)  83.2 us
    all_gather x1, waiting for transfers between devices, body(): lax.all_gather(ada_weight, 'dp', axis=0, tiled=True)  81.5 us
    unnamed x215, local copies, waits for them, and re-layouts  68.9 us
  transfers between devices with their start and end apart: 22, of which 17 were waited for; matrix products, arithmetic and copies ran while one was open for 19% of the time, Pallas kernels for 0%

commit v1 on v0

v1 whole, which is shorter than its diff:
```python
import functools
import math

import jax
import jax.numpy as jnp
from jax import lax
from jax.experimental import pallas as pl
from jax.experimental.pallas import tpu as pltpu
from jax.sharding import PartitionSpec as P

HD = 64
LANES = 128
EPSILON = 1e-06
GELU_ROOT = math.sqrt(2.0 / math.pi)
GELU_CUBE = 0.044715
MASKED = -1e30
SINGLE = jnp.float32
HALF = jnp.bfloat16
MEGA = 2**20


def up(value, multiple):
    return -(-value // multiple) * multiple


def params(limit=56):
    return pltpu.CompilerParams(
        dimension_semantics=None, vmem_limit_bytes=limit * MEGA
    )


def cost(flops, nbytes, trans=0):
    return pl.CostEstimate(flops=int(flops), bytes_accessed=int(nbytes), transcendentals=int(trans))


def nt_dot(a, b):
    return lax.dot_general(a, b, (((1,), (1,)), ((), ())), preferred_element_type=SINGLE)


def tn_dot(a, b):
    return lax.dot_general(a, b, (((0,), (0,)), ((), ())), preferred_element_type=SINGLE)


def nn_dot(a, b):
    return jnp.dot(a, b, preferred_element_type=SINGLE)


def layer_norm(values):
    center = values - jnp.mean(values, axis=-1, keepdims=True)
    inv_std = lax.rsqrt(jnp.mean(center * center, axis=-1, keepdims=True) + EPSILON)
    return (center * inv_std, inv_std)


def norm_back(normed, inv_std, upstream):
    first = jnp.mean(upstream, axis=-1, keepdims=True)
    second = jnp.mean(upstream * normed, axis=-1, keepdims=True)
    return inv_std * (upstream - first - normed * second)


def gelu_both(values):
    square = values * values
    inner = GELU_ROOT * (values + GELU_CUBE * square * values)
    tangent = jnp.tanh(inner)
    half = 0.5 * (1.0 + tangent)
    slope = half + 0.5 * values * (1.0 - tangent * tangent) * GELU_ROOT * (
        1.0 + 3.0 * GELU_CUBE * square
    )
    return values * half, slope


def silu_slope(values):
    sigma = jax.nn.sigmoid(values)
    return sigma + values * sigma * (1.0 - sigma)


def whole(shape, single=False):
    zeros = (0,) * len(shape)
    if single:
        return pl.BlockSpec(shape, lambda *_: zeros, pipeline_mode=pl.Buffered(1))
    return pl.BlockSpec(shape, lambda *_: zeros)


def rows_spec(rows, width):
    return pl.BlockSpec((1, rows, width), lambda s: (s, 0, 0))


def qkv_kernel(img, x_ref, mod_ref, w_ref, b_ref, a_ref, o_ref):
    wide = o_ref.shape[2]
    for t, sl in ((0, slice(0, img)), (1, slice(img, x_ref.shape[1]))):
        normed, _ = layer_norm(x_ref[0, sl].astype(SINGLE))
        a = (normed * (1.0 + mod_ref[t, 1:2]) + mod_ref[t, 0:1]).astype(HALF)
        a_ref[0, sl] = a
        o_ref[0, sl] = (
            nn_dot(a, w_ref[:, t * wide : (t + 1) * wide]) + b_ref[t : t + 1]
        ).astype(HALF)


def project_qkv(n, img, x_all, mods, weight, bias):
    _, rows, width = x_all.shape
    wide = weight.shape[1] // 2
    return pl.pallas_call(
        functools.partial(qkv_kernel, img),
        grid=(n,),
        in_specs=[rows_spec(rows, width), whole(mods.shape), whole(weight.shape, True), whole(bias.shape)],
        out_specs=[rows_spec(rows, width), rows_spec(rows, wide)],
        out_shape=[
            jax.ShapeDtypeStruct((n, rows, width), HALF),
            jax.ShapeDtypeStruct((n, rows, wide), HALF),
        ],
        compiler_params=params(),
        cost_estimate=cost(2 * n * rows * width * wide, 30 * MEGA),
        name="project_qkv",
    )(x_all, mods, weight, bias)


def halves(shape):
    lane = lax.broadcasted_iota(jnp.int32, shape, len(shape) - 1)
    return lane < HD


def attn_kernel(q_ref, k_ref, v_ref, mask_ref, o_ref, lse_ref):
    n, rows, _ = k_ref.shape
    queries = q_ref[0] * HALF(1.0 / math.sqrt(HD))
    keys = k_ref[...].reshape(n * rows, LANES)
    values = v_ref[...].reshape(n * rows, LANES)
    first = halves(queries.shape)
    outs, logs = [], []
    for head in range(2):
        own = first if head == 0 else jnp.logical_not(first)
        scores = nt_dot(jnp.where(own, queries, HALF(0)), keys) + mask_ref[...]
        maxima = jnp.max(scores, axis=-1, keepdims=True)
        raised = jnp.exp(scores - maxima)
        totals = jnp.sum(raised, axis=-1, keepdims=True)
        weights = (raised * (1.0 / totals)).astype(HALF)
        outs.append(nn_dot(weights, values))
        logs.append(maxima + jnp.log(totals))
    o_ref[0] = jnp.where(first, outs[0], outs[1]).astype(HALF)
    lse_ref[0] = jnp.where(first, logs[0], logs[1])


def attend(n, qkv, mask):
    _, rows, wide = qkv.shape
    pairs = wide // 3 // LANES
    total = n * rows
    block = pl.BlockSpec((1, rows, LANES), lambda h, s: (s, 0, h))
    return pl.pallas_call(
        attn_kernel,
        grid=(pairs, n),
        in_specs=[
            block,
            pl.BlockSpec((n, rows, LANES), lambda h, s: (0, 0, pairs + h)),
            pl.BlockSpec((n, rows, LANES), lambda h, s: (0, 0, 2 * pairs + h)),
            whole(mask.shape),
        ],
        out_specs=[block, block],
        out_shape=[
            jax.ShapeDtypeStruct((n, rows, pairs * LANES), HALF),
            jax.ShapeDtypeStruct((n, rows, pairs * LANES), SINGLE),
        ],
        compiler_params=params(),
        cost_estimate=cost(2 * 2 * 4 * pairs * total * total * LANES, 20 * MEGA, 2 * pairs * total * total),
        name="attend",
    )(qkv, qkv, qkv, mask)


def attn_back_kernel(
    q_ref, k_ref, v_ref, o_ref, g_ref, lse_ref, mask_ref, dq_ref, dk_ref, dv_ref, qb_ref, vb_ref,
    acc_ref, lse_row, delta_row,
):
    step = pl.program_id(1)
    last = pl.num_programs(1) - 1
    n, rows, _ = q_ref.shape
    total = n * rows
    grads = g_ref[...].reshape(total, LANES)
    queries = q_ref[...].reshape(total, LANES) * HALF(1.0 / math.sqrt(HD))

    @pl.when(step == 0)
    def _():
        acc_ref[...] = jnp.zeros_like(acc_ref)
        product = grads.astype(SINGLE) * o_ref[...].reshape(total, LANES).astype(SINGLE)
        turned = product.T
        logs = lse_ref[...].reshape(total, LANES).T
        for head in range(2):
            delta_row[head : head + 1] = jnp.sum(
                turned[head * HD : (head + 1) * HD], axis=0, keepdims=True
            )
            lse_row[head : head + 1] = logs[head * HD : head * HD + 1]
        vb_ref[0] = jnp.zeros_like(vb_ref[0])

    keys, values = k_ref[0], v_ref[0]
    first = halves(keys.shape)
    mask = mask_ref[0][:, 0:1]
    dks, dvs = [], []
    for head in range(2):
        own = first if head == 0 else jnp.logical_not(first)
        key_own = jnp.where(own, keys, HALF(0))
        scores = nt_dot(key_own, queries)
        probs = jnp.exp((scores - lse_row[head : head + 1]) + mask)
        grad_prob = nt_dot(jnp.where(own, values, HALF(0)), grads)
        grad_score = (probs * (grad_prob - delta_row[head : head + 1])).astype(HALF)
        dvs.append(nn_dot(probs.astype(HALF), grads))
        dks.append(nn_dot(grad_score, queries))
        acc_ref[...] += tn_dot(grad_score, key_own)
    dk_ref[0] = jnp.where(first, dks[0], dks[1]).astype(HALF)
    dv = jnp.where(first, dvs[0], dvs[1])
    dv_ref[0] = dv.astype(HALF)
    img = mask_ref.shape[2]
    vb_ref[0, 0:1] += jnp.sum(dv[:img], axis=0, keepdims=True)
    vb_ref[0, 1:2] += jnp.sum(dv[img:], axis=0, keepdims=True)

    @pl.when(step == last)
    def _():
        dq = (acc_ref[...] * (1.0 / math.sqrt(HD))).reshape(n, rows, LANES)
        dq_ref[...] = dq.astype(HALF)
        qb_ref[0, 0:1] = jnp.sum(jnp.sum(dq[:, :img], axis=0), axis=0, keepdims=True)
        qb_ref[0, 1:2] = jnp.sum(jnp.sum(dq[:, img:], axis=0), axis=0, keepdims=True)


def attend_back(n, img, qkv, mixture, grad_mix, lse, mask_col):
    _, rows, wide = qkv.shape
    pairs = wide // 3 // LANES
    total = n * rows
    full = pl.BlockSpec((n, rows, LANES), lambda h, s: (0, 0, h))
    block = pl.BlockSpec((1, rows, LANES), lambda h, s: (s, 0, h))
    bias = pl.BlockSpec((1, 2, LANES), lambda h, s: (h, 0, 0))
    lw = pairs * LANES
    return pl.pallas_call(
        attn_back_kernel,
        grid=(pairs, n),
        in_specs=[
            full,
            pl.BlockSpec((1, rows, LANES), lambda h, s: (s, 0, pairs + h)),
            pl.BlockSpec((1, rows, LANES), lambda h, s: (s, 0, 2 * pairs + h)),
            full,
            full,
            full,
            pl.BlockSpec((1, rows, img), lambda h, s: (s, 0, 0)),
        ],
        out_specs=[full, block, block, bias, bias],
        out_shape=[jax.ShapeDtypeStruct((n, rows, lw), HALF)] * 3
        + [jax.ShapeDtypeStruct((pairs, 2, LANES), SINGLE)] * 2,
        scratch_shapes=[
            pltpu.VMEM((total, LANES), SINGLE),
            pltpu.VMEM((2, total), SINGLE),
            pltpu.VMEM((2, total), SINGLE),
        ],
        compiler_params=params(),
        cost_estimate=cost(2 * 5 * 4 * pairs * total * total * LANES, 30 * MEGA, 2 * pairs * total * total),
        name="attend_back",
    )(qkv, qkv, qkv, mixture, grad_mix, lse, mask_col)


def middle_kernel(img, mix_ref, x_ref, w_ref, b_ref, mod_ref, y_ref, m_ref, o_ref):
    width = x_ref.shape[1]
    for t, sl in ((0, slice(0, img)), (1, slice(img, x_ref.shape[0]))):
        attn = nt_dot(mix_ref[sl], w_ref[:, t * width : (t + 1) * width]) + b_ref[t : t + 1]
        y_ref[sl] = attn
        middle = x_ref[sl].astype(SINGLE) + mod_ref[t, 2:3] * attn
        m_ref[sl] = middle
        normed, _ = layer_norm(middle)
        o_ref[sl] = (normed * (1.0 + mod_ref[t, 4:5]) + mod_ref[t, 3:4]).astype(HALF)


def middle_rows(img, mixture, x_loc, weight, bias, mods):
    rows, width = x_loc.shape
    return pl.pallas_call(
        functools.partial(middle_kernel, img),
        out_shape=[
            jax.ShapeDtypeStruct((rows, width), SINGLE),
            jax.ShapeDtypeStruct((rows, width), SINGLE),
            jax.ShapeDtypeStruct((rows, width), HALF),
        ],
        compiler_params=params(),
        cost_estimate=cost(2 * rows * width * width, 16 * MEGA),
        name="middle_rows",
    )(mixture, x_loc, weight, bias, mods)


def mlp_kernel(img, tile, b_ref, e_ref, mod_ref, w1_ref, b1_ref, w2_ref, g_ref, dz_ref, dy_ref, db_ref, sum_ref, acc_ref):
    step = pl.program_id(0)
    units = g_ref.shape[2]

    @pl.when(step == 0)
    def _():
        sum_ref[...] = jnp.zeros_like(sum_ref)

    for t, sl in ((0, slice(0, img)), (1, slice(img, b_ref.shape[1]))):
        rows = b_ref[0, sl]
        grad = (mod_ref[t, 5:6] * e_ref[0, sl].astype(SINGLE)).astype(HALF)
        dy_ref[0, sl] = grad

        for k in range(units // tile):
            here = slice(k * tile, (k + 1) * tile)
            cols = slice(t * units + k * tile, t * units + (k + 1) * tile)
            w1 = w1_ref[:, cols]
            pre = nn_dot(rows, w1) + b1_ref[t : t + 1, here]
            hidden, slope = gelu_both(pre)
            g_ref[0, sl, here] = hidden.astype(HALF)
            dz = nn_dot(grad, w2_ref[:, cols]) * slope
            sum_ref[t : t + 1, here] += jnp.sum(dz, axis=0, keepdims=True)
            dzh = dz.astype(HALF)
            dz_ref[0, sl, here] = dzh
            part = nt_dot(dzh, w1)
            if k == 0:
                acc_ref[sl] = part
            else:
                acc_ref[sl] += part
        db_ref[0, sl] = acc_ref[sl].astype(HALF)


def feed_forward(n, img, mlp_in, cot, mods, w1, b1, w2):
    rows, width = mlp_in.shape[1:]
    units = w1.shape[1] // 2
    tile = min(512, units)
    while units % tile:
        tile -= LANES
    return pl.pallas_call(
        functools.partial(mlp_kernel, img, tile),
        grid=(n,),
        in_specs=[
            rows_spec(rows, width),
            rows_spec(rows, width),
            whole(mods.shape),
            whole(w1.shape, True),
            whole(b1.shape),
            whole(w2.shape, True),
        ],
        out_specs=[
            rows_spec(rows, units),
            rows_spec(rows, units),
            rows_spec(rows, width),
            rows_spec(rows, width),
            whole((2, units)),
        ],
        out_shape=[
            jax.ShapeDtypeStruct((n, rows, units), HALF),
            jax.ShapeDtypeStruct((n, rows, units), HALF),
            jax.ShapeDtypeStruct((n, rows, width), HALF),
            jax.ShapeDtypeStruct((n, rows, width), HALF),
            jax.ShapeDtypeStruct((2, units), SINGLE),
        ],
        scratch_shapes=[pltpu.VMEM((rows, width), SINGLE)],
        compiler_params=params(),
        cost_estimate=cost(6 * n * rows * width * units, 50 * MEGA, n * rows * units),
        name="feed_forward",
    )(mlp_in, cot, mods, w1, b1, w2)


def out_kernel(img, g_ref, e_ref, w2_ref, y_ref, sum_ref):
    units = g_ref.shape[2]

    @pl.when(pl.program_id(0) == 0)
    def _():
        sum_ref[...] = jnp.zeros_like(sum_ref)

    for t, sl in ((0, slice(0, img)), (1, slice(img, g_ref.shape[1]))):
        part = nt_dot(g_ref[0, sl], w2_ref[:, t * units : (t + 1) * units])
        y_ref[0, sl] = part.astype(HALF)
        sum_ref[t : t + 1] += jnp.sum(part * e_ref[0, sl].astype(SINGLE), axis=0, keepdims=True)


def feed_out(n, img, hidden, cot, w2):
    _, rows, units = hidden.shape
    width = w2.shape[0]
    return pl.pallas_call(
        functools.partial(out_kernel, img),
        grid=(n,),
        in_specs=[rows_spec(rows, units), rows_spec(rows, width), whole(w2.shape, True)],
        out_specs=[rows_spec(rows, width), whole((2, width))],
        out_shape=[
            jax.ShapeDtypeStruct((n, rows, width), HALF),
            jax.ShapeDtypeStruct((2, width), SINGLE),
        ],
        compiler_params=params(),
        cost_estimate=cost(2 * n * rows * width * units, 20 * MEGA),
        name="feed_out",
    )(hidden, cot, w2)


def grad_kernel(img, l_ref, r_ref, o_ref):
    n = l_ref.shape[0]
    stream = pl.program_id(0)
    for t, sl in ((0, slice(0, img)), (1, slice(img, l_ref.shape[1]))):

        @pl.when(stream == t)
        def _():
            left = l_ref[:, sl].reshape(-1, l_ref.shape[2])
            right = r_ref[:, sl].reshape(-1, r_ref.shape[2])
            o_ref[...] = tn_dot(left, right).astype(HALF)


def weight_grad(n, img, left, right, name):
    rows, depth = left.shape[1:]
    wide = right.shape[2]
    tile = 384 if wide % 384 == 0 else (256 if wide % 256 == 0 else LANES)
    tiles = wide // tile
    return pl.pallas_call(
        functools.partial(grad_kernel, img),
        grid=(2, tiles),
        in_specs=[
            whole((n, rows, depth), True),
            pl.BlockSpec((n, rows, tile), lambda t, k: (0, 0, k)),
        ],
        out_specs=pl.BlockSpec((depth, tile), lambda t, k: (0, t * tiles + k)),
        out_shape=jax.ShapeDtypeStruct((depth, 2 * wide), HALF),
        compiler_params=params(),
        cost_estimate=cost(2 * n * rows * depth * wide, 20 * MEGA),
        name=name,
    )(left, right)


def middle_back_kernel(img, db_ref, m_ref, y_ref, e_ref, w_ref, mod_ref, dm_ref, dy_ref, do_ref, sum_ref):
    width = m_ref.shape[1]
    for t, sl in ((0, slice(0, img)), (1, slice(img, m_ref.shape[0]))):
        grad_in = db_ref[sl]
        normed, inv_std = layer_norm(m_ref[sl])
        upstream = e_ref[sl].astype(SINGLE)
        grad_middle = upstream + norm_back(normed, inv_std, grad_in * (1.0 + mod_ref[t, 4:5]))
        dm_ref[sl] = grad_middle
        grad_attn = mod_ref[t, 2:3] * grad_middle
        half = grad_attn.astype(HALF)
        dy_ref[sl] = half
        do_ref[sl] = nn_dot(half, w_ref[:, t * width : (t + 1) * width]).astype(HALF)

        def total(value):
            return jnp.sum(value, axis=0, keepdims=True)

        sum_ref[t, 0:1] = total(grad_middle * y_ref[sl])
        sum_ref[t, 1:2] = total(grad_in)
        sum_ref[t, 2:3] = total(grad_in * normed)
        sum_ref[t, 3:4] = total(grad_attn)
        sum_ref[t, 4:5] = total(upstream)


def middle_back(img, grad_in, middle, attn_out, cot, weight, mods):
    rows, width = middle.shape
    return pl.pallas_call(
        functools.partial(middle_back_kernel, img),
        out_shape=[
            jax.ShapeDtypeStruct((rows, width), SINGLE),
            jax.ShapeDtypeStruct((rows, width), HALF),
            jax.ShapeDtypeStruct((rows, width), HALF),
            jax.ShapeDtypeStruct((2, 8, width), SINGLE),
        ],
        compiler_params=params(),
        cost_estimate=cost(2 * rows * width * width, 20 * MEGA),
        name="middle_back",
    )(grad_in, middle, attn_out, cot, weight, mods)


def attn_in_kernel(img, dq_ref, dk_ref, dv_ref, x_ref, w_ref, da_ref, sum_ref):
    lw = dq_ref.shape[2]

    @pl.when(pl.program_id(0) == 0)
    def _():
        sum_ref[...] = jnp.zeros_like(sum_ref)

    for t, sl in ((0, slice(0, img)), (1, slice(img, x_ref.shape[1]))):
        part = None
        for c, ref in enumerate((dq_ref, dk_ref, dv_ref)):
            start = (3 * t + c) * lw
            term = nt_dot(ref[0, sl], w_ref[:, start : start + lw])
            part = term if part is None else part + term
        da_ref[0, sl] = part.astype(HALF)
        normed, _ = layer_norm(x_ref[0, sl].astype(SINGLE))
        sum_ref[t, 0:1] += jnp.sum(part, axis=0, keepdims=True)
        sum_ref[t, 1:2] += jnp.sum(part * normed, axis=0, keepdims=True)


def attn_in_back(n, img, dq, dk, dv, x_all, weight):
    _, rows, lw = dq.shape
    width = x_all.shape[2]
    return pl.pallas_call(
        functools.partial(attn_in_kernel, img),
        grid=(n,),
        in_specs=[rows_spec(rows, lw)] * 3 + [rows_spec(rows, width), whole(weight.shape, True)],
        out_specs=[rows_spec(rows, width), whole((2, 2, width))],
        out_shape=[
            jax.ShapeDtypeStruct((n, rows, width), HALF),
            jax.ShapeDtypeStruct((2, 2, width), SINGLE),
        ],
        compiler_params=params(),
        cost_estimate=cost(6 * n * rows * width * lw, 30 * MEGA),
        name="attn_in_back",
    )(dq, dk, dv, x_all, weight)


def hops(n):
    return [(a, a + 1) for a in range(n - 1)], [(a + 1, a) for a in range(n - 1)]


def line_gather(rows, n):
    me = lax.axis_index("seq")
    right, left = hops(n)
    held = jnp.zeros((n + 1,) + rows.shape, rows.dtype)
    held = lax.dynamic_update_index_in_dim(held, rows, me, 0)
    from_left = from_right = rows
    for k in range(1, n):
        from_left = lax.ppermute(from_left, "seq", right)
        from_right = lax.ppermute(from_right, "seq", left)
        held = lax.dynamic_update_index_in_dim(
            held, from_left, jnp.where(me >= k, me - k, n), 0
        )
        held = lax.dynamic_update_index_in_dim(
            held, from_right, jnp.where(me + k < n, me + k, n), 0
        )
    return held


def line_sum(parts, n):
    me = lax.axis_index("seq")
    right, left = hops(n)

    def term(s):
        return lax.dynamic_index_in_dim(parts, jnp.clip(s, 0, n - 1), 0, keepdims=False).astype(
            SINGLE
        )

    result = term(me)
    for sign, pattern in ((1, right), (-1, left)):
        carry = None
        for k in range(n - 1, 0, -1):
            value = term(me + sign * k)
            if carry is not None:
                value = value + carry.astype(SINGLE)
            carry = lax.ppermute(value.astype(HALF), "seq", pattern)
        result = result + carry.astype(SINGLE)
    return result


def swap(parts, n):
    me = lax.axis_index("seq")
    held = jnp.zeros_like(parts)
    held = lax.dynamic_update_index_in_dim(
        held, lax.dynamic_index_in_dim(parts, me, 0, keepdims=False), me, 0
    )
    for k in range(1, n):
        piece = lax.dynamic_index_in_dim(parts, lax.rem(me + k, n), 0, keepdims=False)
        got = lax.ppermute(piece, "seq", [(a, (a + k) % n) for a in range(n)])
        held = lax.dynamic_update_index_in_dim(held, got, lax.rem(me + n - k, n), 0)
    return held


def body(
    image_tokens,
    text_tokens,
    text_lengths,
    conditioning,
    ada_weight,
    ada_bias,
    qkv_weight,
    qv_bias,
    proj_weight,
    proj_bias,
    fc1_weight,
    fc1_bias,
    fc2_weight,
    fc2_bias,
    image_cotangent,
    text_cotangent,
):
    n = lax.axis_size("seq")
    dp = lax.axis_size("dp")
    img, width = image_tokens.shape[1:]
    slots = text_tokens.shape[1]
    pad = up(slots, 16)
    rows = img + pad
    depth = qkv_weight.shape[0]
    lw = qkv_weight.shape[3]
    lwp = up(lw, LANES)
    units = fc1_weight.shape[2]
    mod_cols = ada_weight.shape[2]
    my_seq = lax.axis_index("dp")

    def stacked(image, text):
        return jnp.concatenate([image, jnp.pad(text, ((0, pad - slots), (0, 0)))], axis=0)

    length = text_lengths[0, 0]
    live_text = (jnp.arange(slots, dtype=jnp.int32) < length)[:, None]
    x_loc = stacked(image_tokens[0], text_tokens[0])
    e_loc = stacked(
        image_cotangent[0], jnp.where(live_text, text_cotangent[0], jnp.zeros((), HALF))
    )
    x_all = line_gather(x_loc, n)

    qkv_local = jnp.pad(qkv_weight, ((0, 0), (0, 0), (0, 0), (0, lwp - lw))).reshape(depth, 6 * lwp)
    qkv_full = lax.all_gather(qkv_local, "dp", axis=0, tiled=True)
    share = proj_weight.shape[0]
    proj_turned = proj_weight.transpose(2, 1, 0)
    proj_line = lax.all_gather(proj_turned, "seq", axis=2, tiled=True).reshape(depth, 2 * width)
    proj_full = lax.all_gather(proj_line, "dp", axis=0, tiled=True)
    fc1_full = lax.all_gather(fc1_weight.reshape(depth, 2 * units), "dp", axis=0, tiled=True)
    fc2_turned = fc2_weight.transpose(2, 1, 0).reshape(depth, 2 * units)
    fc2_full = lax.all_gather(fc2_turned, "dp", axis=0, tiled=True)

    cond_float = conditioning.astype(SINGLE)
    cond_act = jax.nn.silu(cond_float).astype(HALF)
    act_all = lax.all_gather(cond_act, "dp", axis=0, tiled=True)
    act_slice = lax.dynamic_slice_in_dim(act_all, my_seq * depth, depth, axis=1)
    ada_flat = ada_weight.reshape(depth, 2 * mod_cols)
    mod_part = jnp.dot(act_slice, ada_flat, preferred_element_type=SINGLE)
    mod_local = lax.psum_scatter(mod_part, "dp", scatter_dimension=0, tiled=True).reshape(
        2, mod_cols
    ) + ada_bias.astype(SINGLE)
    side = jnp.concatenate(
        [
            mod_local.reshape(-1),
            proj_bias.astype(SINGLE).reshape(-1),
            fc2_bias.astype(SINGLE).reshape(-1),
            jnp.full((LANES,), length.astype(SINGLE)),
        ]
    )
    side_all = lax.all_gather(side, "seq", axis=0, tiled=False)
    bias_cols = proj_bias.shape[1]
    cut = 2 * mod_cols

    def columns(start, cols):
        return side_all[:, start : start + 2 * cols].reshape(n, 2, cols).transpose(1, 0, 2)

    mods = jnp.pad(
        columns(0, mod_cols).reshape(2, 6, width), ((0, 0), (0, 2), (0, 0))
    )
    proj_shift = columns(cut, bias_cols).reshape(2, width)
    fc2_shift = columns(cut + 2 * bias_cols, bias_cols).reshape(2, width)
    lengths_all = side_all[:, cut + 4 * bias_cols]

    slot = jnp.arange(rows, dtype=SINGLE)[None, :] - img
    live = jnp.logical_or(slot < 0, jnp.logical_and(slot < lengths_all[:, None], slot < slots))
    mask = jnp.where(live, SINGLE(0), SINGLE(MASKED))
    mask_row = mask.reshape(1, n * rows)
    mask_col = jnp.broadcast_to(mask[:, :, None], (n, rows, img))
    live_loc = jnp.concatenate(
        [jnp.ones((img, 1), SINGLE), jnp.pad(live_text.astype(SINGLE), ((0, pad - slots), (0, 0)))]
    )

    bias_rows = jnp.stack(
        [qv_bias[:, 0], jnp.zeros_like(qv_bias[:, 0]), qv_bias[:, 1]], axis=1
    ).astype(SINGLE)
    bias_rows = jnp.pad(bias_rows, ((0, 0), (0, 0), (0, lwp - lw))).reshape(2, 3 * lwp)
    attn_in, qkv_rows = project_qkv(n, img, x_all, mods, qkv_full, bias_rows)
    mixture, lse = attend(n, qkv_rows, mask_row)
    e_all = line_gather(e_loc, n)
    mix_loc = swap(mixture[:, :, :lw], n).transpose(1, 0, 2).reshape(rows, width)

    attn_out, middle, mlp_loc = middle_rows(img, mix_loc, x_loc, proj_full, proj_shift, mods)
    mlp_in = line_gather(mlp_loc, n)
    hidden, grad_pre, grad_mlp, mlp_in_part, fc1_bias_part = feed_forward(
        n, img, mlp_in, e_all, mods, fc1_full, fc1_bias.astype(SINGLE), fc2_full
    )
    grad_mlp_in = line_sum(mlp_in_part, n)
    fc1_part = weight_grad(n, img, mlp_in, grad_pre, "fc1_grad")
    fc1_sum = lax.psum_scatter(fc1_part, "dp", scatter_dimension=0, tiled=True)
    fc2_part = weight_grad(n, img, grad_mlp, hidden, "fc2_grad")
    fc2_sum = lax.psum_scatter(fc2_part, "dp", scatter_dimension=0, tiled=True)
    mlp_out_part, gate_two_part = feed_out(n, img, hidden, e_all, fc2_full)

    grad_middle, grad_attn, grad_mix_loc, sums = middle_back(
        img, grad_mlp_in, middle, attn_out, e_loc, proj_full, mods
    )
    grad_mix = swap(grad_mix_loc.reshape(rows, n, lw).transpose(1, 0, 2), n)
    grad_mix = jnp.pad(grad_mix, ((0, 0), (0, 0), (0, lwp - lw)))
    mlp_sum = line_sum(mlp_out_part, n)
    proj_part = weight_grad(1, img, grad_attn[None], mix_loc[None], "proj_grad")
    proj_sum = lax.psum_scatter(proj_part, "dp", scatter_dimension=0, tiled=True)
    proj_own = lax.psum_scatter(
        proj_sum.reshape(depth, 2, n, share).transpose(2, 0, 1, 3).astype(SINGLE),
        "seq",
        scatter_dimension=0,
        tiled=False,
    )
    grad_q, grad_k, grad_v, q_bias_part, v_bias_part = attend_back(
        n, img, qkv_rows, mixture, grad_mix, lse, mask_col
    )
    attn_in_part, mod_one = attn_in_back(n, img, grad_q, grad_k, grad_v, x_all, qkv_full)
    grad_attn_in = line_sum(attn_in_part, n)
    qkv_part = weight_grad(
        n, img, attn_in, jnp.concatenate([grad_q, grad_k, grad_v], axis=2), "qkv_grad"
    )
    qkv_sum = lax.psum_scatter(qkv_part, "dp", scatter_dimension=0, tiled=True)

    def by_row(vectors):
        return jnp.concatenate(
            [
                jnp.broadcast_to(vectors[0:1], (img, width)),
                jnp.broadcast_to(vectors[1:2], (pad, width)),
            ]
        )

    block_out = (
        (middle + by_row(mods[:, 5]) * (mlp_sum + by_row(fc2_shift))) * live_loc
    ).astype(HALF)
    normed, inv_std = layer_norm(x_loc.astype(SINGLE))
    input_grad = (
        grad_middle + norm_back(normed, inv_std, grad_attn_in * (1.0 + by_row(mods[:, 1])))
    ) * live_loc

    upstream_sum = sums[:, 4]
    gate_two = gate_two_part + fc2_shift * upstream_sum
    mod_grads = jnp.stack(
        [mod_one[:, 0], mod_one[:, 1], sums[:, 0], sums[:, 1], sums[:, 2], gate_two], axis=1
    ).reshape(2, n, mod_cols)
    rest = jnp.stack([sums[:, 3], mods[:, 5] * upstream_sum]).reshape(4, n, bias_cols)
    packed = jnp.concatenate(
        [
            mod_grads.transpose(1, 0, 2).reshape(n, -1),
            rest.transpose(1, 0, 2).reshape(n, -1),
        ],
        axis=1,
    )
    own = lax.psum_scatter(packed, "seq", scatter_dimension=0, tiled=False)
    q_bias = q_bias_part.transpose(1, 0, 2).reshape(2, lwp)[:, :lw]
    v_bias = v_bias_part.transpose(1, 0, 2).reshape(2, lwp)[:, :lw]
    qv_part = jnp.stack([q_bias, v_bias], axis=1)
    wide_row = jnp.concatenate([own, qv_part.reshape(-1), fc1_bias_part.reshape(-1)])
    every = lax.all_gather(wide_row, "dp", axis=0, tiled=False)
    total = jnp.sum(every, axis=0)
    mod_half = every[:, :cut].astype(HALF).reshape(dp, 2, mod_cols)
    ada_grad = jnp.einsum("nd,ntc->dtc", act_slice, mod_half, preferred_element_type=SINGLE)
    ada_bias_grad = total[:cut].reshape(2, mod_cols)
    proj_bias_grad = total[cut : cut + 2 * bias_cols].reshape(2, bias_cols)
    fc2_bias_grad = total[cut + 2 * bias_cols : cut + 4 * bias_cols].reshape(2, bias_cols)
    after = cut + 4 * bias_cols
    qv_bias_grad = total[after : after + 4 * lw].reshape(2, 2, lw)
    fc1_bias_grad = total[after + 4 * lw :].reshape(2, units)
    cond_part = jnp.einsum(
        "nc,dc->nd", mod_half.reshape(dp, cut), ada_flat, preferred_element_type=SINGLE
    )
    cond_cols = lax.psum(cond_part, "seq")
    cond_all = lax.all_gather(cond_cols, "dp", axis=1, tiled=True)
    cond_grad = lax.dynamic_slice_in_dim(cond_all, my_seq, 1, axis=0) * silu_slope(cond_float)

    def streams(flat, last):
        return flat.astype(SINGLE).reshape(depth, 2, last)

    qkv_grad = qkv_sum.astype(SINGLE).reshape(depth, 2, 3, lwp)[..., :lw]
    fc2_grad = streams(fc2_sum, units).transpose(2, 1, 0)
    proj_grad = proj_own.transpose(2, 1, 0)
    return (
        block_out[None, :img],
        block_out[None, img : img + slots],
        input_grad[None, :img],
        input_grad[None, img : img + slots],
        cond_grad,
        ada_grad,
        ada_bias_grad,
        qkv_grad,
        qv_bias_grad,
        proj_grad,
        proj_bias_grad,
        streams(fc1_sum, units),
        fc1_bias_grad,
        fc2_grad,
        fc2_bias_grad,
    )


def solution(mesh):
    in_specs = (
        P("dp", "seq", None),
        P("dp", "seq", None),
        P("dp", "seq"),
        P("dp", None),
        P("dp", None, "seq"),
        P(None, "seq"),
        P("dp", None, None, "seq"),
        P(None, None, "seq"),
        P("seq", None, "dp"),
        P(None, "seq"),
        P("dp", None, "seq"),
        P(None, "seq"),
        P("seq", None, "dp"),
        P(None, "seq"),
        P("dp", "seq", None),
        P("dp", "seq", None),
    )
    out_specs = (
        P("dp", "seq", None),
        P("dp", "seq", None),
        P("dp", "seq", None),
        P("dp", "seq", None),
        P("dp", None),
        P("dp", None, "seq"),
        P(None, "seq"),
        P("dp", None, None, "seq"),
        P(None, None, "seq"),
        P("seq", None, "dp"),
        P(None, "seq"),
        P("dp", None, "seq"),
        P(None, "seq"),
        P("seq", None, "dp"),
        P(None, "seq"),
    )
    return jax.shard_map(body, mesh=mesh, in_specs=in_specs, out_specs=out_specs, check_vma=False)
```

time: 2160 us -> 908 us (0.42)
  waiting for transfers between devices: 1260 us -> 307 us
  blocking collectives: 321 us -> 60.2 us
  matrix products: 259 us -> 4.92 us
  Pallas kernels: 0 us -> 237 us
  starting transfers between devices: 1.69 us -> 122 us
  other arithmetic: 117 us -> 41.2 us
  local copies, waits for them, and re-layouts: 172 us -> 106 us
    unnamed x29 -> x14, waiting for transfers between devices: 488 us -> 26.9 us
    reduce_scatter x6 -> x5, waiting for transfers between devices: 447 us -> 32.4 us  [the longest x1 32.4 us: body(): lax.psum_scatter(proj_sum.reshape(depth, 2, n, share).transpose(2, 0, 1,...]
    all_gather x9 -> x5, waiting for transfers between devices: 328 us -> 16 us  [the longest x1 16 us: body(): lax.all_gather(proj_turned, 'seq', axis=2, tiled=True)]
    dot_general x32 -> x3, matrix products: 259 us -> 4.92 us  [the longest x1 2.48 us: body(): jnp.einsum('nd,ntc->dtc', act_slice, mod_half, preferred_element_type=SIN...]
    pallas_call x0 -> x12, Pallas kernels: none -> 237 us  [the longest x4 55.8 us: weight_grad(): pl.pallas_call(functools.partial(grad_kernel, img), grid=(2, tiles), in_s...]
    ppermute x0 -> x42, waiting for transfers between devices: none -> 232 us  [the longest x18 131 us: line_sum(): carry = lax.ppermute(value.astype(HALF), 'seq', pattern)]
    all_gather x7 -> x4, blocking collectives: 272 us -> 41.7 us  [the longest x1 13.3 us: body(): side_all = lax.all_gather(side, 'seq', axis=0, tiled=False)]
    ppermute x0 -> x42, starting transfers between devices: none -> 122 us  [the longest x18 56.2 us: line_sum(): carry = lax.ppermute(value.astype(HALF), 'seq', pattern)]
  transfers between devices with their start and end apart: 22 -> 54, of which waited for: 17 -> 26; matrix products, arithmetic and copies ran while one was open for 19% -> 15% of each run, Pallas kernels for 0% -> 20%
where the time goes in v1:
time: 908 us; the launch traced here: 897 us
  waiting for transfers between devices  307 us (34%)
  Pallas kernels  237 us (26%)
  starting transfers between devices  122 us (13%)
  local copies, waits for them, and re-layouts  106 us (12%)
  blocking collectives  60.2 us (7%)
  other arithmetic  41.2 us (5%)
  between operations  18.1 us (2%)
    ppermute x18, waiting for transfers between devices, line_sum(): carry = lax.ppermute(value.astype(HALF), 'seq', pattern)  131 us
    ppermute x9, waiting for transfers between devices, line_gather(): from_left = lax.ppermute(from_left, 'seq', right)  76.5 us
    ppermute x18, starting transfers between devices, line_sum(): carry = lax.ppermute(value.astype(HALF), 'seq', pattern)  56.2 us
    pallas_call x4, Pallas kernels, weight_grad(): pl.pallas_call(functools.partial(grad_kernel, img), grid=(2, tiles), in_s...  55.8 us
    pallas_call x1, Pallas kernels, attend_back(): pl.pallas_call(attn_back_kernel, grid=(pairs, n), in_specs=[full, pl.Bloc...  44.2 us
    ppermute x9, starting transfers between devices, line_gather(): from_left = lax.ppermute(from_left, 'seq', right)  42.6 us
    pallas_call x1, Pallas kernels, feed_forward(): pl.pallas_call(functools.partial(mlp_kernel, img, tile), grid=(n,), in_sp...  40.1 us
    reduce_scatter x1, waiting for transfers between devices, body(): lax.psum_scatter(proj_sum.reshape(depth, 2, n, share).transpose(2, 0, 1,...  32.4 us
  transfers between devices with their start and end apart: 54, of which 26 were waited for; matrix products, arithmetic and copies ran while one was open for 15% of the time, Pallas kernels for 20%

profile of v1, /device:TPU:0, one launch (start us, length us, event | category | flops | bytes accessed | tf_op | source)
XLA Modules:
  0.0 896.7 jit_solution(13169391976107435350)
XLA Ops:
  11.2 10.6 %all-gather.2 = bf16[8,1,1536]{2,1,0:T(2,128)(2,1)S(1)} all-gather(bf16[1,1,1536]{2,1,0:T(2,128)(2,1)S(1)} %get-tuple-element.148), channel_id=1, replica_groups=mesh['dp'=8,'seq'=4] {'dp'}, dimensions={0}, use_global_device_ids=true | all-gather | bytes 27648 | tf_op jit(solution)/shard_map/all_gather | solution.py:598
  27.3 16.0 %all-gather.14.cloned.1.call-done = bf16[192,2,1536]{2,0,1:T(8,128)(2,1)} async-done(((bf16[192,2,384]{2,0,1:T(8,128)(2,1)}), bf16[192,2,1536]{2,0,1:T(8,128)(2,1)}) %all-gather.14.cloned.1.call-update) | async-done | bytes 1179664 | tf_op jit(solution)/shard_map/all_gather | solution.py:590
  71.9 26.0 %all-reduce.10.cloned.1.call-done = f32[8,4608]{1,0:T(8,128)} async-done(((f32[8,4608]{1,0:T(8,128)}), f32[8,4608]{1,0:T(8,128)}) %all-reduce.10.cloned.1.call-update) | async-done | bytes 147472
  99.6 13.3 %all-gather.3 = f32[4,1,6272]{2,1,0:T(1,128)S(1)} all-gather(f32[1,1,6272]{2,1,0:T(1,128)S(1)} %reshape.455), channel_id=2, replica_groups=mesh['dp'=8,'seq'=4] {'seq'}, dimensions={0}, use_global_device_ids=true | all-gather | bytes 125440 | tf_op jit(solution)/shard_map/all_gather | solution.py:613
  147.8 16.5 %collective-permute-done.17 = bf16[336,1536]{1,0:T(8,128)(2,1)} collective-permute-done((bf16[336,1536]{1,0:T(8,128)(2,1)}, bf16[336,1536]{1,0:T(8,128)(2,1)}, u32[]{:S(2)}, u32[]{:S(2)}) %collective-permute-start.17) | collective-permute-done | bytes 1032224 | tf_op jit(solution)/shard_map/ppermute | solution.py:499
  176.3 10.0 %collective-permute-done.4 = bf16[336,1536]{1,0:T(8,128)(2,1)S(1)} collective-permute-done((bf16[336,1536]{1,0:T(8,128)(2,1)S(1)}, bf16[336,1536]{1,0:T(8,128)(2,1)S(1)}, u32[]{:S(2)}, u32[]{:S(2)}) %collective-permute-start.4) | collective-permute-done | bytes 1032224 | tf_op jit(solution)/shard_map/ppermute | solution.py:499
  191.8 13.2 %project_qkv.1 = (bf16[4,336,1536]{2,1,0:T(8,128)(2,1)}, bf16[4,336,1152]{2,1,0:T(8,128)(2,1)}) custom-call(bf16[5,336,1536]{2,1,0:T(8,128)(2,1)} %bitcast_dynamic-update-slice_fusion.14.x_ref, f32[2,8,1536]{2,1,0:T(8,128)} %pad.19.mod_ref, bf16[1536,2304]{1,0:T(8,128)(2,1)} %all-gather.12.cloned.1.call-done.w_ref, f32[2,1152]{1,0:T(2,128)} %bitcast.291), custom_call_target="tpu_custom_call" | custom-call | flops 4756340736 | bytes 31457280 | tf_op jit(solution)/shard_map/project_qkv/pallas_call | solution.py:101
  205.0 31.3 %attend.1 = (bf16[4,336,384]{2,1,0:T(8,128)(2,1)}, f32[4,336,384]{2,1,0:T(8,128)}) custom-call(bf16[4,336,1152]{2,1,0:T(8,128)(2,1)} %get-tuple-element.40.q_ref.k_ref.v_ref, bf16[4,336,1152]{2,1,0:T(8,128)(2,1)} %get-tuple-element.40.q_ref.k_ref.v_ref, bf16[4,336,1152]{2,1,0:T(8,128)(2,1)} %get-tuple-element.40.q_ref.k_ref.v_ref, f32[1,1344]{1,0:T(1,128)} %select_n.158.mask_ref), custom_call_target="tpu_custom_call" | custom-call | flops 11098128384 | bytes 20971520 | tf_op jit(solution)/shard_map/attend/pallas_call | solution.py:146
  255.6 9.7 %middle_rows.1 = (f32[336,1536]{1,0:T(8,128)}, f32[336,1536]{1,0:T(8,128)}, bf16[336,1536]{1,0:T(8,128)(2,1)}) custom-call(bf16[336,1536]{1,0:T(8,128)(2,1)} %bitcast.260, bf16[336,1536]{1,0:T(8,128)(2,1)} %copy-done, bf16[1536,3072]{1,0:T(8,128)(2,1)} %all-gather.16.cloned.1.call-done.w_ref, f32[2,1536]{1,0:T(2,128)} %bitcast.287, f32[2,8,1536]{2,1,0:T(8,128)} %pad.19.mod_ref), custom_call_target="tpu_custom_call" | custom-call | flops 1585446912 | bytes 16777216 | tf_op jit(solution)/shard_map/middle_rows/pallas_call | solution.py:266
  276.7 14.0 %collective-permute-done.9 = bf16[336,1536]{1,0:T(8,128)(2,1)S(1)} collective-permute-done((bf16[336,1536]{1,0:T(8,128)(2,1)}, bf16[336,1536]{1,0:T(8,128)(2,1)S(1)}, u32[]{:S(2)}, u32[]{:S(2)}) %collective-permute-start.9) | collective-permute-done | bytes 1032224 | tf_op jit(solution)/shard_map/ppermute | solution.py:499
  298.4 15.5 %collective-permute-done.11 = bf16[336,1536]{1,0:T(8,128)(2,1)S(1)} collective-permute-done((bf16[336,1536]{1,0:T(8,128)(2,1)S(1)}, bf16[336,1536]{1,0:T(8,128)(2,1)S(1)}, u32[]{:S(2)}, u32[]{:S(2)}) %collective-permute-start.11) | collective-permute-done | bytes 1032224 | tf_op jit(solution)/shard_map/ppermute | solution.py:499
  321.8 14.6 %collective-permute-done.13 = bf16[336,1536]{1,0:T(8,128)(2,1)S(1)} collective-permute-done((bf16[336,1536]{1,0:T(8,128)(2,1)S(1)}, bf16[336,1536]{1,0:T(8,128)(2,1)S(1)}, u32[]{:S(2)}, u32[]{:S(2)}) %collective-permute-start.13) | collective-permute-done | bytes 1032224 | tf_op jit(solution)/shard_map/ppermute | solution.py:499
  341.7 40.1 %feed_forward.1 = (bf16[4,336,1536]{2,1,0:T(8,128)(2,1)}, bf16[4,336,1536]{2,1,0:T(8,128)(2,1)}, bf16[4,336,1536]{2,1,0:T(8,128)(2,1)}, bf16[4,336,1536]{2,1,0:T(8,128)(2,1)}, f32[2,1536]{1,0:T(2,128)}) custom-call(bf16[5,336,1536]{2,1,0:T(8,128)(2,1)} %bitcast_dynamic-update-slice_fusion.7.b_ref.l_ref, ...), custom_call_target="tpu_custom_call" | custom-call | flops 19025362944 | bytes 52428800 | tf_op jit(solution)/shard_map/feed_forward/pallas_call | solution.py:317
  389.3 15.2 %collective-permute-done.27 = bf16[336,1536]{1,0:T(8,128)(2,1)} collective-permute-done((bf16[336,1536]{1,0:T(8,128)(2,1)}, bf16[336,1536]{1,0:T(8,128)(2,1)}, u32[]{:S(2)}, u32[]{:S(2)}) %collective-permute-start.27) | collective-permute-done | bytes 1032224 | tf_op jit(solution)/shard_map/ppermute | solution.py:526
  414.0 14.1 %collective-permute-done.28 = bf16[336,1536]{1,0:T(8,128)(2,1)} collective-permute-done((bf16[336,1536]{1,0:T(8,128)(2,1)}, bf16[336,1536]{1,0:T(8,128)(2,1)}, u32[]{:S(2)}, u32[]{:S(2)}) %collective-permute-start.28) | collective-permute-done | bytes 1032224 | tf_op jit(solution)/shard_map/ppermute | solution.py:526
  438.1 13.2 %collective-permute-done.31 = bf16[336,1536]{1,0:T(8,128)(2,1)} collective-permute-done((bf16[336,1536]{1,0:T(8,128)(2,1)S(1)}, bf16[336,1536]{1,0:T(8,128)(2,1)}, u32[]{:S(2)}, u32[]{:S(2)}) %collective-permute-start.31) | collective-permute-done | bytes 1032224 | tf_op jit(solution)/shard_map/ppermute | solution.py:526
  457.0 16.3 %collective-permute-done.32 = bf16[336,1536]{1,0:T(8,128)(2,1)} collective-permute-done((bf16[336,1536]{1,0:T(8,128)(2,1)}, bf16[336,1536]{1,0:T(8,128)(2,1)}, u32[]{:S(2)}, u32[]{:S(2)}) %collective-permute-start.32) | collective-permute-done | bytes 1032224 | tf_op jit(solution)/shard_map/ppermute | solution.py:526
  476.9 10.8 %middle_back.1 = (f32[336,1536]{1,0:T(8,128)}, bf16[336,1536]{1,0:T(8,128)(2,1)}, bf16[336,1536]{1,0:T(8,128)(2,1)}, f32[2,8,1536]{2,1,0:T(8,128)}) custom-call(f32[336,1536]{1,0:T(8,128)} %fusion.25.db_ref, f32[336,1536]{1,0:T(8,128)} %get-tuple-element.42.m_ref, f32[336,1536]{1,0:T(8,128)} %get-tuple-element.47.y_ref, bf16[336,1536]{1,0:T(8,128)(2,1)} %copy-done.8, ...), custom_call_target="tpu_custom_call" | custom-call | flops 1585446912 | bytes 20971520 | tf_op jit(solution)/shard_map/middle_back/pallas_call | solution.py:437
  487.7 9.6 %proj_grad.1 = bf16[1536,3072]{1,0:T(8,128)(2,1)} custom-call(bf16[1,336,1536]{2,1,0:T(8,128)(2,1)} %bitcast.268, bf16[1,336,1536]{2,1,0:T(8,128)(2,1)} %broadcast_in_dim_reshape.3.r_ref), custom_call_target="tpu_custom_call" | custom-call | flops 1585446912 | bytes 20971520 | tf_op jit(solution)/shard_map/proj_grad/pallas_call | solution.py:397
  497.4 16.6 %feed_out.1 = (bf16[4,336,1536]{2,1,0:T(8,128)(2,1)}, f32[2,1536]{1,0:T(2,128)}) custom-call(bf16[4,336,1536]{2,1,0:T(8,128)(2,1)} %get-tuple-element.44.g_ref.r_ref, bf16[5,336,1536]{2,1,0:T(8,128)(2,1)} %bitcast_dynamic-update-slice_fusion.e_ref, bf16[1536,3072]{1,0:T(8,128)(2,1)} %all-gather.20.cloned.1.call-done.w2_ref), custom_call_target="tpu_custom_call" | custom-call | flops 6341787648 | bytes 20971520 | tf_op jit(solution)/shard_map/feed_out/pallas_call | solution.py:365
  533.4 44.2 %attend_back.1 = (bf16[4,336,384]{2,1,0:T(8,128)(2,1)}, bf16[4,336,384]{2,1,0:T(8,128)(2,1)}, bf16[4,336,384]{2,1,0:T(8,128)(2,1)}, f32[3,2,128]{2,1,0:T(2,128)}, f32[3,2,128]{2,1,0:T(2,128)}) custom-call(bf16[4,336,1152]{2,1,0:T(8,128)(2,1)} %get-tuple-element.40.q_ref.k_ref.v_ref, bf16[4,336,1152]{2,1,0:T(8,128)(2,1)} %get-tuple-element.40.q_ref.k_ref.v_ref, ...), custom_call_target="tpu_custom_call" | custom-call | flops 27745320960 | bytes 31457280 | tf_op jit(solution)/shard_map/attend_back/pallas_call | solution.py:227
  577.6 15.6 %attn_in_back.1 = (bf16[4,336,1536]{2,1,0:T(8,128)(2,1)}, f32[2,2,1536]{2,1,0:T(2,128)}) custom-call(bf16[4,336,384]{2,1,0:T(8,128)(2,1)} %get-tuple-element.51.dq_ref, bf16[4,336,384]{2,1,0:T(8,128)(2,1)} %get-tuple-element.52.dk_ref, bf16[4,336,384]{2,1,0:T(8,128)(2,1)} %get-tuple-element.53.dv_ref, ...), custom_call_target="tpu_custom_call" | custom-call | flops 4756340736 | bytes 31457280 | tf_op jit(solution)/shard_map/attn_in_back/pallas_call | solution.py:473
  594.7 16.4 %fc2_grad.1 = bf16[1536,3072]{1,0:T(8,128)(2,1)} custom-call(bf16[4,336,1536]{2,1,0:T(8,128)(2,1)} %get-tuple-element.64.l_ref, bf16[4,336,1536]{2,1,0:T(8,128)(2,1)} %get-tuple-element.44.g_ref.r_ref), custom_call_target="tpu_custom_call" | custom-call | flops 6341787648 | bytes 20971520 | tf_op jit(solution)/shard_map/fc2_grad/pallas_call | solution.py:397
  611.2 17.0 %fc1_grad.1 = bf16[1536,3072]{1,0:T(8,128)(2,1)} custom-call(bf16[5,336,1536]{2,1,0:T(8,128)(2,1)} %bitcast_dynamic-update-slice_fusion.7.b_ref.l_ref, bf16[4,336,1536]{2,1,0:T(8,128)(2,1)} %get-tuple-element.63.r_ref), custom_call_target="tpu_custom_call" | custom-call | flops 6341787648 | bytes 20971520 | tf_op jit(solution)/shard_map/fc1_grad/pallas_call | solution.py:397
  632.1 12.8 %qkv_grad.1 = bf16[1536,2304]{1,0:T(8,128)(2,1)} custom-call(bf16[4,336,1536]{2,1,0:T(8,128)(2,1)} %get-tuple-element.61.l_ref, bf16[4,336,1152]{2,1,0:T(8,128)(2,1)} %pad_maximum_fusion.r_ref), custom_call_target="tpu_custom_call" | custom-call | flops 4756340736 | bytes 20971520 | tf_op jit(solution)/shard_map/qkv_grad/pallas_call | solution.py:397
  652.9 17.9 %collective-permute-done.21 = bf16[336,1536]{1,0:T(8,128)(2,1)S(1)} collective-permute-done((bf16[336,1536]{1,0:T(8,128)(2,1)S(1)}, bf16[336,1536]{1,0:T(8,128)(2,1)S(1)}, u32[]{:S(2)}, u32[]{:S(2)}) %collective-permute-start.21) | collective-permute-done | bytes 1032224 | tf_op jit(solution)/shard_map/ppermute | solution.py:526
  675.8 18.3 %collective-permute-done.22 = bf16[336,1536]{1,0:T(8,128)(2,1)S(1)} collective-permute-done((bf16[336,1536]{1,0:T(8,128)(2,1)S(1)}, bf16[336,1536]{1,0:T(8,128)(2,1)S(1)}, u32[]{:S(2)}, u32[]{:S(2)}) %collective-permute-start.22) | collective-permute-done | bytes 1032224 | tf_op jit(solution)/shard_map/ppermute | solution.py:526
  723.9 18.7 %collective-permute-done.36 = bf16[336,1536]{1,0:T(8,128)(2,1)} collective-permute-done((bf16[336,1536]{1,0:T(8,128)(2,1)}, bf16[336,1536]{1,0:T(8,128)(2,1)}, u32[]{:S(2)}, u32[]{:S(2)}) %collective-permute-start.36) | collective-permute-done | bytes 1032224 | tf_op jit(solution)/shard_map/ppermute | solution.py:526
  755.8 8.8 collective-permute-done.39
  804.9 18.5 %psum.7 = f32[8,192]{1,0:T(8,128)S(1)} all-reduce(f32[8,192]{1,0:T(8,128)S(1)} %fusion.49), channel_id=1, replica_groups=mesh['dp'=8,'seq'=4] {'seq'}, use_global_device_ids=true, to_apply=%region_6.7 | all-reduce | flops 1536 | bytes 12288 | tf_op jit(solution)/shard_map/psum | solution.py:728
  823.4 9.6 %all-gather.5 = f32[8,192,8]{1,2,0:T(8,128)S(1)} all-gather(f32[1,192,8]{1,2,0:T(8,128)S(1)} %bitcast.290), channel_id=1, replica_groups=mesh['dp'=8,'seq'=4] {'dp'}, dimensions={0}, use_global_device_ids=true | all-gather | bytes 55296 | tf_op jit(solution)/shard_map/all_gather | solution.py:729
  856.4 32.4 %reduce-scatter.10.cloned.1.call-done = f32[1,192,2,384]{3,1,2,0:T(8,128)} async-done(((f32[4,192,2,384]{3,1,2,0:T(8,128)}), f32[1,192,2,384]{3,1,2,0:T(8,128)}) %reduce-scatter.10.cloned.1.call-update) | async-done | bytes 589840 | tf_op jit(solution)/shard_map/reduce_scatter | solution.py:665
  (352 shorter events, 322.0 us)
Async XLA Ops:
  8.0 35.3 %all-gather.14.cloned.1.call-start = ((), (), s32[]{:S(2)}) async-start(), calls=%async_computation.6 | async-start | bytes 1474560 | tf_op jit(solution)/shard_map/all_gather | solution.py:590
  8.8 89.1 %all-reduce.10.cloned.1.call-start = ((), (), s32[]{:S(2)}) async-start(), calls=%async_computation.15 | async-start | bytes 294912
  23.5 168.3 %all-gather.12.cloned.1.call-start = ((), (), s32[]{:S(2)}) async-start(), calls=%async_computation.5 | async-start | bytes 7962624 | tf_op jit(solution)/shard_map/all_gather | solution.py:587
  27.3 228.3 %all-gather.16.cloned.1.call-start = ((), (), s32[]{:S(2)}) async-start(), calls=%async_computation.7 | async-start | bytes 10616832 | tf_op jit(solution)/shard_map/all_gather | solution.py:591
  45.8 295.9 %all-gather.20.cloned.1.call-start = ((), (), s32[]{:S(2)}) async-start(), calls=%async_computation.9 | async-start | bytes 10616832 | tf_op jit(solution)/shard_map/all_gather | solution.py:594
  47.1 294.6 %all-gather.18.cloned.1.call-start = ((), (), s32[]{:S(2)}) async-start(), calls=%async_computation.8 | async-start | bytes 10616832 | tf_op jit(solution)/shard_map/all_gather | solution.py:592
  48.6 719.9 %reduce-scatter.8.cloned.1.call-start = ((), (), s32[]{:S(2)}) async-start(), calls=%async_computation.11 | async-start | bytes 10616832 | tf_op jit(solution)/shard_map/reduce_scatter | solution.py:664
  50.8 64.4 %collective-permute-start = (bf16[336,1536]{1,0:T(8,128)(2,1)S(1)}, bf16[336,1536]{1,0:T(8,128)(2,1)}, u32[]{:S(2)}, u32[]{:S(2)}) collective-permute-start(bf16[336,1536]{1,0:T(8,128)(2,1)S(1)} %get-tuple-element.147.x_ref), channel_id=1, source_target_pairs={{0,1},{1,2},{2,3},{4,5},{5,6},{6,7},{8,9},{9,10},{10,11},{12,13},{... | collective-permute-start | bytes 3096584 | tf_op jit(solution)/shard_map/ppermute | solution.py:499
  55.2 63.4 %collective-permute-start.1 = (bf16[336,1536]{1,0:T(8,128)(2,1)S(1)}, bf16[336,1536]{1,0:T(8,128)(2,1)}, u32[]{:S(2)}, u32[]{:S(2)}) collective-permute-start(bf16[336,1536]{1,0:T(8,128)(2,1)S(1)} %get-tuple-element.147.x_ref), channel_id=1, source_target_pairs={{1,0},{2,1},{3,2},{5,4},{6,5},{7,6},{9,8},{10,9},{11,10},{13,12},{... | collective-permute-start | bytes 3096584 | tf_op jit(solution)/shard_map/ppermute | solution.py:500
  57.3 62.6 %collective-permute-start.15 = (bf16[336,1536]{1,0:T(8,128)(2,1)S(1)}, bf16[336,1536]{1,0:T(8,128)(2,1)}, u32[]{:S(2)}, u32[]{:S(2)}) collective-permute-start(bf16[336,1536]{1,0:T(8,128)(2,1)S(1)} %fusion.32.e_ref), channel_id=1, source_target_pairs={{0,1},{1,2},{2,3},{4,5},{5,6},{6,7},{8,9},{9,10},{10,11},{12,13},{... | collective-permute-start | bytes 3096584 | tf_op jit(solution)/shard_map/ppermute | solution.py:499
  62.9 62.7 %collective-permute-start.16 = (bf16[336,1536]{1,0:T(8,128)(2,1)S(1)}, bf16[336,1536]{1,0:T(8,128)(2,1)}, u32[]{:S(2)}, u32[]{:S(2)}) collective-permute-start(bf16[336,1536]{1,0:T(8,128)(2,1)S(1)} %fusion.32.e_ref), channel_id=1, source_target_pairs={{1,0},{2,1},{3,2},{5,4},{6,5},{7,6},{9,8},{10,9},{11,10},{13,12},{... | collective-permute-start | bytes 3096584 | tf_op jit(solution)/shard_map/ppermute | solution.py:500
  115.2 26.9 %collective-permute-start.2 = (bf16[336,1536]{1,0:T(8,128)(2,1)}, bf16[336,1536]{1,0:T(8,128)(2,1)S(1)}, u32[]{:S(2)}, u32[]{:S(2)}) collective-permute-start(bf16[336,1536]{1,0:T(8,128)(2,1)} %collective-permute-done), channel_id=1, source_target_pairs={{0,1},{1,2},{2,3},{4,5},{5,6},{6,7},{8,9},{9,10},{10,11},{12,13},{... | collective-permute-start | bytes 3096584 | tf_op jit(solution)/shard_map/ppermute | solution.py:499
  118.6 27.9 %collective-permute-start.3 = (bf16[336,1536]{1,0:T(8,128)(2,1)}, bf16[336,1536]{1,0:T(8,128)(2,1)S(1)}, u32[]{:S(2)}, u32[]{:S(2)}) collective-permute-start(bf16[336,1536]{1,0:T(8,128)(2,1)} %collective-permute-done.1), channel_id=1, source_target_pairs={{1,0},{2,1},{3,2},{5,4},{6,5},{7,6},{9,8},{10,9},{11,10},{13,12},{... | collective-permute-start | bytes 3096584 | tf_op jit(solution)/shard_map/ppermute | solution.py:500
  119.9 44.3 %collective-permute-start.17 = (bf16[336,1536]{1,0:T(8,128)(2,1)}, bf16[336,1536]{1,0:T(8,128)(2,1)}, u32[]{:S(2)}, u32[]{:S(2)}) collective-permute-start(bf16[336,1536]{1,0:T(8,128)(2,1)} %collective-permute-done.15), channel_id=1, source_target_pairs={{0,1},{1,2},{2,3},{4,5},{5,6},{6,7},{8,9},{9,10},{10,11},{12,13},{... | collective-permute-start | bytes 3096584 | tf_op jit(solution)/shard_map/ppermute | solution.py:499
  125.5 44.1 %collective-permute-start.18 = (bf16[336,1536]{1,0:T(8,128)(2,1)}, bf16[336,1536]{1,0:T(8,128)(2,1)S(1)}, u32[]{:S(2)}, u32[]{:S(2)}) collective-permute-start(bf16[336,1536]{1,0:T(8,128)(2,1)} %collective-permute-done.16), channel_id=1, source_target_pairs={{1,0},{2,1},{3,2},{5,4},{6,5},{7,6},{9,8},{10,9},{11,10},{13,12},{... | collective-permute-start | bytes 3096584 | tf_op jit(solution)/shard_map/ppermute | solution.py:500
  142.1 44.1 %collective-permute-start.4 = (bf16[336,1536]{1,0:T(8,128)(2,1)S(1)}, bf16[336,1536]{1,0:T(8,128)(2,1)S(1)}, u32[]{:S(2)}, u32[]{:S(2)}) collective-permute-start(bf16[336,1536]{1,0:T(8,128)(2,1)S(1)} %collective-permute-done.2), channel_id=1, source_target_pairs={{0,1},{1,2},{2,3},{4,5},{5,6},{6,7},{8,9},{9,10},{10,11},{12,13},{... | collective-permute-start | bytes 3096584 | tf_op jit(solution)/shard_map/ppermute | solution.py:499
  146.5 44.2 %collective-permute-start.5 = (bf16[336,1536]{1,0:T(8,128)(2,1)S(1)}, bf16[336,1536]{1,0:T(8,128)(2,1)S(1)}, u32[]{:S(2)}, u32[]{:S(2)}) collective-permute-start(bf16[336,1536]{1,0:T(8,128)(2,1)S(1)} %collective-permute-done.3), channel_id=1, source_target_pairs={{1,0},{2,1},{3,2},{5,4},{6,5},{7,6},{9,8},{10,9},{11,10},{13,12},{... | collective-permute-start | bytes 3096584 | tf_op jit(solution)/shard_map/ppermute | solution.py:500
  164.2 76.1 %collective-permute-start.19 = (bf16[336,1536]{1,0:T(8,128)(2,1)}, bf16[336,1536]{1,0:T(8,128)(2,1)}, u32[]{:S(2)}, u32[]{:S(2)}) collective-permute-start(bf16[336,1536]{1,0:T(8,128)(2,1)} %collective-permute-done.17), channel_id=1, source_target_pairs={{0,1},{1,2},{2,3},{4,5},{5,6},{6,7},{8,9},{9,10},{10,11},{12,13},{... | collective-permute-start | bytes 3096584 | tf_op jit(solution)/shard_map/ppermute | solution.py:499
  169.6 102.3 %collective-permute-start.20 = (bf16[336,1536]{1,0:T(8,128)(2,1)S(1)}, bf16[336,1536]{1,0:T(8,128)(2,1)S(1)}, u32[]{:S(2)}, u32[]{:S(2)}) collective-permute-start(bf16[336,1536]{1,0:T(8,128)(2,1)S(1)} %collective-permute-done.18), channel_id=1, source_target_pairs={{1,0},{2,1},{3,2},{5,4},{6,5},{7,6},{9,8},{10,9},{11,10},{13,12},{... | collective-permute-start | bytes 3096584 | tf_op jit(solution)/shard_map/ppermute | solution.py:500
  265.3 25.4 %collective-permute-start.9 = (bf16[336,1536]{1,0:T(8,128)(2,1)}, bf16[336,1536]{1,0:T(8,128)(2,1)S(1)}, u32[]{:S(2)}, u32[]{:S(2)}) collective-permute-start(bf16[336,1536]{1,0:T(8,128)(2,1)} %get-tuple-element.43), channel_id=1, source_target_pairs={{0,1},{1,2},{2,3},{4,5},{5,6},{6,7},{8,9},{9,10},{10,11},{12,13},{... | collective-permute-start | bytes 3096584 | tf_op jit(solution)/shard_map/ppermute | solution.py:499
  432.0 25.0 %collective-permute-start.29 = (bf16[336,1536]{1,0:T(8,128)(2,1)S(1)}, bf16[336,1536]{1,0:T(8,128)(2,1)}, u32[]{:S(2)}, u32[]{:S(2)}) collective-permute-start(bf16[336,1536]{1,0:T(8,128)(2,1)S(1)} %get-tuple-element.154), channel_id=1, source_target_pairs={{0,1},{1,2},{2,3},{4,5},{5,6},{6,7},{8,9},{9,10},{10,11},{12,13},{... | collective-permute-start | bytes 3096584 | tf_op jit(solution)/shard_map/ppermute | solution.py:526
  497.3 275.7 %all-reduce.12.cloned.1.call-start = ((), (), s32[]{:S(2)}) async-start(), calls=%async_computation.16 | async-start | bytes 196608
  594.7 249.8 %reduce-scatter.14.cloned.1.call-start = ((), (), s32[]{:S(2)}) async-start(), calls=%async_computation.14 | async-start | bytes 10616832 | tf_op jit(solution)/shard_map/reduce_scatter | solution.py:654
  611.2 236.4 %reduce-scatter.12.cloned.1.call-start = ((), (), s32[]{:S(2)}) async-start(), calls=%async_computation.13 | async-start | bytes 10616832 | tf_op jit(solution)/shard_map/reduce_scatter | solution.py:652
  628.2 223.5 %reduce-scatter.6.cloned.1.call-start = ((), (), s32[]{:S(2)}) async-start(), calls=%async_computation.10 | async-start | bytes 7962624 | tf_op jit(solution)/shard_map/reduce_scatter | solution.py:679
  645.0 243.8 %reduce-scatter.10.cloned.1.call-start = ((), (), s32[]{:S(2)}) async-start(), calls=%async_computation.12 | async-start | bytes 2949120 | tf_op jit(solution)/shard_map/reduce_scatter | solution.py:665
  697.9 50.9 %collective-permute-start.23 = (bf16[336,1536]{1,0:T(8,128)(2,1)S(1)}, bf16[336,1536]{1,0:T(8,128)(2,1)}, u32[]{:S(2)}, u32[]{:S(2)}) collective-permute-start(bf16[336,1536]{1,0:T(8,128)(2,1)S(1)} %get-tuple-element.158), channel_id=1, source_target_pairs={{0,1},{1,2},{2,3},{4,5},{5,6},{6,7},{8,9},{9,10},{10,11},{12,13},{... | collective-permute-start | bytes 3096584 | tf_op jit(solution)/shard_map/ppermute | solution.py:526
  706.9 35.7 %collective-permute-start.36 = (bf16[336,1536]{1,0:T(8,128)(2,1)}, bf16[336,1536]{1,0:T(8,128)(2,1)}, u32[]{:S(2)}, u32[]{:S(2)}) collective-permute-start(bf16[336,1536]{1,0:T(8,128)(2,1)} %get-tuple-element.152), channel_id=1, source_target_pairs={{0,1},{1,2},{2,3},{4,5},{5,6},{6,7},{8,9},{9,10},{10,11},{12,13},{... | collective-permute-start | bytes 3096584 | tf_op jit(solution)/shard_map/ppermute | solution.py:526
  721.2 27.9 %collective-permute-start.26 = (bf16[336,1536]{1,0:T(8,128)(2,1)}, bf16[336,1536]{1,0:T(8,128)(2,1)}, u32[]{:S(2)}, u32[]{:S(2)}) collective-permute-start(bf16[336,1536]{1,0:T(8,128)(2,1)} %fusion.27), channel_id=1, source_target_pairs={{1,0},{2,1},{3,2},{5,4},{6,5},{7,6},{9,8},{10,9},{11,10},{13,12},{... | collective-permute-start | bytes 3096584 | tf_op jit(solution)/shard_map/ppermute | solution.py:526
  722.6 42.0 %collective-permute-start.39 = (bf16[336,1536]{1,0:T(8,128)(2,1)S(1)}, bf16[336,1536]{1,0:T(8,128)(2,1)S(1)}, u32[]{:S(2)}, u32[]{:S(2)}) collective-permute-start(bf16[336,1536]{1,0:T(8,128)(2,1)S(1)} %get-tuple-element.153), channel_id=1, source_target_pairs={{1,0},{2,1},{3,2},{5,4},{6,5},{7,6},{9,8},{10,9},{11,10},{13,12},{... | collective-permute-start | bytes 3096584 | tf_op jit(solution)/shard_map/ppermute | solution.py:526
  783.6 53.1 %collective-permute-start.38 = (bf16[336,1536]{1,0:T(8,128)(2,1)}, bf16[336,1536]{1,0:T(8,128)(2,1)S(1)}, u32[]{:S(2)}, u32[]{:S(2)}) collective-permute-start(bf16[336,1536]{1,0:T(8,128)(2,1)} %get-tuple-element.150), channel_id=1, source_target_pairs={{0,1},{1,2},{2,3},{4,5},{5,6},{6,7},{8,9},{9,10},{10,11},{12,13},{... | collective-permute-start | bytes 3096584 | tf_op jit(solution)/shard_map/ppermute | solution.py:526
  791.4 45.2 %collective-permute-start.41 = (bf16[336,1536]{1,0:T(8,128)(2,1)}, bf16[336,1536]{1,0:T(8,128)(2,1)S(1)}, u32[]{:S(2)}, u32[]{:S(2)}) collective-permute-start(bf16[336,1536]{1,0:T(8,128)(2,1)} %fusion.17), channel_id=1, source_target_pairs={{1,0},{2,1},{3,2},{5,4},{6,5},{7,6},{9,8},{10,9},{11,10},{13,12},{... | collective-permute-start | bytes 3096584 | tf_op jit(solution)/shard_map/ppermute | solution.py:526
  (63 other events, 921.6 us)
Sparse Core Ops, SparseCore 0:
  10.5 32.8 all-gather.13
  45.8 48.5 all-gather.11
  96.9 58.8 all-gather.15
  157.5 58.8 all-gather.19
  218.1 58.8 all-gather.17
  594.8 34.8 all-reduce.11
Sparse Core Ops, SparseCore 1:
  23.6 74.3 all-reduce.9
  497.4 77.0 reduce-scatter.7
  611.2 76.9 reduce-scatter.13
  692.1 76.3 reduce-scatter.11
  772.4 65.7 reduce-scatter.5
  841.1 47.7 reduce-scatter.9

commit v2 on v1

v2 whole, which is shorter than its diff:
```python
import functools
import math

import jax
import jax.numpy as jnp
from jax import lax
from jax.experimental import pallas as pl
from jax.experimental.pallas import tpu as pltpu
from jax.sharding import PartitionSpec as P

HD = 64
LANES = 128
EPSILON = 1e-06
GELU_ROOT = math.sqrt(2.0 / math.pi)
GELU_CUBE = 0.044715
MASKED = -1e30
SINGLE = jnp.float32
HALF = jnp.bfloat16
MEGA = 2**20


def up(value, multiple):
    return -(-value // multiple) * multiple


def params(limit=56):
    return pltpu.CompilerParams(vmem_limit_bytes=limit * MEGA)


def remote(collective, limit=56):
    return pltpu.CompilerParams(
        collective_id=collective, has_side_effects=True, vmem_limit_bytes=limit * MEGA
    )


def cost(flops, nbytes, trans=0):
    return pl.CostEstimate(flops=int(flops), bytes_accessed=int(nbytes), transcendentals=int(trans))


def nt_dot(a, b):
    return lax.dot_general(a, b, (((1,), (1,)), ((), ())), preferred_element_type=SINGLE)


def tn_dot(a, b):
    return lax.dot_general(a, b, (((0,), (0,)), ((), ())), preferred_element_type=SINGLE)


def nn_dot(a, b):
    return jnp.dot(a, b, preferred_element_type=SINGLE)


def layer_norm(values):
    center = values - jnp.mean(values, axis=-1, keepdims=True)
    inv_std = lax.rsqrt(jnp.mean(center * center, axis=-1, keepdims=True) + EPSILON)
    return (center * inv_std, inv_std)


def norm_back(normed, inv_std, upstream):
    first = jnp.mean(upstream, axis=-1, keepdims=True)
    second = jnp.mean(upstream * normed, axis=-1, keepdims=True)
    return inv_std * (upstream - first - normed * second)


def gelu_both(values):
    square = values * values
    inner = GELU_ROOT * (values + GELU_CUBE * square * values)
    tangent = jnp.tanh(inner)
    half = 0.5 * (1.0 + tangent)
    slope = half + 0.5 * values * (1.0 - tangent * tangent) * GELU_ROOT * (
        1.0 + 3.0 * GELU_CUBE * square
    )
    return values * half, slope


def silu_slope(values):
    sigma = jax.nn.sigmoid(values)
    return sigma + values * sigma * (1.0 - sigma)


def whole(shape, single=False):
    zeros = (0,) * len(shape)
    if single:
        return pl.BlockSpec(shape, lambda *_: zeros, pipeline_mode=pl.Buffered(1))
    return pl.BlockSpec(shape, lambda *_: zeros)


def rows_spec(rows, width):
    return pl.BlockSpec((1, rows, width), lambda s: (s, 0, 0))


MESH = pl.DeviceIdType.MESH


def on_line(position):
    return {"seq": position}


def both(first, second):
    return jnp.logical_and(first, second)


def flip(value, mask):
    bit = 1
    while bit <= mask:
        if mask & bit:
            value = value + bit - 2 * bit * lax.rem(lax.div(value, bit), 2)
        bit *= 2
    return value


def greet(n, line=None, group=None):
    me, my = lax.axis_index("seq"), lax.axis_index("dp")
    dp = lax.axis_size("dp")
    barrier = pltpu.get_barrier_semaphore()
    peers = []
    if line == "all":
        peers += [on_line(lax.rem(me + offset, n)) for offset in range(1, n)]
    if group == "all":
        peers += [{"dp": lax.rem(my + offset, dp)} for offset in range(1, dp)]
    if group == "paths":
        peers += [{"dp": flip(my, 1)}] + [{"dp": flip(my, mask)} for mask in masks_of(dp)]
    for peer in peers:
        pl.semaphore_signal(barrier, inc=1, device_id=peer, device_id_type=MESH)
    if line == "near":
        for sign in (1, -1):
            near = me + sign

            @pl.when(both(near >= 0, near < n))
            def _():
                pl.semaphore_signal(barrier, inc=1, device_id=on_line(near), device_id_type=MESH)

    count = len(peers)
    if line == "near":
        count = count + lax.min(me, 1) + lax.min(n - 1 - me, 1)
    pl.semaphore_wait(barrier, count)


def masks_of(dp):
    masks, bit = [], 2
    while bit < dp:
        masks.append(bit)
        bit *= 2
    return masks


class GroupGather:
    def __init__(self, src, out, send, recv, pass_send, pass_recv, local):
        self.src, self.out = src, out
        self.send, self.recv, self.local = send, recv, local
        self.pass_send, self.pass_recv = pass_send, pass_recv
        self.my = lax.axis_index("dp")
        masks = masks_of(out.shape[0])
        self.orders = (masks, masks[::-1])
        self.phases = len(masks)

    @staticmethod
    def scratch(dp):
        return [pltpu.SemaphoreType.DMA((2, dp // 2)) for _ in range(4)] + [
            pltpu.SemaphoreType.DMA
        ]

    def span(self, half, count):
        mask = 0
        for k in range(self.phases):
            if count >> k & 1:
                mask |= self.orders[half][k]
        return mask

    def copy(self, half, phase, count, block):
        src = self.src.at[half] if count == 0 else self.out.at[block, half]
        index = 2**phase - 1 + count
        return pltpu.make_async_remote_copy(
            src_ref=src,
            dst_ref=self.out.at[block, half],
            send_sem=self.send.at[half, index],
            recv_sem=self.recv.at[half, index],
            device_id={"dp": flip(self.my, self.orders[half][phase])},
            device_id_type=MESH,
        )

    def hand(self, half, index, block, own=False):
        src = self.src.at[half] if own else self.out.at[block, half]
        return pltpu.make_async_remote_copy(
            src_ref=src,
            dst_ref=self.out.at[block, half],
            send_sem=self.pass_send.at[half, index],
            recv_sem=self.pass_recv.at[half, index],
            device_id={"dp": flip(self.my, 1)},
            device_id_type=MESH,
        )

    def begin(self):
        for half in range(2):
            self.copy(half, 0, 0, self.my).start()
        for half in range(2):
            self.hand(half, 0, self.my, True).start()
        pltpu.make_async_copy(self.src, self.out.at[self.my], self.local).start()

    def arrive(self, phase):
        for half in range(2):
            mask = self.orders[half][phase]
            for count in range(2**phase):
                block = flip(self.my, mask ^ self.span(half, count))
                self.copy(half, phase, count, block).wait_recv()
            if phase + 1 < self.phases:
                for count in range(2 ** (phase + 1)):
                    block = flip(self.my, self.span(half, count))
                    self.copy(half, phase + 1, count, block).start()
            for count in range(2**phase):
                block = flip(self.my, mask ^ self.span(half, count))
                self.hand(half, 2**phase + count, block).start()

    def finish(self):
        pltpu.make_async_copy(self.src, self.out.at[self.my], self.local).wait()
        other = flip(self.my, 1)
        for half in range(2):
            self.hand(half, 0, other, True).wait()
            for phase in range(self.phases):
                mask = self.orders[half][phase]
                for count in range(2**phase):
                    self.copy(half, phase, count, self.my).wait_send()
                    block = flip(other, mask ^ self.span(half, count))
                    self.hand(half, 2**phase + count, block).wait()


class LineGather:
    def __init__(self, n, src, out, send, recv, local, first=0, stop=None, land=None):
        self.n, self.src, self.out, self.land = n, src, out, land
        self.send, self.recv, self.local = send, recv, local
        self.first, self.stop = first, n - 1 if stop is None else stop
        self.me = lax.axis_index("seq")

    @staticmethod
    def scratch(n):
        return [
            pltpu.SemaphoreType.DMA((2, n - 1)),
            pltpu.SemaphoreType.DMA((2, n - 1)),
            pltpu.SemaphoreType.DMA,
        ]

    def inside(self, position):
        return both(position >= 0, position < self.n)

    def copy(self, way, hop, block, near):
        if hop > self.first:
            src = self.out.at[block]
        else:
            src = self.src if hop == 0 else self.src.at[way]
        return pltpu.make_async_remote_copy(
            src_ref=src,
            dst_ref=self.out.at[block] if self.land is None else self.land.at[way],
            send_sem=self.send.at[way, hop],
            recv_sem=self.recv.at[way, hop],
            device_id=on_line(near),
            device_id_type=MESH,
        )

    def each(self, hop):
        for way, sign in ((0, 1), (1, -1)):
            yield way, sign, self.me - sign * hop, self.me + sign

    def begin(self):
        self.launch(self.first)

    def launch(self, hop):
        for way, sign, block, near in self.each(hop):

            @pl.when(both(self.inside(block), self.inside(near)))
            def _():
                self.copy(way, hop, block, near).start()

    def keep(self):
        return pltpu.make_async_copy(self.src, self.out.at[self.me], self.local)

    def arrive(self, hop):
        for way, sign, block, near in self.each(hop + 1):

            @pl.when(self.inside(block))
            def _():
                self.copy(way, hop, block, near).wait_recv()

        if hop + 1 < self.stop:
            self.launch(hop + 1)

    def finish(self):
        for hop in range(self.first, self.stop):
            for way, sign, block, near in self.each(hop):

                @pl.when(both(self.inside(block), self.inside(near)))
                def _():
                    self.copy(way, hop, block, near).wait_send()


class LineSum:
    def __init__(self, n, part, out, got, mine, passed, send, recv, load, first=0, stop=None, tail=None, prev=None):
        self.n, self.part, self.out = n, part, out
        self.got, self.mine, self.passed = got, mine, passed
        self.send, self.recv, self.load = send, recv, load
        self.first, self.stop = first, n - 1 if stop is None else stop
        self.tail, self.prev = tail, prev
        self.me = lax.axis_index("seq")

    @staticmethod
    def scratch(n, rows, width, first=0, stop=None):
        stop = n - 1 if stop is None else stop
        return [
            pltpu.VMEM((2, stop - first + (first > 0), rows, width), HALF),
            pltpu.VMEM((2, rows, width), HALF),
            pltpu.VMEM((2, max(stop - max(first, 1), 1), rows, width), HALF),
            pltpu.SemaphoreType.DMA((2, n - 1)),
            pltpu.SemaphoreType.DMA((2, n - 1)),
            pltpu.SemaphoreType.DMA((2, 2)),
        ]

    def inside(self, position):
        return both(position >= 0, position < self.n)

    def each(self, step):
        reach = self.n - 1 - step
        for way, sign in ((0, 1), (1, -1)):
            yield way, self.me + sign * reach, self.me + sign, self.me - sign

    def slot(self, way, step):
        return self.passed.at[way, max(step - max(self.first, 1), 0)]

    def copy(self, way, step, src, near):
        if self.tail is not None and step == self.stop - 1:
            dst = self.tail.at[way]
        else:
            dst = self.got.at[way, step - self.first]
        return pltpu.make_async_remote_copy(
            src_ref=src,
            dst_ref=dst,
            send_sem=self.send.at[way, step],
            recv_sem=self.recv.at[way, step],
            device_id=on_line(near),
            device_id_type=MESH,
        )

    def round(self, step):
        for way, owner, near, behind in self.each(step):
            if step == 0:

                @pl.when(self.inside(owner))
                def _():
                    self.copy(way, step, self.part(owner), near).start()

                continue

            @pl.when(both(self.inside(owner), jnp.logical_not(self.inside(behind))))
            def _():
                self.copy(way, step, self.part(owner), near).start()

            @pl.when(both(self.inside(owner), self.inside(behind)))
            def _():
                fetch = pltpu.make_async_copy(
                    self.part(owner), self.mine.at[way], self.load.at[way, 0]
                )
                fetch.start()
                slot = self.slot(way, step)
                if step == self.first:
                    index = self.stop - self.first
                    held = pltpu.make_async_copy(
                        self.prev.at[way], self.got.at[way, index], self.load.at[way, 1]
                    )
                    held.start()
                    held.wait()
                else:
                    index = step - 1 - self.first
                    self.copy(way, step - 1, slot, near).wait_recv()
                fetch.wait()
                total = self.mine[way].astype(SINGLE) + self.got[way, index].astype(SINGLE)
                self.passed[way, step - max(self.first, 1)] = total.astype(HALF)
                self.copy(way, step, slot, near).start()

    def sent(self):
        for step in range(self.first, self.stop):
            for way, owner, near, behind in self.each(step):

                @pl.when(self.inside(owner))
                def _():
                    self.copy(way, step, self.slot(way, step), near).wait_send()

    def close(self):
        last = self.stop - 1
        for way, owner, near, behind in self.each(last + 1):

            @pl.when(both(self.inside(owner), self.inside(behind)))
            def _():
                self.copy(way, last, self.slot(way, last), near).wait_recv()

        self.sent()

    def finish(self):
        last = self.n - 2
        fetch = pltpu.make_async_copy(self.part(self.me), self.mine.at[0], self.load.at[0, 0])
        fetch.start()
        fetch.wait()
        self.out[...] = self.mine[0].astype(SINGLE)
        for way, owner, near, behind in self.each(last):

            @pl.when(self.inside(behind))
            def _():
                self.copy(way, last, self.slot(way, last), near).wait_recv()
                self.out[...] += self.got[way, last - self.first].astype(SINGLE)

        self.sent()


def at_rows(ref):
    return lambda owner: ref.at[owner]


def at_step(step, when, action):
    @pl.when(step == when)
    def _():
        action()


def to_group(my, dp, offset, src, dst, send, recv):
    peer = lax.rem(my + offset, dp)
    return pltpu.make_async_remote_copy(
        src_ref=src if src.shape == dst.shape[1:] else src.at[peer],
        dst_ref=dst.at[my],
        send_sem=send.at[offset - 1],
        recv_sem=recv.at[offset - 1],
        device_id={"dp": peer},
        device_id_type=MESH,
    )


def to_line(me, n, offset, src, dst, send, recv):
    peer = lax.rem(me + offset, n)
    return pltpu.make_async_remote_copy(
        src_ref=src if src.shape == dst.shape[1:] else src.at[peer],
        dst_ref=dst.at[me],
        send_sem=send.at[offset - 1],
        recv_sem=recv.at[offset - 1],
        device_id=on_line(peer),
        device_id_type=MESH,
    )


def start_kernel(
    n, dp, x_ref, act_ref, ada_ref, side_ref, qkv_ref, fc1_ref, x_all, side_all, acts, qkv_all, fc1_all,
    part, parts, row, a_send, a_recv, p_send, p_recv, s_send, s_recv, *sems,
):
    me, my = lax.axis_index("seq"), lax.axis_index("dp")
    depth, cols = ada_ref.shape
    greet(n, "all", "all")
    gather = LineGather(n, x_ref, x_all, *sems[:3])
    qkv = GroupGather(qkv_ref, qkv_all, *sems[3:8])
    fc1 = GroupGather(fc1_ref, fc1_all, *sems[8:13])
    gather.begin()
    others = range(1, dp)
    act_go = [to_group(my, dp, k, act_ref, acts, a_send, a_recv) for k in others]
    for copy in act_go:
        copy.start()
    gather.keep().start()
    acts[my] = act_ref[my]
    for copy in act_go:
        copy.wait_recv()
    product = nn_dot(acts[:, 0, :depth].astype(HALF), ada_ref[...])
    for k in range(dp):
        part[k] = product[k : k + 1]
    part_go = [to_group(my, dp, k, part, parts, p_send, p_recv) for k in others]
    for copy in part_go:
        copy.start()
    qkv.begin()
    fc1.begin()
    parts[my] = part[my]
    for copy in part_go:
        copy.wait_recv()
    row[...] = side_ref[...]
    row[:, :cols] += jnp.sum(parts[...], axis=0)
    row_go = [to_line(me, n, k, row, side_all, s_send, s_recv) for k in range(1, n)]
    for copy in row_go:
        copy.start()
    side_all[me] = row[...]
    for hop in range(max(n - 1, qkv.phases)):
        if hop < n - 1:
            gather.arrive(hop)
        if hop < qkv.phases:
            qkv.arrive(hop)
            fc1.arrive(hop)
    for copy in row_go:
        copy.wait()
    for copy in act_go + part_go:
        copy.wait_send()
    gather.keep().wait()
    gather.finish()
    qkv.finish()
    fc1.finish()


def start(n, dp, x_loc, act_parts, ada, side, qkv, fc1):
    rows, width = x_loc.shape
    cols = ada.shape[1]
    anywhere = pl.BlockSpec(memory_space=pl.ANY)
    inner = pl.BlockSpec(memory_space=pltpu.VMEM)
    return pl.pallas_call(
        functools.partial(start_kernel, n, dp),
        in_specs=[anywhere, inner, inner, inner, anywhere, anywhere],
        out_specs=[anywhere, inner, inner, anywhere, anywhere],
        out_shape=[
            jax.ShapeDtypeStruct((n, rows, width), HALF),
            jax.ShapeDtypeStruct((n,) + side.shape, SINGLE),
            jax.ShapeDtypeStruct(act_parts.shape, SINGLE),
            jax.ShapeDtypeStruct((dp,) + qkv.shape, HALF),
            jax.ShapeDtypeStruct((dp,) + fc1.shape, HALF),
        ],
        scratch_shapes=[
            pltpu.VMEM((dp, 1, cols), SINGLE),
            pltpu.VMEM((dp, 1, cols), SINGLE),
            pltpu.VMEM(side.shape, SINGLE),
            pltpu.SemaphoreType.DMA((dp - 1,)),
            pltpu.SemaphoreType.DMA((dp - 1,)),
            pltpu.SemaphoreType.DMA((dp - 1,)),
            pltpu.SemaphoreType.DMA((dp - 1,)),
            pltpu.SemaphoreType.DMA((n - 1,)),
            pltpu.SemaphoreType.DMA((n - 1,)),
        ]
        + LineGather.scratch(n)
        + GroupGather.scratch(dp)
        + GroupGather.scratch(dp),
        compiler_params=remote(1),
        cost_estimate=cost(10**6, 100 * MEGA),
        name="start",
    )(x_loc, act_parts, ada, side, qkv, fc1)


def qkv_kernel(n, img, x_ref, mod_ref, w_ref, b_ref, p_ref, a_ref, o_ref, p_line, *sems):
    step = pl.program_id(0)
    wide = o_ref.shape[2]
    gather = LineGather(n, p_ref, p_line, *sems)

    def begin():
        greet(n, "near")
        gather.begin()
        gather.keep().start()

    at_step(step, 0, begin)
    for t, sl in ((0, slice(0, img)), (1, slice(img, x_ref.shape[1]))):
        normed, _ = layer_norm(x_ref[0, sl].astype(SINGLE))
        a = (normed * (1.0 + mod_ref[t, 1:2]) + mod_ref[t, 0:1]).astype(HALF)
        a_ref[0, sl] = a
        o_ref[0, sl] = (
            nn_dot(a, w_ref[:, t * wide : (t + 1) * wide]) + b_ref[t : t + 1]
        ).astype(HALF)
    for hop in range(n - 1):
        at_step(step, min(n - 1, 2 * hop + 1), functools.partial(gather.arrive, hop))

    def finish():
        gather.keep().wait()
        gather.finish()

    at_step(step, n - 1, finish)


def project_qkv(n, img, x_all, mods, weight, bias, proj):
    _, rows, width = x_all.shape
    wide = weight.shape[1] // 2
    anywhere = pl.BlockSpec(memory_space=pl.ANY)
    return pl.pallas_call(
        functools.partial(qkv_kernel, n, img),
        grid=(n,),
        in_specs=[
            rows_spec(rows, width),
            whole(mods.shape),
            whole(weight.shape, True),
            whole(bias.shape),
            anywhere,
        ],
        out_specs=[rows_spec(rows, width), rows_spec(rows, wide), anywhere],
        out_shape=[
            jax.ShapeDtypeStruct((n, rows, width), HALF),
            jax.ShapeDtypeStruct((n, rows, wide), HALF),
            jax.ShapeDtypeStruct((n,) + proj.shape, HALF),
        ],
        scratch_shapes=LineGather.scratch(n),
        compiler_params=remote(8),
        cost_estimate=cost(2 * n * rows * width * wide, 30 * MEGA),
        name="project_qkv",
    )(x_all, mods, weight, bias, proj)


def halves(shape):
    lane = lax.broadcasted_iota(jnp.int32, shape, len(shape) - 1)
    return lane < HD


def attn_kernel(
    n, q_ref, k_ref, v_ref, mask_ref, e_ref, p_ref, o_ref, lse_ref, e_near, mix_ref, p_all,
    o_buf, o_send, o_recv, o_local, *sems,
):
    pair, block = pl.program_id(0), pl.program_id(1)
    pairs = pl.num_programs(0)
    step = pair * n + block
    me = lax.axis_index("seq")
    count, rows, _ = k_ref.shape
    gather = LineGather(n, e_ref, None, *sems[:3], first=0, stop=1, land=e_near)
    proj = GroupGather(p_ref, p_all, *sems[3:])

    def begin():
        greet(n, "all", "paths")
        gather.begin()
        proj.begin()

    at_step(step, 0, begin)
    queries = q_ref[0] * HALF(1.0 / math.sqrt(HD))
    keys = k_ref[...].reshape(n * rows, LANES)
    values = v_ref[...].reshape(n * rows, LANES)
    first = halves(queries.shape)
    outs, logs = [], []
    for head in range(2):
        own = first if head == 0 else jnp.logical_not(first)
        scores = nt_dot(jnp.where(own, queries, HALF(0)), keys) + mask_ref[...]
        maxima = jnp.max(scores, axis=-1, keepdims=True)
        raised = jnp.exp(scores - maxima)
        totals = jnp.sum(raised, axis=-1, keepdims=True)
        weights = (raised * (1.0 / totals)).astype(HALF)
        outs.append(nn_dot(weights, values))
        logs.append(maxima + jnp.log(totals))
    mixed = jnp.where(first, outs[0], outs[1]).astype(HALF)
    o_ref[0] = mixed
    o_buf[pair, block] = mixed
    lse_ref[0] = jnp.where(first, logs[0], logs[1])
    static_pairs = o_buf.shape[0]

    def columns(sender, which):
        start = (sender * static_pairs + which) * LANES
        return mix_ref.at[:, pl.ds(pl.multiple_of(start, LANES), LANES)]

    def away(which, offset):
        peer = lax.rem(me + offset, n)
        return pltpu.make_async_remote_copy(
            src_ref=o_buf.at[which, peer],
            dst_ref=columns(me, which),
            send_sem=o_send.at[which, offset - 1],
            recv_sem=o_recv.at[which, offset - 1],
            device_id=on_line(peer),
            device_id_type=MESH,
        )

    for offset in range(1, n):

        @pl.when(block == lax.rem(me + offset, n))
        def _():
            away(pair, offset).start()

    @pl.when(block == me)
    def _():
        pltpu.make_async_copy(o_buf.at[pair, me], columns(me, pair), o_local.at[pair]).start()

    last = static_pairs * n - 1
    for phase in range(proj.phases):
        at_step(step, min(last, 5 * phase + 5), functools.partial(proj.arrive, phase))

    def finish():
        gather.arrive(0)
        proj.finish()
        for which in range(static_pairs):
            pltpu.make_async_copy(o_buf.at[which, me], columns(me, which), o_local.at[which]).wait()
            for offset in range(1, n):
                away(which, offset).wait()
        gather.finish()

    at_step(step, last, finish)


def attend(n, dp, qkv, mask, e_loc, proj):
    _, rows, wide = qkv.shape
    width = e_loc.shape[1]
    pairs = wide // 3 // LANES
    total = n * rows
    block = pl.BlockSpec((1, rows, LANES), lambda h, s: (s, 0, h))
    anywhere = pl.BlockSpec(memory_space=pl.ANY)
    return pl.pallas_call(
        functools.partial(attn_kernel, n),
        grid=(pairs, n),
        in_specs=[
            block,
            pl.BlockSpec((n, rows, LANES), lambda h, s: (0, 0, pairs + h)),
            pl.BlockSpec((n, rows, LANES), lambda h, s: (0, 0, 2 * pairs + h)),
            whole(mask.shape),
            anywhere,
            anywhere,
        ],
        out_specs=[block, block, anywhere, anywhere, anywhere],
        out_shape=[
            jax.ShapeDtypeStruct((n, rows, pairs * LANES), HALF),
            jax.ShapeDtypeStruct((n, rows, pairs * LANES), SINGLE),
            jax.ShapeDtypeStruct((2, rows, width), HALF),
            jax.ShapeDtypeStruct((rows, n * pairs * LANES), HALF),
            jax.ShapeDtypeStruct((dp,) + proj.shape, HALF),
        ],
        scratch_shapes=[
            pltpu.VMEM((pairs, n, rows, LANES), HALF),
            pltpu.SemaphoreType.DMA((pairs, n - 1)),
            pltpu.SemaphoreType.DMA((pairs, n - 1)),
            pltpu.SemaphoreType.DMA((pairs,)),
        ]
        + LineGather.scratch(n)
        + GroupGather.scratch(dp),
        compiler_params=remote(2),
        cost_estimate=cost(2 * 2 * 4 * pairs * total * total * LANES, 20 * MEGA, 2 * pairs * total * total),
        name="attend",
    )(qkv, qkv, qkv, mask, e_loc, proj)


def attn_back_kernel(
    lines, img, pairs, q_ref, k_ref, v_ref, o_ref, g_ref, lse_ref, mask_ref, y_ref, l_ref, r_ref,
    dq_ref, dk_ref, dv_ref, qb_ref, vb_ref, sum_ref, p_ref,
    acc_ref, lse_row, delta_row, turned, *line_scratch,
):
    linear = pl.program_id(0)
    attn_steps = pairs * lines
    step = lax.rem(linear, lines)
    n, rows, _ = q_ref.shape
    total = n * rows
    line = LineSum(lines, at_rows(y_ref), sum_ref, *line_scratch)

    def begin():
        greet(lines, "near")
        line.round(0)

    at_step(linear, 0, begin)

    @pl.when(linear < attn_steps)
    def _():
        grads = g_ref[...].reshape(total, LANES)
        queries = q_ref[...].reshape(total, LANES) * HALF(1.0 / math.sqrt(HD))

        @pl.when(step == 0)
        def _():
            acc_ref[...] = jnp.zeros_like(acc_ref)
            product = grads.astype(SINGLE) * o_ref[...].reshape(total, LANES).astype(SINGLE)
            flipped = product.T
            logs = lse_ref[...].reshape(total, LANES).T
            for head in range(2):
                delta_row[head : head + 1] = jnp.sum(
                    flipped[head * HD : (head + 1) * HD], axis=0, keepdims=True
                )
                lse_row[head : head + 1] = logs[head * HD : head * HD + 1]
            vb_ref[0] = jnp.zeros_like(vb_ref[0])

        keys, values = k_ref[0], v_ref[0]
        first = halves(keys.shape)
        mask = mask_ref[0][:, 0:1]
        dks, dvs = [], []
        for head in range(2):
            own = first if head == 0 else jnp.logical_not(first)
            key_own = jnp.where(own, keys, HALF(0))
            scores = nt_dot(key_own, queries)
            probs = jnp.exp((scores - lse_row[head : head + 1]) + mask)
            grad_prob = nt_dot(jnp.where(own, values, HALF(0)), grads)
            grad_score = (probs * (grad_prob - delta_row[head : head + 1])).astype(HALF)
            dvs.append(nn_dot(probs.astype(HALF), grads))
            dks.append(nn_dot(grad_score, queries))
            acc_ref[...] += tn_dot(grad_score, key_own)
        dk_ref[0] = jnp.where(first, dks[0], dks[1]).astype(HALF)
        dv = jnp.where(first, dvs[0], dvs[1])
        dv_ref[0] = dv.astype(HALF)
        vb_ref[0, 0:1] += jnp.sum(dv[:img], axis=0, keepdims=True)
        vb_ref[0, 1:2] += jnp.sum(dv[img:], axis=0, keepdims=True)

        @pl.when(step == lines - 1)
        def _():
            dq = (acc_ref[...] * (1.0 / math.sqrt(HD))).reshape(n, rows, LANES)
            dq_ref[...] = dq.astype(HALF)
            qb_ref[0, 0:1] = jnp.sum(jnp.sum(dq[:, :img], axis=0), axis=0, keepdims=True)
            qb_ref[0, 1:2] = jnp.sum(jnp.sum(dq[:, img:], axis=0), axis=0, keepdims=True)

    for t, sl in ((0, slice(0, img)), (1, slice(img, rows))):

        @pl.when(linear == attn_steps)
        def _():
            turned[:, sl] = l_ref[sl].T

        @pl.when(both(linear >= attn_steps, lax.rem(linear - attn_steps, 2) == t))
        def _():
            p_ref[...] = nn_dot(turned[:, sl], r_ref[sl]).astype(HALF)

    for hop in range(1, lines - 1):
        at_step(linear, 6 * hop, functools.partial(line.round, hop))
    at_step(linear, attn_steps + 2 * lines - 1, line.finish)


def attend_back(n, img, qkv, mixture, grad_mix, lse, mask_col, out_parts, grad_attn, mix_loc):
    _, rows, wide = qkv.shape
    pairs = wide // 3 // LANES
    total = n * rows
    lw = pairs * LANES
    steps = pairs * n
    width = out_parts.shape[2]

    def head(k):
        return lax.min(lax.div(k, n), pairs - 1)

    def place(k):
        return lax.select(k < steps, lax.rem(k, n), n - 1)

    def later(k):
        return lax.max(k - steps, 0)

    full = pl.BlockSpec((n, rows, LANES), lambda k: (0, 0, head(k)))

    def block(base):
        return pl.BlockSpec((1, rows, LANES), lambda k: (place(k), 0, base + head(k)))

    bias = pl.BlockSpec((1, 2, LANES), lambda k: (head(k), 0, 0))
    anywhere = pl.BlockSpec(memory_space=pl.ANY)
    return pl.pallas_call(
        functools.partial(attn_back_kernel, n, img, pairs),
        grid=(steps + 2 * n,),
        in_specs=[
            full,
            block(pairs),
            block(2 * pairs),
            full,
            full,
            full,
            pl.BlockSpec((1, rows, LANES), lambda k: (place(k), 0, 0)),
            anywhere,
            whole(grad_attn.shape, True),
            pl.BlockSpec((rows, lw), lambda k: (0, lax.div(later(k), 2))),
        ],
        out_specs=[
            full,
            block(0),
            block(0),
            bias,
            bias,
            whole(out_parts.shape[1:], True),
            pl.BlockSpec((width, lw), lambda k: (0, later(k))),
        ],
        out_shape=[jax.ShapeDtypeStruct((n, rows, lw), HALF)] * 3
        + [jax.ShapeDtypeStruct((pairs, 2, LANES), SINGLE)] * 2
        + [
            jax.ShapeDtypeStruct(out_parts.shape[1:], SINGLE),
            jax.ShapeDtypeStruct((width, 2 * n * lw), HALF),
        ],
        scratch_shapes=[
            pltpu.VMEM((total, LANES), SINGLE),
            pltpu.VMEM((2, total), SINGLE),
            pltpu.VMEM((2, total), SINGLE),
            pltpu.VMEM((width, rows), HALF),
        ]
        + LineSum.scratch(n, rows, width),
        compiler_params=remote(3, 60),
        cost_estimate=cost(2 * 5 * 4 * pairs * total * total * LANES, 30 * MEGA, 2 * pairs * total * total),
        name="attend_back",
    )(qkv, qkv, qkv, mixture, grad_mix, lse, mask_col, out_parts, grad_attn, mix_loc)


def proj_columns(w_ref, z, t):
    dp, n, depth, cols = w_ref.shape
    half = cols // 2
    return w_ref[:, z, :, t * half : (t + 1) * half].reshape(dp * depth, half)


def middle_kernel(
    n, img, mix_ref, x_ref, w_ref, b_ref, mod_ref, fc2_ref, y_ref, m_ref, all_ref, fc2_all, own, *sems
):
    greet(n, "near", "paths")
    fc2 = GroupGather(fc2_ref, fc2_all, *sems[3:])
    fc2.begin()
    lw = mix_ref.shape[1] // n
    heads = w_ref.shape[3] // 2
    for t, sl in ((0, slice(0, img)), (1, slice(img, x_ref.shape[0]))):
        attn = b_ref[t : t + 1]
        for z in range(n):
            attn = attn + nt_dot(mix_ref[sl, z * lw : z * lw + heads], proj_columns(w_ref, z, t))
        y_ref[sl] = attn
        middle = x_ref[sl].astype(SINGLE) + mod_ref[t, 2:3] * attn
        m_ref[sl] = middle
        normed, _ = layer_norm(middle)
        own[sl] = (normed * (1.0 + mod_ref[t, 4:5]) + mod_ref[t, 3:4]).astype(HALF)
    gather = LineGather(n, own, all_ref, *sems[:3])
    gather.begin()
    gather.keep().start()
    for hop in range(max(n - 1, fc2.phases)):
        if hop < fc2.phases:
            fc2.arrive(hop)
        if hop < n - 1:
            gather.arrive(hop)
    gather.keep().wait()
    gather.finish()
    fc2.finish()


def middle_rows(n, dp, img, mixture, x_loc, weight, bias, mods, fc2):
    rows, width = x_loc.shape
    inner = pl.BlockSpec(memory_space=pltpu.VMEM)
    anywhere = pl.BlockSpec(memory_space=pl.ANY)
    return pl.pallas_call(
        functools.partial(middle_kernel, n, img),
        in_specs=[inner] * 5 + [anywhere],
        out_specs=[inner, inner, anywhere, anywhere],
        out_shape=[
            jax.ShapeDtypeStruct((rows, width), SINGLE),
            jax.ShapeDtypeStruct((rows, width), SINGLE),
            jax.ShapeDtypeStruct((n, rows, width), HALF),
            jax.ShapeDtypeStruct((dp,) + fc2.shape, HALF),
        ],
        scratch_shapes=[pltpu.VMEM((rows, width), HALF)]
        + LineGather.scratch(n)
        + GroupGather.scratch(dp),
        compiler_params=remote(4),
        cost_estimate=cost(2 * rows * width * width, 100 * MEGA),
        name="middle_rows",
    )(mixture, x_loc, weight, bias, mods, fc2)


def by_distance(me, n, count):
    low = lax.min(me, n - 1 - me)
    near = lax.select(lax.rem(count, 2) == 1, lax.div(count + 1, 2), -lax.div(count, 2))
    far = lax.select(me < n - 1 - me, count - low, low - count)
    return me + lax.select(count <= 2 * low, near, far)


def mlp_kernel(n, img, tile, b_ref, e_loc, e_near, mod_ref, w1_ref, b1_ref, w2_ref,
    g_ref, dz_ref, dy_ref, db_ref, y_ref, sum_ref, gate_ref, acc_ref, out_ref, e_all, near_sem, *sems):
    step = pl.program_id(0)
    me = lax.axis_index("seq")
    owner = by_distance(me, n, step)
    e_ref = e_all.at[pl.ds(owner, 1)]
    gather = LineGather(n, e_near, e_all, *sems, first=1)
    own = pltpu.make_async_copy(e_loc, e_all.at[me], near_sem.at[2])

    def nears(action):
        for way, sign in ((0, 1), (1, -1)):
            block = me - sign

            @pl.when(both(block >= 0, block < n))
            def _():
                action(
                    pltpu.make_async_copy(e_near.at[way], e_all.at[block], near_sem.at[way])
                )

    def begin():
        greet(n, "near")
        gather.begin()
        own.start()
        nears(lambda copy: copy.start())
        own.wait()
        nears(lambda copy: copy.wait())

    at_step(step, 0, begin)
    for hop in range(1, n - 1):
        at_step(step, hop + 1, functools.partial(gather.arrive, hop))
    at_step(step, n - 1, gather.finish)
    units = g_ref.shape[2]

    @pl.when(step == 0)
    def _():
        sum_ref[...] = jnp.zeros_like(sum_ref)
        gate_ref[...] = jnp.zeros_like(gate_ref)

    for t, sl in ((0, slice(0, img)), (1, slice(img, b_ref.shape[1]))):
        rows = b_ref[0, sl]
        grad = (mod_ref[t, 5:6] * e_ref[0, sl].astype(SINGLE)).astype(HALF)
        dy_ref[0, sl] = grad

        for k in range(units // tile):
            here = slice(k * tile, (k + 1) * tile)
            cols = slice(t * units + k * tile, t * units + (k + 1) * tile)
            w1 = w1_ref[:, cols]
            pre = nn_dot(rows, w1) + b1_ref[t : t + 1, here]
            hidden, slope = gelu_both(pre)
            hidden = hidden.astype(HALF)
            g_ref[0, sl, here] = hidden
            w2 = w2_ref[:, cols]
            out = nt_dot(hidden, w2)
            dz = nn_dot(grad, w2) * slope
            sum_ref[t : t + 1, here] += jnp.sum(dz, axis=0, keepdims=True)
            dzh = dz.astype(HALF)
            dz_ref[0, sl, here] = dzh
            part = nt_dot(dzh, w1)
            if k == 0:
                acc_ref[sl] = part
                out_ref[sl] = out
            else:
                acc_ref[sl] += part
                out_ref[sl] += out
        db_ref[0, sl] = acc_ref[sl].astype(HALF)
        out = out_ref[sl]
        y_ref[0, sl] = out.astype(HALF)
        gate_ref[t : t + 1] += jnp.sum(out * e_ref[0, sl].astype(SINGLE), axis=0, keepdims=True)


def feed_forward(n, img, mlp_in, e_loc, e_near, mods, w1, b1, w2):
    rows, width = mlp_in.shape[1:]
    units = w1.shape[1] // 2
    tile = min(512, units)
    while units % tile:
        tile -= LANES

    def owned(columns):
        return pl.BlockSpec(
            (1, rows, columns), lambda k: (by_distance(lax.axis_index("seq"), n, k), 0, 0)
        )

    return pl.pallas_call(
        functools.partial(mlp_kernel, n, img, tile),
        grid=(n,),
        in_specs=[
            owned(width),
            pl.BlockSpec(memory_space=pl.ANY),
            pl.BlockSpec(memory_space=pl.ANY),
            whole(mods.shape),
            whole(w1.shape, True),
            whole(b1.shape),
            whole(w2.shape, True),
        ],
        out_specs=[
            owned(units),
            owned(units),
            owned(width),
            owned(width),
            owned(width),
            whole((2, units)),
            whole((2, width)),
        ],
        out_shape=[
            jax.ShapeDtypeStruct((n, rows, units), HALF),
            jax.ShapeDtypeStruct((n, rows, units), HALF),
            jax.ShapeDtypeStruct((n, rows, width), HALF),
            jax.ShapeDtypeStruct((n, rows, width), HALF),
            jax.ShapeDtypeStruct((n, rows, width), HALF),
            jax.ShapeDtypeStruct((2, units), SINGLE),
            jax.ShapeDtypeStruct((2, width), SINGLE),
        ],
        scratch_shapes=[
            pltpu.VMEM((rows, width), SINGLE),
            pltpu.VMEM((rows, width), SINGLE),
            pltpu.VMEM((n, rows, width), HALF),
            pltpu.SemaphoreType.DMA((3,)),
        ]
        + LineGather.scratch(n),
        compiler_params=remote(9, 60),
        cost_estimate=cost(6 * n * rows * width * units, 50 * MEGA, n * rows * units),
        name="feed_forward",
    )(mlp_in, e_loc, e_near, mods, w1, b1, w2)


def grads_kernel(n, img, plan, rounds, *refs):
    lefts = max(p[0] for p in plan) + 1
    rights = max(p[1] for p in plan) + 1
    l_refs, r_refs = refs[:lefts], refs[lefts : lefts + rights]
    rest = refs[lefts + rights :]
    step = pl.program_id(0)
    if rounds:
        parts, o_ref, tail, turned = rest[:4]
        line = LineSum(n, at_rows(parts), None, *rest[4:], stop=n - 2, tail=tail)

        def begin():
            greet(n, "near")
            line.round(0)

        at_step(step, 0, begin)
    else:
        o_ref, turned = rest
    tile = o_ref.shape[1]
    before = None
    for k, (left, right, stream, column) in enumerate(plan):

        @pl.when(step == k)
        def _():
            l_ref, r_ref = l_refs[left], r_refs[right]
            count, rows, _ = l_ref.shape
            sl = slice(0, img) if stream == 0 else slice(img, rows)
            size = count * (sl.stop - sl.start)
            if before != (left, stream):
                turned[:, :size] = l_ref[:, sl].reshape(size, l_ref.shape[2]).T
            values = r_ref[:, sl, column : column + tile].reshape(size, tile)
            o_ref[...] = nn_dot(turned[:, :size], values).astype(HALF)

        before = (left, stream)
    if rounds:
        for hop, when in enumerate(rounds):
            at_step(step, when, functools.partial(line.round, hop + 1))
        at_step(step, len(plan) - 1, line.close)


def weight_grads(n, img, lefts, rights, plan, tile, name, rounds=(), parts=None, collective=None):
    rows, depth = lefts[0].shape[1:]
    in_specs = [whole(a.shape, True) for a in (*lefts, *rights)]
    out_specs = [pl.BlockSpec((depth, tile), lambda k: (0, k))]
    out_shape = [jax.ShapeDtypeStruct((depth, len(plan) * tile), HALF)]
    longest = max(up(n * img, LANES), up(n * (rows - img), LANES))
    scratch = [pltpu.VMEM((depth, longest), HALF)]
    arrays = (*lefts, *rights)
    if rounds:
        anywhere = pl.BlockSpec(memory_space=pl.ANY)
        in_specs.append(anywhere)
        out_specs.append(anywhere)
        out_shape.append(jax.ShapeDtypeStruct((2,) + parts.shape[1:], HALF))
        scratch += LineSum.scratch(n, *parts.shape[1:], stop=n - 2)
        arrays += (parts,)
    return pl.pallas_call(
        functools.partial(grads_kernel, n, img, plan, rounds),
        grid=(len(plan),),
        in_specs=in_specs,
        out_specs=out_specs,
        out_shape=out_shape,
        scratch_shapes=scratch,
        compiler_params=remote(collective, 60) if rounds else params(60),
        cost_estimate=cost(2 * n * rows * depth * len(plan) * tile // 2, 60 * MEGA),
        name=name,
    )(*arrays)


def middle_back_kernel(
    n, img, part_ref, prev_ref, m_ref, y_ref, e_ref, w_ref, mod_ref, dm_ref, dy_ref, sum_ref, all_ref,
    db_ref, mix, send, recv, local, *line_scratch,
):
    me = lax.axis_index("seq")
    rows, width = m_ref.shape
    heads = w_ref.shape[3] // 2
    streams = ((0, slice(0, img)), (1, slice(img, rows)))
    greet(n, "all")
    line = LineSum(n, at_rows(part_ref), db_ref, *line_scratch, first=n - 2, prev=prev_ref)
    line.round(n - 2)
    if mix.shape[2] > heads:
        mix[...] = jnp.zeros_like(mix)
    line.finish()
    for t, sl in streams:
        grad_in = db_ref[sl]
        normed, inv_std = layer_norm(m_ref[sl])
        upstream = e_ref[sl].astype(SINGLE)
        grad_middle = upstream + norm_back(normed, inv_std, grad_in * (1.0 + mod_ref[t, 4:5]))
        dm_ref[sl] = grad_middle
        grad_attn = mod_ref[t, 2:3] * grad_middle
        dy_ref[sl] = grad_attn.astype(HALF)

        def total(value):
            return jnp.sum(value, axis=0, keepdims=True)

        sum_ref[t, 0:1] = total(grad_middle * y_ref[sl])
        sum_ref[t, 1:2] = total(grad_in)
        sum_ref[t, 2:3] = total(grad_in * normed)
        sum_ref[t, 3:4] = total(grad_attn)
        sum_ref[t, 4:5] = total(upstream)

    def exchange(peer, block):
        return pltpu.make_async_remote_copy(
            src_ref=mix.at[peer],
            dst_ref=all_ref.at[block],
            send_sem=send.at[peer],
            recv_sem=recv.at[block],
            device_id=on_line(peer),
            device_id_type=MESH,
        )

    keep = pltpu.make_async_copy(mix.at[me], all_ref.at[me], local)
    for peer in range(n):
        for t, sl in streams:
            mix[peer, sl, :heads] = nn_dot(dy_ref[sl], proj_columns(w_ref, peer, t)).astype(HALF)

        @pl.when(peer != me)
        def _():
            exchange(peer, me).start()

        @pl.when(peer == me)
        def _():
            keep.start()

    for peer in range(n):

        @pl.when(peer != me)
        def _():
            exchange(peer, peer).wait()

    keep.wait()


def middle_back(n, img, parts, prev, middle, attn_out, cot, weight, mods, lwp):
    rows, width = middle.shape
    inner = pl.BlockSpec(memory_space=pltpu.VMEM)
    anywhere = pl.BlockSpec(memory_space=pl.ANY)
    return pl.pallas_call(
        functools.partial(middle_back_kernel, n, img),
        in_specs=[anywhere, anywhere] + [inner] * 5,
        out_specs=[inner, inner, inner, anywhere],
        out_shape=[
            jax.ShapeDtypeStruct((rows, width), SINGLE),
            jax.ShapeDtypeStruct((rows, width), HALF),
            jax.ShapeDtypeStruct((2, 8, width), SINGLE),
            jax.ShapeDtypeStruct((n, rows, lwp), HALF),
        ],
        scratch_shapes=[
            pltpu.VMEM((rows, width), SINGLE),
            pltpu.VMEM((n, rows, lwp), HALF),
            pltpu.SemaphoreType.DMA((n,)),
            pltpu.SemaphoreType.DMA((n,)),
            pltpu.SemaphoreType.DMA,
        ]
        + LineSum.scratch(n, rows, width, first=n - 2),
        compiler_params=remote(5),
        cost_estimate=cost(2 * rows * width * width, 60 * MEGA),
        name="middle_back",
    )(parts, prev, middle, attn_out, cot, weight, mods)


def attn_in_kernel(img, dq_ref, dk_ref, dv_ref, x_ref, w_ref, da_ref, sum_ref):
    lw = dq_ref.shape[2]

    @pl.when(pl.program_id(0) == 0)
    def _():
        sum_ref[...] = jnp.zeros_like(sum_ref)

    for t, sl in ((0, slice(0, img)), (1, slice(img, x_ref.shape[1]))):
        part = None
        for c, ref in enumerate((dq_ref, dk_ref, dv_ref)):
            start = (3 * t + c) * lw
            term = nt_dot(ref[0, sl], w_ref[:, start : start + lw])
            part = term if part is None else part + term
        da_ref[0, sl] = part.astype(HALF)
        normed, _ = layer_norm(x_ref[0, sl].astype(SINGLE))
        sum_ref[t, 0:1] += jnp.sum(part, axis=0, keepdims=True)
        sum_ref[t, 1:2] += jnp.sum(part * normed, axis=0, keepdims=True)


def attn_in_back(n, img, dq, dk, dv, x_all, weight):
    _, rows, lw = dq.shape
    width = x_all.shape[2]
    return pl.pallas_call(
        functools.partial(attn_in_kernel, img),
        grid=(n,),
        in_specs=[rows_spec(rows, lw)] * 3 + [rows_spec(rows, width), whole(weight.shape, True)],
        out_specs=[rows_spec(rows, width), whole((2, 2, width))],
        out_shape=[
            jax.ShapeDtypeStruct((n, rows, width), HALF),
            jax.ShapeDtypeStruct((2, 2, width), SINGLE),
        ],
        compiler_params=params(),
        cost_estimate=cost(6 * n * rows * width * lw, 30 * MEGA),
        name="attn_in_back",
    )(dq, dk, dv, x_all, weight)


def end_kernel(
    n, dp, cut, parts, packed, extra, ada_ref, sum_ref, every, cond_ref,
    z_got, row, c_part, c_got, c_all, z_send, z_recv, e_send, e_recv, c_send, c_recv, a_send, a_recv,
    *line_scratch,
):
    me, my = lax.axis_index("seq"), lax.axis_index("dp")
    depth = ada_ref.shape[0]
    span = packed.shape[2]
    greet(n, "all", "all")
    line = LineSum(n, at_rows(parts), sum_ref, *line_scratch)
    line.round(0)
    mates, others = range(1, n), range(1, dp)
    z_go = [to_line(me, n, k, packed, z_got, z_send, z_recv) for k in mates]
    for copy in z_go:
        copy.start()
    z_got[me] = packed[me]
    for copy in z_go:
        copy.wait_recv()
    row[:, :span] = jnp.sum(z_got[...], axis=0)
    row[:, span:] = extra[...]
    e_go = [to_group(my, dp, k, row, every, e_send, e_recv) for k in others]
    for copy in e_go:
        copy.start()
    every[my] = row[...]
    for copy in e_go:
        copy.wait_recv()
    product = nt_dot(every[:, 0, :cut].astype(HALF), ada_ref[...])
    c_part[...] = jnp.zeros_like(c_part)
    for k in range(dp):
        c_part[k, :, :depth] = product[k : k + 1]
    c_go = [to_group(my, dp, k, c_part, c_got, c_send, c_recv) for k in others]
    for copy in c_go:
        copy.start()
    c_got[my] = c_part[my]
    for copy in c_go:
        copy.wait_recv()
    a_go = [to_line(me, n, k, c_got, c_all, a_send, a_recv) for k in mates]
    for copy in a_go:
        copy.start()
    c_all[me] = c_got[...]
    for hop in range(1, n - 1):
        line.round(hop)
    for copy in a_go:
        copy.wait_recv()
    cond_ref[...] = jnp.sum(c_all[...], axis=0)
    for copy in z_go + e_go + c_go + a_go:
        copy.wait_send()
    line.finish()


def end(n, dp, cut, parts, packed, extra, ada):
    rows, width = parts.shape[1:]
    depth = up(ada.shape[0], LANES)
    span = packed.shape[2] + extra.shape[1]
    inner = pl.BlockSpec(memory_space=pltpu.VMEM)
    sems = [n - 1, n - 1, dp - 1, dp - 1, dp - 1, dp - 1, n - 1, n - 1]
    return pl.pallas_call(
        functools.partial(end_kernel, n, dp, cut),
        in_specs=[pl.BlockSpec(memory_space=pl.ANY), inner, inner, inner],
        out_specs=[inner] * 3,
        out_shape=[
            jax.ShapeDtypeStruct((rows, width), SINGLE),
            jax.ShapeDtypeStruct((dp, 1, span), SINGLE),
            jax.ShapeDtypeStruct((dp, 1, depth), SINGLE),
        ],
        scratch_shapes=[
            pltpu.VMEM(packed.shape, SINGLE),
            pltpu.VMEM((1, span), SINGLE),
            pltpu.VMEM((dp, 1, depth), SINGLE),
            pltpu.VMEM((dp, 1, depth), SINGLE),
            pltpu.VMEM((n, dp, 1, depth), SINGLE),
        ]
        + [pltpu.SemaphoreType.DMA((k,)) for k in sems]
        + LineSum.scratch(n, rows, width),
        compiler_params=remote(7),
        cost_estimate=cost(10**6, 100 * MEGA),
        name="end",
    )(parts, packed, extra, ada)


def proj_sum_kernel(n, wide, parts, sum_ref, *line_scratch):
    greet(n, "near")

    def part(owner):
        return parts.at[:, pl.ds(pl.multiple_of(owner * wide, LANES), wide)]

    line = LineSum(n, part, sum_ref, *line_scratch)
    for hop in range(n - 1):
        line.round(hop)
    line.finish()


def sum_proj(n, parts):
    depth, wide = parts.shape[0], parts.shape[1] // n
    return pl.pallas_call(
        functools.partial(proj_sum_kernel, n, wide),
        in_specs=[pl.BlockSpec(memory_space=pl.ANY)],
        out_specs=pl.BlockSpec(memory_space=pltpu.VMEM),
        out_shape=jax.ShapeDtypeStruct((depth, wide), SINGLE),
        scratch_shapes=LineSum.scratch(n, depth, wide),
        compiler_params=remote(10, 32),
        cost_estimate=cost(10**6, 20 * MEGA),
        name="sum_proj",
    )(parts)


def body(
    image_tokens,
    text_tokens,
    text_lengths,
    conditioning,
    ada_weight,
    ada_bias,
    qkv_weight,
    qv_bias,
    proj_weight,
    proj_bias,
    fc1_weight,
    fc1_bias,
    fc2_weight,
    fc2_bias,
    image_cotangent,
    text_cotangent,
):
    n = lax.axis_size("seq")
    dp = lax.axis_size("dp")
    img, width = image_tokens.shape[1:]
    slots = text_tokens.shape[1]
    pad = up(slots, 16)
    rows = img + pad
    depth = qkv_weight.shape[0]
    lw = qkv_weight.shape[3]
    lwp = up(lw, LANES)
    units = fc1_weight.shape[2]
    mod_cols = ada_weight.shape[2]
    my_seq = lax.axis_index("dp")

    def stacked(image, text):
        return jnp.concatenate([image, jnp.pad(text, ((0, pad - slots), (0, 0)))], axis=0)

    length = text_lengths[0, 0]
    live_text = (jnp.arange(slots, dtype=jnp.int32) < length)[:, None]
    x_loc = stacked(image_tokens[0], text_tokens[0])
    e_loc = stacked(
        image_cotangent[0], jnp.where(live_text, text_cotangent[0], jnp.zeros((), HALF))
    )

    def split(shard):
        return shard.reshape(2, -1, shard.shape[-1])

    qkv_local = jnp.pad(qkv_weight, ((0, 0), (0, 0), (0, 0), (0, lwp - lw))).reshape(depth, 6 * lwp)
    share = proj_weight.shape[0]
    proj_turned = proj_weight.transpose(2, 1, 0).reshape(depth, 2 * share)
    fc1_local = fc1_weight.reshape(depth, 2 * units)
    fc2_turned = fc2_weight.transpose(2, 1, 0).reshape(depth, 2 * units)

    cond_float = conditioning.astype(SINGLE)
    cond_act = jax.nn.silu(cond_float).astype(HALF)
    act_parts = jnp.pad(
        cond_act.astype(SINGLE).reshape(dp, 1, depth), ((0, 0), (0, 0), (0, up(depth, LANES) - depth))
    )
    ada_flat = ada_weight.reshape(depth, 2 * mod_cols)
    bias_cols = proj_bias.shape[1]
    cut = 2 * mod_cols
    side = jnp.concatenate(
        [
            ada_bias.astype(SINGLE).reshape(-1),
            proj_bias.astype(SINGLE).reshape(-1),
            fc2_bias.astype(SINGLE).reshape(-1),
            jnp.full((LANES,), length.astype(SINGLE)),
        ]
    )[None]
    x_all, side_all, acts, qkv_full, fc1_full = start(
        n, dp, x_loc, act_parts, ada_flat, side, split(qkv_local), split(fc1_local)
    )
    qkv_full = qkv_full.reshape(width, 6 * lwp)
    fc1_full = fc1_full.reshape(width, 2 * units)
    act_slice = acts[:, 0, :depth].astype(HALF)
    side_all = side_all[:, 0]

    def columns(begin, cols):
        return side_all[:, begin : begin + 2 * cols].reshape(n, 2, cols).transpose(1, 0, 2)

    mods = jnp.pad(columns(0, mod_cols).reshape(2, 6, width), ((0, 0), (0, 2), (0, 0)))
    proj_shift = columns(cut, bias_cols).reshape(2, width)
    fc2_shift = columns(cut + 2 * bias_cols, bias_cols).reshape(2, width)
    lengths_all = side_all[:, cut + 4 * bias_cols]

    slot = jnp.arange(rows, dtype=SINGLE)[None, :] - img
    live = jnp.logical_or(slot < 0, jnp.logical_and(slot < lengths_all[:, None], slot < slots))
    mask = jnp.where(live, SINGLE(0), SINGLE(MASKED))
    mask_row = mask.reshape(1, n * rows)
    mask_col = jnp.broadcast_to(mask[:, :, None], (n, rows, LANES))
    live_loc = jnp.concatenate(
        [jnp.ones((img, 1), SINGLE), jnp.pad(live_text.astype(SINGLE), ((0, pad - slots), (0, 0)))]
    )

    bias_rows = jnp.stack(
        [qv_bias[:, 0], jnp.zeros_like(qv_bias[:, 0]), qv_bias[:, 1]], axis=1
    ).astype(SINGLE)
    bias_rows = jnp.pad(bias_rows, ((0, 0), (0, 0), (0, lwp - lw))).reshape(2, 3 * lwp)
    attn_in, qkv_rows, proj_line = project_qkv(
        n, img, x_all, mods, qkv_full, bias_rows, proj_turned
    )
    mixture, lse, e_near, mix_loc, proj_full = attend(
        n, dp, qkv_rows, mask_row, e_loc, split(proj_line)
    )
    proj_full = proj_full.reshape(dp, n, depth, 2 * share)

    attn_out, middle, mlp_in, fc2_full = middle_rows(
        n, dp, img, mix_loc, x_loc, proj_full, proj_shift, mods, split(fc2_turned)
    )
    fc2_full = fc2_full.reshape(width, 2 * units)
    hidden, grad_pre, grad_mlp, mlp_in_part, mlp_out_part, fc1_bias_part, gate_two_part = (
        feed_forward(
            n, img, mlp_in, e_loc, e_near, mods, fc1_full, fc1_bias.astype(SINGLE), fc2_full
        )
    )
    tile = units // 4 if units % (4 * LANES) == 0 else units // 2
    tiles = units // tile
    fc_plan = [(w, w, t, k * tile) for w in range(2) for t in range(2) for k in range(tiles)]
    fc_rounds = [(k + 1) * 4 * tiles * 2 // (3 * (n - 2)) for k in range(n - 3)]
    fc_part, running = weight_grads(
        n, img, (mlp_in, grad_mlp), (grad_pre, hidden), fc_plan, tile, "fc_grads", fc_rounds, mlp_in_part, 6
    )
    fc_sum = lax.psum_scatter(fc_part, "dp", scatter_dimension=0, tiled=True)

    grad_middle, grad_attn, sums, grad_mix = middle_back(
        n, img, mlp_in_part, running, middle, attn_out, e_loc, proj_full, mods, lwp
    )
    grad_q, grad_k, grad_v, q_bias_part, v_bias_part, mlp_sum, proj_part = attend_back(
        n, img, qkv_rows, mixture, grad_mix, lse, mask_col, mlp_out_part, grad_attn, mix_loc
    )
    proj_part, fc_sum = lax.optimization_barrier((proj_part, fc_sum))
    proj_half = lax.psum_scatter(proj_part, "dp", scatter_dimension=0, tiled=True)
    attn_in_part, mod_one = attn_in_back(n, img, grad_q, grad_k, grad_v, x_all, qkv_full)
    qkv_plan = [(0, c, t, 0) for t in range(2) for c in range(3)]
    (qkv_part,) = weight_grads(
        n, img, (attn_in,), (grad_q, grad_k, grad_v), qkv_plan, lwp, "qkv_grad"
    )
    qkv_part, fc_sum = lax.optimization_barrier((qkv_part, fc_sum))
    qkv_sum = lax.psum_scatter(qkv_part, "dp", scatter_dimension=0, tiled=True)
    fc1_sum, fc2_sum = fc_sum[:, : 2 * units], fc_sum[:, 2 * units :]
    proj_own = sum_proj(n, proj_half)

    upstream_sum = sums[:, 4]
    gate_two = gate_two_part + fc2_shift * upstream_sum
    mod_grads = jnp.stack(
        [mod_one[:, 0], mod_one[:, 1], sums[:, 0], sums[:, 1], sums[:, 2], gate_two], axis=1
    ).reshape(2, n, mod_cols)
    rest = jnp.stack([sums[:, 3], mods[:, 5] * upstream_sum]).reshape(4, n, bias_cols)
    packed = jnp.concatenate(
        [
            mod_grads.transpose(1, 0, 2).reshape(n, -1),
            rest.transpose(1, 0, 2).reshape(n, -1),
        ],
        axis=1,
    )
    q_bias = q_bias_part.transpose(1, 0, 2).reshape(2, lwp)[:, :lw]
    v_bias = v_bias_part.transpose(1, 0, 2).reshape(2, lwp)[:, :lw]
    extra = jnp.concatenate(
        [jnp.stack([q_bias, v_bias], axis=1).reshape(-1), fc1_bias_part.reshape(-1)]
    )
    grad_attn_in, every, cond_sum = end(
        n, dp, cut, attn_in_part, packed[:, None], extra[None], ada_flat
    )
    every = every[:, 0]
    total = jnp.sum(every, axis=0)

    def by_row(vectors):
        return jnp.concatenate(
            [
                jnp.broadcast_to(vectors[0:1], (img, width)),
                jnp.broadcast_to(vectors[1:2], (pad, width)),
            ]
        )

    block_out = (
        (middle + by_row(mods[:, 5]) * (mlp_sum + by_row(fc2_shift))) * live_loc
    ).astype(HALF)
    normed, inv_std = layer_norm(x_loc.astype(SINGLE))
    input_grad = (
        grad_middle + norm_back(normed, inv_std, grad_attn_in * (1.0 + by_row(mods[:, 1])))
    ) * live_loc

    mod_half = every[:, :cut].astype(HALF).reshape(dp, 2, mod_cols)
    ada_grad = jnp.einsum("nd,ntc->dtc", act_slice, mod_half, preferred_element_type=SINGLE)
    ada_bias_grad = total[:cut].reshape(2, mod_cols)
    proj_bias_grad = total[cut : cut + 2 * bias_cols].reshape(2, bias_cols)
    fc2_bias_grad = total[cut + 2 * bias_cols : cut + 4 * bias_cols].reshape(2, bias_cols)
    after = cut + 4 * bias_cols
    qv_bias_grad = total[after : after + 4 * lw].reshape(2, 2, lw)
    fc1_bias_grad = total[after + 4 * lw :].reshape(2, units)
    cond_grad = cond_sum[:, 0, :depth].reshape(1, width) * silu_slope(cond_float)

    def streams(flat, last):
        return flat.astype(SINGLE).reshape(depth, 2, last)

    qkv_grad = qkv_sum.astype(SINGLE).reshape(depth, 2, 3, lwp)[..., :lw]
    fc2_grad = streams(fc2_sum, units).transpose(2, 1, 0)
    proj_grad = proj_own.reshape(depth, 2, lwp)[..., :share].transpose(2, 1, 0)
    return (
        block_out[None, :img],
        block_out[None, img : img + slots],
        input_grad[None, :img],
        input_grad[None, img : img + slots],
        cond_grad,
        ada_grad,
        ada_bias_grad,
        qkv_grad,
        qv_bias_grad,
        proj_grad,
        proj_bias_grad,
        streams(fc1_sum, units),
        fc1_bias_grad,
        fc2_grad,
        fc2_bias_grad,
    )


def solution(mesh):
    in_specs = (
        P("dp", "seq", None),
        P("dp", "seq", None),
        P("dp", "seq"),
        P("dp", None),
        P("dp", None, "seq"),
        P(None, "seq"),
        P("dp", None, None, "seq"),
        P(None, None, "seq"),
        P("seq", None, "dp"),
        P(None, "seq"),
        P("dp", None, "seq"),
        P(None, "seq"),
        P("seq", None, "dp"),
        P(None, "seq"),
        P("dp", "seq", None),
        P("dp", "seq", None),
    )
    out_specs = (
        P("dp", "seq", None),
        P("dp", "seq", None),
        P("dp", "seq", None),
        P("dp", "seq", None),
        P("dp", None),
        P("dp", None, "seq"),
        P(None, "seq"),
        P("dp", None, None, "seq"),
        P(None, None, "seq"),
        P("seq", None, "dp"),
        P(None, "seq"),
        P("dp", None, "seq"),
        P(None, "seq"),
        P("seq", None, "dp"),
        P(None, "seq"),
    )
    return jax.shard_map(body, mesh=mesh, in_specs=in_specs, out_specs=out_specs, check_vma=False)
```

time: 908 us -> 752 us (0.83); the launches traced: 897 us -> 750 us
  Pallas kernels: 237 us -> 670 us
  waiting for transfers between devices: 307 us -> 4.08 us
  starting transfers between devices: 122 us -> 0.12 us
  blocking collectives: 60.2 us -> 0 us
  local copies, waits for them, and re-layouts: 106 us -> 47.9 us
  other arithmetic: 41.2 us -> 11.8 us
    pallas_call x11, Pallas kernels: 222 us -> 655 us  [the longest x1 103 us: start(): pl.pallas_call(functools.partial(start_kernel, n, dp), in_specs=[anywhere...]
    ppermute x42 -> x0, waiting for transfers between devices: 232 us -> none  [the longest x18 131 us: line_sum(): carry = lax.ppermute(value.astype(HALF), 'seq', pattern)]
    ppermute x42 -> x0, starting transfers between devices: 122 us -> none  [the longest x18 56.2 us: line_sum(): carry = lax.ppermute(value.astype(HALF), 'seq', pattern)]
    all_gather x4 -> x0, blocking collectives: 41.7 us -> none  [the longest x1 13.3 us: body(): side_all = lax.all_gather(side, 'seq', axis=0, tiled=False)]
    reduce_scatter x3 -> x1, waiting for transfers between devices: 32.4 us -> 0.01 us  [body(): fc_sum = lax.psum_scatter(fc_part, 'dp', scatter_dimension=0, tiled=True)]
    dynamic_update_slice x27 -> x0, local copies, waits for them, and re-layouts: 28.9 us -> none  [the longest x9 14.5 us: line_gather(): lax.dynamic_update_index_in_dim(held, from_left, jnp.where(me >= k, me -...]
    unnamed x14 -> x3, waiting for transfers between devices: 26.9 us -> 0.71 us
    convert_element_type x10 -> x1, other arithmetic: 22.6 us -> 0.04 us  [body(): cond_act = jax.nn.silu(cond_float).astype(HALF)]
  transfers between devices with their start and end apart: 54 -> 3, of which waited for: 26 -> 1; matrix products, arithmetic and copies ran while one was open for 15% -> 4% of each run, Pallas kernels for 20% -> 34%
where the time goes in v2:
time: 752 us; the launch traced here: 750 us
  Pallas kernels  670 us (89%)
  local copies, waits for them, and re-layouts  47.9 us (6%)
  between operations  15.3 us (2%)
  other arithmetic  11.8 us (2%)
    pallas_call x1, Pallas kernels, start(): pl.pallas_call(functools.partial(start_kernel, n, dp), in_specs=[anywhere...  103 us
    pallas_call x1, Pallas kernels, end(): pl.pallas_call(functools.partial(end_kernel, n, dp, cut), in_specs=[pl.Bl...  94.4 us
    pallas_call x1, Pallas kernels, middle_rows(): pl.pallas_call(functools.partial(middle_kernel, n, img), in_specs=[inner]...  82.6 us
    pallas_call x1, Pallas kernels, attend_back(): pl.pallas_call(functools.partial(attn_back_kernel, n, img, pairs), grid=(...  77.3 us
    pallas_call x2, Pallas kernels, weight_grads(): pl.pallas_call(functools.partial(grads_kernel, n, img, plan, rounds), gri...  74.6 us
    pallas_call x1, Pallas kernels, feed_forward(): pl.pallas_call(functools.partial(mlp_kernel, n, img, tile), grid=(n,), in...  65.4 us
    pallas_call x1, Pallas kernels, middle_back(): pl.pallas_call(functools.partial(middle_back_kernel, n, img), in_specs=[a...  54.8 us
    pallas_call x1, Pallas kernels, attend(): pl.pallas_call(functools.partial(attn_kernel, n), grid=(pairs, n), in_spe...  50.2 us
  transfers between devices with their start and end apart: 3, of which 1 were waited for; matrix products, arithmetic and copies ran while one was open for 4% of the time, Pallas kernels for 34%

profile of v2, /device:TPU:0, one launch (start us, length us, event | category | flops | bytes accessed | tf_op | source)
XLA Modules:
  0.0 750.1 jit_solution(10859286467323677716)
XLA Ops:
  10.7 2.9 copy.80
  14.9 2.0 reshape_reshape.9.qkv_ref
  16.9 1.7 reshape_reshape.10.fc1_ref
  18.6 1.1 convert_reduce_fusion
  19.7 103.2 %start.1 = (bf16[4,336,1536]{2,1,0:T(8,128)(2,1)}, f32[4,1,6272]{2,1,0:T(1,128)}, f32[8,1,256]{2,1,0:T(1,128)}, bf16[8,2,96,2304]{3,2,1,0:T(8,128)(2,1)}, bf16[8,2,96,3072]{3,2,1,0:T(8,128)(2,1)}) custom-call(bf16[336,1536]{1,0:T(8,128)(2,1)} %get-tuple-element.159.x_ref, f32[8,1,256]{2,1,0:T(1,128)} %pad_convert_fusion.act_ref, bf16[192,4608]{1,0:T(8,128)(2,1)} %bitcast.97, ...), custom_call_target="tpu_custom_call" | custom-call | flops 1000000 | bytes 104857600 | tf_op jit(solution)/shard_map/start/pallas_call | solution.py:501
  127.0 1.2 copy.63
  128.2 1.7 reshape_reshape.11.fc2_ref
  131.3 1.0 fusion.17.e_ref.e_loc
  132.3 29.1 %project_qkv.1 = (bf16[4,336,1536]{2,1,0:T(8,128)(2,1)}, bf16[4,336,1152]{2,1,0:T(8,128)(2,1)}, bf16[4,192,768]{2,1,0:T(8,128)(2,1)}) custom-call(bf16[4,336,1536]{2,1,0:T(8,128)(2,1)} %get-tuple-element.61.x_ref, f32[2,8,1536]{2,1,0:T(8,128)} %pad.27.mod_ref, bf16[1536,2304]{1,0:T(8,128)(2,1)} %bitcast.127, f32[2,1152]{1,0:T(2,128)} %bitcast.122, ...), custom_call_target="tpu_custom_call" | custom-call | flops 4756340736 | bytes 31457280 | tf_op jit(solution)/shard_map/project_qkv/pallas_call | solution.py:564
  161.4 50.2 %attend.1 = (bf16[4,336,384]{2,1,0:T(8,128)(2,1)}, f32[4,336,384]{2,1,0:T(8,128)}, bf16[2,336,1536]{2,1,0:T(8,128)(2,1)}, bf16[336,1536]{1,0:T(8,128)(2,1)}, bf16[8,2,384,768]{3,2,1,0:T(8,128)(2,1)}) custom-call(bf16[4,336,1152]{2,1,0:T(8,128)(2,1)} %get-tuple-element.64.q_ref.k_ref.v_ref, bf16[4,336,1152]{2,1,0:T(8,128)(2,1)} %get-tuple-element.64.q_ref.k_ref.v_ref, ...), custom_call_target="tpu_custom_call" | custom-call | flops 11098128384 | bytes 20971520 | tf_op jit(solution)/shard_map/attend/pallas_call | solution.py:678
  211.5 82.6 %middle_rows.1 = (f32[336,1536]{1,0:T(8,128)}, f32[336,1536]{1,0:T(8,128)}, bf16[4,336,1536]{2,1,0:T(8,128)(2,1)}, bf16[8,2,96,3072]{3,2,1,0:T(8,128)(2,1)}) custom-call(bf16[336,1536]{1,0:T(8,128)(2,1)} %get-tuple-element.66.mix_ref.r_ref, bf16[336,1536]{1,0:T(8,128)(2,1)} %get-tuple-element.159.x_ref, bf16[8,4,192,768]{3,2,1,0:T(8,128)(2,1)} %bitcast.95, ...), custom_call_target="tpu_custom_call" | custom-call | flops 1585446912 | bytes 104857600 | tf_op jit(solution)/shard_map/middle_rows/pallas_call | solution.py:896
  294.2 65.4 %feed_forward.1 = (bf16[4,336,1536]{2,1,0:T(8,128)(2,1)}, bf16[4,336,1536]{2,1,0:T(8,128)(2,1)}, bf16[4,336,1536]{2,1,0:T(8,128)(2,1)}, bf16[4,336,1536]{2,1,0:T...) custom-call(bf16[4,336,1536]{2,1,0:T(8,128)(2,1)} %get-tuple-element.70.b_ref.refs_0_, ...), custom_call_target="tpu_custom_call" | custom-call | flops 19025362944 | bytes 52428800 | tf_op jit(solution)/shard_map/feed_forward/pallas_call | solution.py:1004
  359.6 61.7 %fc_grads.1 = (bf16[1536,6144]{1,0:T(8,128)(2,1)}, bf16[2,336,1536]{2,1,0:T(8,128)(2,1)}) custom-call(bf16[4,336,1536]{2,1,0:T(8,128)(2,1)} %get-tuple-element.70.b_ref.refs_0_, bf16[4,336,1536]{2,1,0:T(8,128)(2,1)} %get-tuple-element.75.refs_1_, bf16[4,336,1536]{2,1,0:T(8,128)(2,1)} %get-tuple-element.76.refs_2_, ...), custom_call_target="tpu_custom_call" | custom-call | flops 12683575296 | bytes 62914560 | tf_op jit(solution)/shard_map/fc_grads/pallas_call | solution.py:1101
  421.4 54.8 %middle_back.1 = (f32[336,1536]{1,0:T(8,128)}, bf16[336,1536]{1,0:T(8,128)(2,1)}, f32[2,8,1536]{2,1,0:T(8,128)}, bf16[4,336,384]{2,1,0:T(8,128)(2,1)}) custom-call(bf16[4,336,1536]{2,1,0:T(8,128)(2,1)} %get-tuple-element.74.refs_4_.part_ref, bf16[2,336,1536]{2,1,0:T(8,128)(2,1)} %get-tuple-element.78.prev_ref, f32[336,1536]{1,0:T(8,128)} %get-tuple-element.68.m_ref, ...), custom_call_target="tpu_custom_call" | custom-call | flops 1585446912 | bytes 62914560 | tf_op jit(solution)/shard_map/middle_back/pallas_call | solution.py:1182
  476.2 1.1 broadcast_in_dim.109.mask_ref
  477.3 77.3 %attend_back.1 = (bf16[4,336,384]{2,1,0:T(8,128)(2,1)}, bf16[4,336,384]{2,1,0:T(8,128)(2,1)}, bf16[4,336,384]{2,1,0:T(8,128)(2,1)}, f32[3,2,128]{2,1,0:T(2,128)}...) custom-call(bf16[4,336,1152]{2,1,0:T(8,128)(2,1)} %get-tuple-element.64.q_ref.k_ref.v_ref, ...), custom_call_target="tpu_custom_call" | custom-call | flops 27745320960 | bytes 31457280 | tf_op jit(solution)/shard_map/attend_back/pallas_call | solution.py:813
  554.6 12.9 %qkv_grad.1 = bf16[1536,2304]{1,0:T(8,128)(2,1)} custom-call(bf16[4,336,1536]{2,1,0:T(8,128)(2,1)} %get-tuple-element.100.refs_0_, bf16[4,336,384]{2,1,0:T(8,128)(2,1)} %get-tuple-element.86.dq_ref.refs_1_, bf16[4,336,384]{2,1,0:T(8,128)(2,1)} %get-tuple-element.87.dk_ref.refs_2_, bf16[4,336,384]{2,1,0:T(8,128)(2,1)} %get-tuple-element.88.dv_ref.refs_3_), custom_call_target="tpu_custom_call" | custom-call | flops 4756340736 | bytes 62914560 | tf_op jit(solution)/shard_map/qkv_grad/pallas_call | solution.py:1101
  569.2 15.5 %attn_in_back.1 = (bf16[4,336,1536]{2,1,0:T(8,128)(2,1)}, f32[2,2,1536]{2,1,0:T(2,128)}) custom-call(bf16[4,336,384]{2,1,0:T(8,128)(2,1)} %get-tuple-element.86.dq_ref.refs_1_, bf16[4,336,384]{2,1,0:T(8,128)(2,1)} %get-tuple-element.87.dk_ref.refs_2_, bf16[4,336,384]{2,1,0:T(8,128)(2,1)} %get-tuple-element.88.dv_ref.refs_3_, ...), custom_call_target="tpu_custom_call" | custom-call | flops 4756340736 | bytes 31457280 | tf_op jit(solution)/shard_map/attn_in_back/pallas_call | solution.py:1228
  586.4 94.4 %end.1 = (f32[336,1536]{1,0:T(8,128)}, f32[8,1,10752]{2,1,0:T(1,128)}, f32[8,1,256]{2,1,0:T(1,128)}) custom-call(bf16[4,336,1536]{2,1,0:T(8,128)(2,1)} %get-tuple-element.89.parts, f32[4,1,6144]{2,1,0:T(1,128)} %broadcast_in_dim.116.packed, f32[1,4608]{1,0:T(1,128)} %broadcast_in_dim.117.extra, bf16[192,4608]{1,0:T(8,128)(2,1)} %bitcast.98), custom_call_target="tpu_custom_call" | custom-call | flops 1000000 | bytes 104857600 | tf_op jit(solution)/shard_map/end/pallas_call | solution.py:1299
  680.8 1.6 fusion.29
  683.2 4.5 copy.71
  692.4 3.5 fusion.8
  695.9 1.3 copy-done.4
  697.3 1.3 copy.70
  703.9 1.3 slice_bitcast_fusion
  705.5 1.6 copy.93
  707.1 3.0 reshape.405
  710.1 2.6 reshape.403
  712.7 2.1 copy.72
  714.8 3.4 reduce-scatter.8.cloned.1.call-done.parts
  718.2 1.3 copy-done
  719.5 23.1 %sum_proj.1 = f32[192,768]{1,0:T(8,128)S(1)} custom-call(bf16[192,3072]{1,0:T(8,128)(2,1)S(1)} %copy-done), custom_call_target="tpu_custom_call" | custom-call | flops 1000000 | bytes 20971520 | tf_op jit(solution)/shard_map/sum_proj/pallas_call | solution.py:1337
  (148 shorter events, 24.7 us)
Async XLA Ops:
  7.2 6.4 copy-start.19
  7.2 7.1 copy-start.12
  7.2 560.3 %reduce-scatter.4.cloned.1.call-start = ((), (), s32[]{:S(2)}) async-start(), calls=%async_computation.3 | async-start | bytes 21233664 | tf_op jit(solution)/shard_map/reduce_scatter | solution.py:1468
  14.3 2.6 copy-start.10
  14.9 3.7 copy-start.13
  14.9 3.6 copy-start.17
  19.7 104.4 %copy-start.21 = (bf16[2,2,384]{2,1,0:T(2,128)(2,1)S(1)}, bf16[2,2,384]{2,1,0:T(2,128)(2,1)}, u32[]{:S(2)}) copy-start(bf16[2,2,384]{2,1,0:T(2,128)(2,1)} %param.23) | copy-start | bytes 9220
  19.7 105.2 %copy-start.15 = (bf16[384,2,192]{0,2,1:T(8,128)(2,1)S(1)}, bf16[384,2,192]{0,2,1:T(8,128)(2,1)}, u32[]{:S(2)}) copy-start(bf16[384,2,192]{0,2,1:T(8,128)(2,1)} %param.24) | copy-start | bytes 884740
  19.7 107.3 %copy-start.11 = (bf16[1536,2,192]{0,2,1:T(8,128)(2,1)S(1)}, bf16[1536,2,192]{0,2,1:T(8,128)(2,1)}, u32[]{:S(2)}) copy-start(bf16[1536,2,192]{0,2,1:T(8,128)(2,1)} %param.28) | copy-start | bytes 3538948
  127.0 2.9 copy-start.25
  127.0 4.2 copy-start.16
  128.2 3.1 copy-start.14
  421.3 288.8 %reduce-scatter.6.cloned.1.call-start = ((), (), s32[]{:S(2)}) async-start(), calls=%async_computation.4 | async-start | bytes 7962624 | tf_op jit(solution)/shard_map/reduce_scatter | solution.py:1484
  567.5 0.8 copy-start.26
  567.5 0.8 copy-start.27
  567.6 0.8 copy-start.20
  567.6 1.5 copy-start.18
  567.6 1.5 copy-start.22
  567.6 150.6 %reduce-scatter.8.cloned.1.call-start = ((), (), s32[]{:S(2)}) async-start(), calls=%async_computation.5 | async-start | bytes 10616832 | tf_op jit(solution)/shard_map/reduce_scatter | solution.py:1477
  586.4 96.1 %copy-start.23 = (f32[8,1,256]{2,1,0:T(1,128)S(1)}, f32[8,1,256]{2,1,0:T(1,128)}, u32[]{:S(2)}) copy-start(f32[8,1,256]{2,1,0:T(1,128)} %get-tuple-element.98) | copy-start | bytes 24580
  683.1 4.7 copy-start.1
  687.7 1.6 copy-start.3
  689.3 1.6 copy-start.9
  690.0 1.8 copy-start.2
  690.1 2.4 copy-start.8
  695.9 1.3 copy-start.4
  695.9 5.6 copy-start.24
  695.9 6.3 copy-start.6
  697.3 6.6 copy-start.5
  703.0 2.2 copy-start.7
  718.2 1.3 copy-start
Sparse Core Ops, SparseCore 0:
  421.4 131.0 reduce-scatter.3
  567.7 70.1 reduce-scatter.5
  641.8 76.3 reduce-scatter.7

commit v3 on v2

--- a/solution.py
+++ b/solution.py
@@ -190,8 +190,9 @@
         )
 
     def begin(self):
-        for half in range(2):
-            self.copy(half, 0, 0, self.my).start()
+        for phase in range(self.phases):
+            for half in range(2):
+                self.copy(half, phase, 0, self.my).start()
         for half in range(2):
             self.hand(half, 0, self.my, True).start()
         pltpu.make_async_copy(self.src, self.out.at[self.my], self.local).start()
@@ -203,7 +204,7 @@
                 block = flip(self.my, mask ^ self.span(half, count))
                 self.copy(half, phase, count, block).wait_recv()
             if phase + 1 < self.phases:
-                for count in range(2 ** (phase + 1)):
+                for count in range(1, 2 ** (phase + 1)):
                     block = flip(self.my, self.span(half, count))
                     self.copy(half, phase + 1, count, block).start()
             for count in range(2**phase):
@@ -221,6 +222,157 @@
                     self.copy(half, phase, count, self.my).wait_send()
                     block = flip(other, mask ^ self.span(half, count))
                     self.hand(half, 2**phase + count, block).wait()
+
+
+class GroupSum:
+    def __init__(self, part, got, hold, passed, came, pass_send, pass_recv, send, recv, load):
+        self.part, self.got, self.hold, self.passed, self.came = part, got, hold, passed, came
+        self.pass_send, self.pass_recv = pass_send, pass_recv
+        self.send, self.recv, self.load = send, recv, load
+        self.my = lax.axis_index("dp")
+        self.dp = part.shape[0]
+        masks = masks_of(self.dp)
+        self.orders = (masks, masks[::-1])
+        self.phases = len(masks)
+
+    @staticmethod
+    def scratch(dp, rows, width):
+        half = dp // 2
+        return [
+            pltpu.VMEM((2, half, rows, width), HALF),
+            pltpu.VMEM((2, half, rows, width), HALF),
+            pltpu.VMEM((2, half - 1, rows, width), HALF),
+            pltpu.VMEM((2, half - 1, rows, width), HALF),
+        ] + [pltpu.SemaphoreType.DMA((2, half)) for _ in range(5)]
+
+    @staticmethod
+    def scratch_inner(dp, rows, width):
+        full = GroupSum.scratch(dp, rows, width)
+        return full[:1] + full[2:8]
+
+    def span(self, half, count):
+        mask = 0
+        for k in range(self.phases):
+            if count >> k & 1:
+                mask |= self.orders[half][k]
+        return mask
+
+    def hand(self, half, count):
+        block = flip(self.my, 1 ^ self.span(half, count))
+        return pltpu.make_async_remote_copy(
+            src_ref=self.part.at[block, half],
+            dst_ref=self.got.at[half, count],
+            send_sem=self.pass_send.at[half, count],
+            recv_sem=self.pass_recv.at[half, count],
+            device_id={"dp": flip(self.my, 1)},
+            device_id_type=MESH,
+        )
+
+    def fetch(self, half, count):
+        block = flip(self.my, self.span(half, count))
+        return pltpu.make_async_copy(
+            self.part.at[block, half], self.hold.at[half, count], self.load.at[half, count]
+        )
+
+    def copy(self, half, phase, index):
+        return pltpu.make_async_remote_copy(
+            src_ref=self.passed.at[half, 2**phase + index - 1],
+            dst_ref=self.came.at[half, 2**phase - 1 + index],
+            send_sem=self.send.at[half, 2**phase - 1 + index],
+            recv_sem=self.recv.at[half, 2**phase - 1 + index],
+            device_id={"dp": flip(self.my, self.orders[half][phase])},
+            device_id_type=MESH,
+        )
+
+    def every(self):
+        return [(half, count) for half in range(2) for count in range(self.dp // 2)]
+
+    def begin(self):
+        for half, count in self.every():
+            self.hand(half, count).start()
+            if self.hold is not None:
+                self.fetch(half, count).start()
+
+    def value(self, half, count, phase):
+        if self.hold is None:
+            mine = self.part[flip(self.my, self.span(half, count)), half]
+        else:
+            mine = self.hold[half, count]
+        total = mine.astype(SINGLE) + self.got[half, count].astype(SINGLE)
+        for later in range(phase, self.phases):
+            total = total + self.came[half, 2**later - 1 + count].astype(SINGLE)
+        return total
+
+    def step(self, number):
+        if number == 0:
+            for half, count in self.every():
+                if self.hold is not None:
+                    self.fetch(half, count).wait()
+                self.hand(half, count).wait_recv()
+        else:
+            self.took(self.phases - number)
+        phase = self.phases - 1 - number
+        for half in range(2):
+            for index in range(2**phase):
+                count = 2**phase + index
+                self.passed[half, count - 1] = self.value(half, count, phase + 1).astype(HALF)
+                self.copy(half, phase, index).start()
+
+    def took(self, phase):
+        for half in range(2):
+            for index in range(2**phase):
+                self.copy(half, phase, index).wait_recv()
+
+    def finish(self, out):
+        self.took(0)
+        for half in range(2):
+            out[half] = self.value(half, 0, 0).astype(out.dtype)
+        self.sent(0)
+
+    def close(self, rest):
+        self.took(1)
+        for half in range(2):
+            for count in range(2):
+                rest[half, count] = self.value(half, count, 1).astype(rest.dtype)
+        self.sent(1)
+
+    def sent(self, first):
+        for half, count in self.every():
+            self.hand(half, count).wait_send()
+        for phase in range(first, self.phases):
+            for half in range(2):
+                for index in range(2**phase):
+                    self.copy(half, phase, index).wait_send()
+
+
+class GroupLast:
+    def __init__(self, rest, came, send, recv):
+        self.rest, self.came, self.send, self.recv = rest, came, send, recv
+        masks = masks_of(lax.axis_size("dp"))
+        self.partners = [flip(lax.axis_index("dp"), mask) for mask in (masks[0], masks[-1])]
+
+    @staticmethod
+    def scratch(rows, width):
+        return [pltpu.VMEM((2, rows, width), HALF)] + [pltpu.SemaphoreType.DMA((2,))] * 2
+
+    def copy(self, half):
+        return pltpu.make_async_remote_copy(
+            src_ref=self.rest.at[half, 1],
+            dst_ref=self.came.at[half],
+            send_sem=self.send.at[half],
+            recv_sem=self.recv.at[half],
+            device_id={"dp": self.partners[half]},
+            device_id_type=MESH,
+        )
+
+    def begin(self):
+        for half in range(2):
+            self.copy(half).start()
+
+    def finish(self, store):
+        for half in range(2):
+            self.copy(half).wait()
+            store(half, self.rest[half, 0].astype(SINGLE) + self.came[half].astype(SINGLE))
 
 
 class LineGather:
@@ -466,11 +618,11 @@
     part_go = [to_group(my, dp, k, part, parts, p_send, p_recv) for k in others]
     for copy in part_go:
         copy.start()
-    qkv.begin()
-    fc1.begin()
     parts[my] = part[my]
     for copy in part_go:
         copy.wait_recv()
+    qkv.begin()
+    fc1.begin()
     row[...] = side_ref[...]
     row[:, :cols] += jnp.sum(parts[...], axis=0)
     row_go = [to_line(me, n, k, row, side_all, s_send, s_recv) for k in range(1, n)]
@@ -500,7 +652,7 @@
     inner = pl.BlockSpec(memory_space=pltpu.VMEM)
     return pl.pallas_call(
         functools.partial(start_kernel, n, dp),
-        in_specs=[anywhere, inner, inner, inner, anywhere, anywhere],
+        in_specs=[inner] * 6,
         out_specs=[anywhere, inner, inner, anywhere, anywhere],
         out_shape=[
             jax.ShapeDtypeStruct((n, rows, width), HALF),
@@ -529,17 +681,8 @@
     )(x_loc, act_parts, ada, side, qkv, fc1)
 
 
-def qkv_kernel(n, img, x_ref, mod_ref, w_ref, b_ref, p_ref, a_ref, o_ref, p_line, *sems):
-    step = pl.program_id(0)
+def qkv_kernel(img, x_ref, mod_ref, w_ref, b_ref, a_ref, o_ref):
     wide = o_ref.shape[2]
-    gather = LineGather(n, p_ref, p_line, *sems)
-
-    def begin():
-        greet(n, "near")
-        gather.begin()
-        gather.keep().start()
-
-    at_step(step, 0, begin)
     for t, sl in ((0, slice(0, img)), (1, slice(img, x_ref.shape[1]))):
         normed, _ = layer_norm(x_ref[0, sl].astype(SINGLE))
         a = (normed * (1.0 + mod_ref[t, 1:2]) + mod_ref[t, 0:1]).astype(HALF)
@@ -547,41 +690,29 @@
         o_ref[0, sl] = (
             nn_dot(a, w_ref[:, t * wide : (t + 1) * wide]) + b_ref[t : t + 1]
         ).astype(HALF)
-    for hop in range(n - 1):
-        at_step(step, min(n - 1, 2 * hop + 1), functools.partial(gather.arrive, hop))
-
-    def finish():
-        gather.keep().wait()
-        gather.finish()
-
-    at_step(step, n - 1, finish)
-
-
-def project_qkv(n, img, x_all, mods, weight, bias, proj):
+
+
+def project_qkv(n, img, x_all, mods, weight, bias):
     _, rows, width = x_all.shape
     wide = weight.shape[1] // 2
-    anywhere = pl.BlockSpec(memory_space=pl.ANY)
     return pl.pallas_call(
-        functools.partial(qkv_kernel, n, img),
+        functools.partial(qkv_kernel, img),
         grid=(n,),
         in_specs=[
             rows_spec(rows, width),
             whole(mods.shape),
             whole(weight.shape, True),
             whole(bias.shape),
-            anywhere,
         ],
-        out_specs=[rows_spec(rows, width), rows_spec(rows, wide), anywhere],
+        out_specs=[rows_spec(rows, width), rows_spec(rows, wide)],
         out_shape=[
             jax.ShapeDtypeStruct((n, rows, width), HALF),
             jax.ShapeDtypeStruct((n, rows, wide), HALF),
-            jax.ShapeDtypeStruct((n,) + proj.shape, HALF),
         ],
-        scratch_shapes=LineGather.scratch(n),
-        compiler_params=remote(8),
+        compiler_params=params(),
         cost_estimate=cost(2 * n * rows * width * wide, 30 * MEGA),
         name="project_qkv",
-    )(x_all, mods, weight, bias, proj)
+    )(x_all, mods, weight, bias)
 
 
 def halves(shape):
@@ -684,7 +815,7 @@
             pl.BlockSpec((n, rows, LANES), lambda h, s: (0, 0, 2 * pairs + h)),
             whole(mask.shape),
             anywhere,
-            anywhere,
+            whole(proj.shape, True),
         ],
         out_specs=[block, block, anywhere, anywhere, anywhere],
         out_shape=[
@@ -710,23 +841,40 @@
 
 def attn_back_kernel(
     lines, img, pairs, q_ref, k_ref, v_ref, o_ref, g_ref, lse_ref, mask_ref, y_ref, l_ref, r_ref,
-    dq_ref, dk_ref, dv_ref, qb_ref, vb_ref, sum_ref, p_ref,
-    acc_ref, lse_row, delta_row, turned, *line_scratch,
+    dq_ref, dk_ref, dv_ref, qb_ref, vb_ref, p_rest, tail,
+    acc_ref, lse_row, delta_row, turned, p_part, *scratch,
 ):
     linear = pl.program_id(0)
+    ahead = 2 * lines
     attn_steps = pairs * lines
-    step = lax.rem(linear, lines)
+    last = ahead + attn_steps - 1
+    step = lax.rem(lax.max(linear - ahead, 0), lines)
     n, rows, _ = q_ref.shape
     total = n * rows
-    line = LineSum(lines, at_rows(y_ref), sum_ref, *line_scratch)
+    line = LineSum(lines, at_rows(y_ref), None, *scratch[:6], stop=lines - 2, tail=tail)
+    group = GroupSum(p_part, scratch[6], None, *scratch[7:], None)
 
     def begin():
-        greet(lines, "near")
+        greet(lines, "near", "paths")
         line.round(0)
 
     at_step(linear, 0, begin)
-
-    @pl.when(linear < attn_steps)
+    tile = r_ref.shape[1]
+    for t, sl in ((0, slice(0, img)), (1, slice(img, rows))):
+
+        @pl.when(linear == 0)
+        def _():
+            turned[:, sl] = l_ref[sl].T
+
+        @pl.when(both(linear < ahead, lax.rem(linear, 2) == t))
+        def _():
+            column = pl.ds(pl.multiple_of(linear * tile, LANES), tile)
+            product = nn_dot(turned[:, sl], r_ref[sl]).astype(HALF)
+            p_part[:, :, :, column] = product.reshape(p_part.shape[:3] + (tile,))
+
+    at_step(linear, ahead, group.begin)
+
+    @pl.when(linear >= ahead)
     def _():
         grads = g_ref[...].reshape(total, LANES)
         queries = q_ref[...].reshape(total, LANES) * HALF(1.0 / math.sqrt(HD))
@@ -771,37 +919,34 @@
             qb_ref[0, 0:1] = jnp.sum(jnp.sum(dq[:, :img], axis=0), axis=0, keepdims=True)
             qb_ref[0, 1:2] = jnp.sum(jnp.sum(dq[:, img:], axis=0), axis=0, keepdims=True)
 
-    for t, sl in ((0, slice(0, img)), (1, slice(img, rows))):
-
-        @pl.when(linear == attn_steps)
-        def _():
-            turned[:, sl] = l_ref[sl].T
-
-        @pl.when(both(linear >= attn_steps, lax.rem(linear - attn_steps, 2) == t))
-        def _():
-            p_ref[...] = nn_dot(turned[:, sl], r_ref[sl]).astype(HALF)
-
-    for hop in range(1, lines - 1):
-        at_step(linear, 6 * hop, functools.partial(line.round, hop))
-    at_step(linear, attn_steps + 2 * lines - 1, line.finish)
-
-
-def attend_back(n, img, qkv, mixture, grad_mix, lse, mask_col, out_parts, grad_attn, mix_loc):
+    for hop in range(1, lines - 2):
+        at_step(linear, min(last, ahead + 5 * hop), functools.partial(line.round, hop))
+
+    for number in range(group.phases - 1):
+        at_step(linear, min(last, ahead + 2 + 4 * number), functools.partial(group.step, number))
+
+    def finish():
+        line.close()
+        group.close(p_rest)
+
+    at_step(linear, last, finish)
+
+
+def attend_back(n, dp, img, qkv, mixture, grad_mix, lse, mask_col, out_parts, grad_attn, mix_loc):
     _, rows, wide = qkv.shape
     pairs = wide // 3 // LANES
     total = n * rows
     lw = pairs * LANES
+    ahead = 2 * n
     steps = pairs * n
     width = out_parts.shape[2]
+    depth = width // dp // 2
+
+    def place(k):
+        return lax.rem(lax.max(k - ahead, 0), n)
 
     def head(k):
-        return lax.min(lax.div(k, n), pairs - 1)
-
-    def place(k):
-        return lax.select(k < steps, lax.rem(k, n), n - 1)
-
-    def later(k):
-        return lax.max(k - steps, 0)
+        return lax.div(lax.max(k - ahead, 0), n)
 
     full = pl.BlockSpec((n, rows, LANES), lambda k: (0, 0, head(k)))
 
@@ -812,7 +957,7 @@
     anywhere = pl.BlockSpec(memory_space=pl.ANY)
     return pl.pallas_call(
         functools.partial(attn_back_kernel, n, img, pairs),
-        grid=(steps + 2 * n,),
+        grid=(ahead + steps,),
         in_specs=[
             full,
             block(pairs),
@@ -823,7 +968,7 @@
             pl.BlockSpec((1, rows, LANES), lambda k: (place(k), 0, 0)),
             anywhere,
             whole(grad_attn.shape, True),
-            pl.BlockSpec((rows, lw), lambda k: (0, lax.div(later(k), 2))),
+            pl.BlockSpec((rows, lw), lambda k: (0, lax.min(lax.div(k, 2), n - 1))),
         ],
         out_specs=[
             full,
@@ -831,23 +976,25 @@
             block(0),
             bias,
             bias,
-            whole(out_parts.shape[1:], True),
-            pl.BlockSpec((width, lw), lambda k: (0, later(k))),
+            whole((2, 2, depth, 2 * n * lw), True),
+            anywhere,
         ],
         out_shape=[jax.ShapeDtypeStruct((n, rows, lw), HALF)] * 3
         + [jax.ShapeDtypeStruct((pairs, 2, LANES), SINGLE)] * 2
         + [
-            jax.ShapeDtypeStruct(out_parts.shape[1:], SINGLE),
-            jax.ShapeDtypeStruct((width, 2 * n * lw), HALF),
+            jax.ShapeDtypeStruct((2, 2, depth, 2 * n * lw), HALF),
+            jax.ShapeDtypeStruct((2, rows, width), HALF),
         ],
         scratch_shapes=[
             pltpu.VMEM((total, LANES), SINGLE),
             pltpu.VMEM((2, total), SINGLE),
             pltpu.VMEM((2, total), SINGLE),
             pltpu.VMEM((width, rows), HALF),
+            pltpu.VMEM((dp, 2, depth, 2 * n * lw), HALF),
         ]
-        + LineSum.scratch(n, rows, width),
-        compiler_params=remote(3, 60),
+        + LineSum.scratch(n, rows, width, stop=n - 2)
+        + GroupSum.scratch_inner(dp, depth, 2 * n * lw),
+        compiler_params=remote(3, 62),
         cost_estimate=cost(2 * 5 * 4 * pairs * total * total * LANES, 30 * MEGA, 2 * pairs * total * total),
         name="attend_back",
     )(qkv, qkv, qkv, mixture, grad_mix, lse, mask_col, out_parts, grad_attn, mix_loc)
@@ -895,7 +1042,7 @@
     anywhere = pl.BlockSpec(memory_space=pl.ANY)
     return pl.pallas_call(
         functools.partial(middle_kernel, n, img),
-        in_specs=[inner] * 5 + [anywhere],
+        in_specs=[inner] * 6,
         out_specs=[inner, inner, anywhere, anywhere],
         out_shape=[
             jax.ShapeDtypeStruct((rows, width), SINGLE),
@@ -1203,58 +1350,133 @@
     )(parts, prev, middle, attn_out, cot, weight, mods)
 
 
-def attn_in_kernel(img, dq_ref, dk_ref, dv_ref, x_ref, w_ref, da_ref, sum_ref):
-    lw = dq_ref.shape[2]
-
-    @pl.when(pl.program_id(0) == 0)
+def attn_in_kernel(
+    n, img, dq_ref, dk_ref, dv_ref, x_ref, a_ref, w_ref, y_ref, prev_ref, p_ref,
+    da_ref, sum_ref, g_ref, y_sum, p_sum, turned, p_own, *scratch,
+):
+    step = pl.program_id(0)
+    count, rows, lw = dq_ref.shape
+    line = LineSum(n, at_rows(y_ref), y_sum, *scratch[:6], first=n - 2, prev=prev_ref)
+    wide = p_sum.shape[1]
+    proj = LineSum(
+        n,
+        lambda owner: p_own.at[:, pl.ds(pl.multiple_of(owner * wide, LANES), wide)],
+        p_sum,
+        *scratch[6:12],
+    )
+    group = GroupLast(p_ref, *scratch[12:])
+    streams = ((0, slice(0, img)), (1, slice(img, rows)))
+
+    def begin():
+        greet(n, "near", "paths")
+        group.begin()
+        line.round(n - 2)
+        sum_ref[...] = jnp.zeros_like(sum_ref)
+
+    at_step(step, 0, begin)
+
+    @pl.when(step < n)
     def _():
-        sum_ref[...] = jnp.zeros_like(sum_ref)
-
-    for t, sl in ((0, slice(0, img)), (1, slice(img, x_ref.shape[1]))):
-        part = None
+        here = lax.min(step, n - 1)
+        for t, sl in streams:
+            part = None
+            for c, ref in enumerate((dq_ref, dk_ref, dv_ref)):
+                start = (3 * t + c) * lw
+                term = nt_dot(ref[here, sl], w_ref[:, start : start + lw])
+                part = term if part is None else part + term
+            da_ref[0, sl] = part.astype(HALF)
+            normed, _ = layer_norm(x_ref[0, sl].astype(SINGLE))
+            sum_ref[t, 0:1] += jnp.sum(part, axis=0, keepdims=True)
+            sum_ref[t, 1:2] += jnp.sum(part * normed, axis=0, keepdims=True)
+
+    for t, sl in streams:
+        size = count * (sl.stop - sl.start)
         for c, ref in enumerate((dq_ref, dk_ref, dv_ref)):
-            start = (3 * t + c) * lw
-            term = nt_dot(ref[0, sl], w_ref[:, start : start + lw])
-            part = term if part is None else part + term
-        da_ref[0, sl] = part.astype(HALF)
-        normed, _ = layer_norm(x_ref[0, sl].astype(SINGLE))
-        sum_ref[t, 0:1] += jnp.sum(part, axis=0, keepdims=True)
-        sum_ref[t, 1:2] += jnp.sum(part * normed, axis=0, keepdims=True)
-
-
-def attn_in_back(n, img, dq, dk, dv, x_all, weight):
+
+            @pl.when(step == n + 3 * t + c)
+            def _():
+                if c == 0:
+                    turned[:, :size] = a_ref[:, sl].reshape(size, a_ref.shape[2]).T
+                g_ref[...] = nn_dot(turned[:, :size], ref[:, sl].reshape(size, lw)).astype(HALF)
+
+    half_rows = p_ref.shape[2]
+
+    def store(half, value):
+        p_own[half * half_rows : (half + 1) * half_rows] = value.astype(HALF)
+
+    def hand_on():
+        group.finish(store)
+        proj.round(0)
+
+    at_step(step, n - 1, hand_on)
+    for hop in range(1, n - 1):
+        at_step(step, min(n + 5, n - 1 + 3 * hop), functools.partial(proj.round, hop))
+
+    def finish():
+        line.finish()
+        proj.finish()
+
+    at_step(step, n + 5, finish)
+
+
+def attn_in_back(n, img, dq, dk, dv, x_all, attn_in, weight, out_parts, running, proj):
     _, rows, lw = dq.shape
     width = x_all.shape[2]
+    anywhere = pl.BlockSpec(memory_space=pl.ANY)
+    row = pl.BlockSpec((1, rows, width), lambda k: (lax.min(k, n - 1), 0, 0))
+    tall, wide = 2 * proj.shape[2], proj.shape[3] // n
+    longest = max(up(n * img, LANES), up(n * (rows - img), LANES))
     return pl.pallas_call(
-        functools.partial(attn_in_kernel, img),
-        grid=(n,),
-        in_specs=[rows_spec(rows, lw)] * 3 + [rows_spec(rows, width), whole(weight.shape, True)],
-        out_specs=[rows_spec(rows, width), whole((2, 2, width))],
+        functools.partial(attn_in_kernel, n, img),
+        grid=(n + 6,),
+        in_specs=[whole(dq.shape, True)] * 3
+        + [row, whole(attn_in.shape, True), whole(weight.shape, True)]
+        + [anywhere, anywhere, whole(proj.shape, True)],
+        out_specs=[
+            row,
+            whole((2, 2, width)),
+            pl.BlockSpec((width, lw), lambda k: (0, lax.max(k - n, 0))),
+            whole((rows, width), True),
+            whole((tall, wide), True),
+        ],
         out_shape=[
             jax.ShapeDtypeStruct((n, rows, width), HALF),
             jax.ShapeDtypeStruct((2, 2, width), SINGLE),
+            jax.ShapeDtypeStruct((width, 6 * lw), HALF),
+            jax.ShapeDtypeStruct((rows, width), SINGLE),
+            jax.ShapeDtypeStruct((tall, wide), SINGLE),
         ],
-        compiler_params=params(),
-        cost_estimate=cost(6 * n * rows * width * lw, 30 * MEGA),
+        scratch_shapes=[
+            pltpu.VMEM((width, longest), HALF),
+            pltpu.VMEM((tall, n * wide), HALF),
+        ]
+        + LineSum.scratch(n, rows, width, first=n - 2)
+        + LineSum.scratch(n, tall, wide)
+        + GroupLast.scratch(*proj.shape[2:]),
+        compiler_params=remote(10, 62),
+        cost_estimate=cost(12 * n * rows * width * lw, 30 * MEGA),
         name="attn_in_back",
-    )(dq, dk, dv, x_all, weight)
+    )(dq, dk, dv, x_all, attn_in, weight, out_parts, running, proj)
 
 
 def end_kernel(
-    n, dp, cut, parts, packed, extra, ada_ref, sum_ref, every, cond_ref,
+    n, dp, cut, parts, qkv_part, packed, extra, ada_ref,
+    sum_ref, qkv_sum, every, cond_ref,
     z_got, row, c_part, c_got, c_all, z_send, z_recv, e_send, e_recv, c_send, c_recv, a_send, a_recv,
-    *line_scratch,
+    *scratch,
 ):
     me, my = lax.axis_index("seq"), lax.axis_index("dp")
     depth = ada_ref.shape[0]
     span = packed.shape[2]
     greet(n, "all", "all")
-    line = LineSum(n, at_rows(parts), sum_ref, *line_scratch)
-    line.round(0)
+    line = LineSum(n, at_rows(parts), sum_ref, *scratch[:6])
+    group = GroupSum(qkv_part, *scratch[6:])
     mates, others = range(1, n), range(1, dp)
     z_go = [to_line(me, n, k, packed, z_got, z_send, z_recv) for k in mates]
     for copy in z_go:
         copy.start()
+    group.begin()
+    line.round(0)
     z_got[me] = packed[me]
     for copy in z_go:
         copy.wait_recv()
@@ -1264,6 +1486,7 @@
     for copy in e_go:
         copy.start()
     every[my] = row[...]
+    group.step(0)
     for copy in e_go:
         copy.wait_recv()
     product = nt_dot(every[:, 0, :cut].astype(HALF), ada_ref[...])
@@ -1274,34 +1497,42 @@
     for copy in c_go:
         copy.start()
     c_got[my] = c_part[my]
-    for copy in c_go:
-        copy.wait_recv()
     a_go = [to_line(me, n, k, c_got, c_all, a_send, a_recv) for k in mates]
-    for copy in a_go:
-        copy.start()
-    c_all[me] = c_got[...]
     for hop in range(1, n - 1):
         line.round(hop)
+        if hop == 1:
+            for copy in c_go:
+                copy.wait_recv()
+            for copy in a_go:
+                copy.start()
+            c_all[me] = c_got[...]
+        if hop < group.phases:
+            group.step(hop)
+    for number in range(max(n - 1, 1), group.phases):
+        group.step(number)
     for copy in a_go:
         copy.wait_recv()
     cond_ref[...] = jnp.sum(c_all[...], axis=0)
+    group.finish(qkv_sum)
+    line.finish()
     for copy in z_go + e_go + c_go + a_go:
         copy.wait_send()
-    line.finish()
-
-
-def end(n, dp, cut, parts, packed, extra, ada):
+
+
+def end(n, dp, cut, parts, qkv_part, packed, extra, ada):
     rows, width = parts.shape[1:]
     depth = up(ada.shape[0], LANES)
     span = packed.shape[2] + extra.shape[1]
     inner = pl.BlockSpec(memory_space=pltpu.VMEM)
+    anywhere = pl.BlockSpec(memory_space=pl.ANY)
     sems = [n - 1, n - 1, dp - 1, dp - 1, dp - 1, dp - 1, n - 1, n - 1]
     return pl.pallas_call(
         functools.partial(end_kernel, n, dp, cut),
-        in_specs=[pl.BlockSpec(memory_space=pl.ANY), inner, inner, inner],
-        out_specs=[inner] * 3,
+        in_specs=[anywhere, anywhere, inner, inner, inner],
+        out_specs=[inner] * 4,
         out_shape=[
             jax.ShapeDtypeStruct((rows, width), SINGLE),
+            jax.ShapeDtypeStruct(qkv_part.shape[1:], SINGLE),
             jax.ShapeDtypeStruct((dp, 1, span), SINGLE),
             jax.ShapeDtypeStruct((dp, 1, depth), SINGLE),
         ],
@@ -1313,37 +1544,42 @@
             pltpu.VMEM((n, dp, 1, depth), SINGLE),
         ]
         + [pltpu.SemaphoreType.DMA((k,)) for k in sems]
-        + LineSum.scratch(n, rows, width),
-        compiler_params=remote(7),
+        + LineSum.scratch(n, rows, width)
+        + GroupSum.scratch(dp, *qkv_part.shape[2:]),
+        compiler_params=remote(7, 60),
         cost_estimate=cost(10**6, 100 * MEGA),
         name="end",
-    )(parts, packed, extra, ada)
-
-
-def proj_sum_kernel(n, wide, parts, sum_ref, *line_scratch):
-    greet(n, "near")
-
-    def part(owner):
-        return parts.at[:, pl.ds(pl.multiple_of(owner * wide, LANES), wide)]
-
-    line = LineSum(n, part, sum_ref, *line_scratch)
-    for hop in range(n - 1):
-        line.round(hop)
-    line.finish()
-
-
-def sum_proj(n, parts):
-    depth, wide = parts.shape[0], parts.shape[1] // n
+    )(parts, qkv_part, packed, extra, ada)
+
+
+def rows_kernel(img, slots, da_ref, dm_ref, x_ref, m_ref, y_ref, mod_ref, shift_ref, live_ref, io_ref, to_ref, ig_ref, tg_ref):
+    for t, sl, out_ref, grad_ref in (
+        (0, slice(0, img), io_ref, ig_ref),
+        (1, slice(img, x_ref.shape[0]), to_ref, tg_ref),
+    ):
+        keep = out_ref.shape[1]
+        live = live_ref[sl]
+        value = m_ref[sl] + mod_ref[t, 5:6] * (y_ref[sl] + shift_ref[t : t + 1])
+        out_ref[0] = (value * live).astype(HALF)[:keep]
+        normed, inv_std = layer_norm(x_ref[sl].astype(SINGLE))
+        grad = dm_ref[sl] + norm_back(normed, inv_std, da_ref[sl] * (1.0 + mod_ref[t, 1:2]))
+        grad_ref[0] = (grad * live)[:keep]
+
+
+def rows_out(img, slots, grad_attn_in, grad_middle, x_loc, middle, mlp_sum, mods, fc2_shift, live):
+    width = x_loc.shape[1]
     return pl.pallas_call(
-        functools.partial(proj_sum_kernel, n, wide),
-        in_specs=[pl.BlockSpec(memory_space=pl.ANY)],
-        out_specs=pl.BlockSpec(memory_space=pltpu.VMEM),
-        out_shape=jax.ShapeDtypeStruct((depth, wide), SINGLE),
-        scratch_shapes=LineSum.scratch(n, depth, wide),
-        compiler_params=remote(10, 32),
-        cost_estimate=cost(10**6, 20 * MEGA),
-        name="sum_proj",
-    )(parts)
+        functools.partial(rows_kernel, img, slots),
+        out_shape=[
+            jax.ShapeDtypeStruct((1, img, width), HALF),
+            jax.ShapeDtypeStruct((1, slots, width), HALF),
+            jax.ShapeDtypeStruct((1, img, width), SINGLE),
+            jax.ShapeDtypeStruct((1, slots, width), SINGLE),
+        ],
+        compiler_params=params(),
+        cost_estimate=cost(10**6, 14 * MEGA),
+        name="rows_out",
+    )(grad_attn_in, grad_middle, x_loc, middle, mlp_sum, mods, fc2_shift, live)
 
 
 def body(
@@ -1412,6 +1648,7 @@
             jnp.full((LANES,), length.astype(SINGLE)),
         ]
     )[None]
+    proj_line = lax.all_gather(proj_turned, "seq", axis=0, tiled=False)
     x_all, side_all, acts, qkv_full, fc1_full = start(
         n, dp, x_loc, act_parts, ada_flat, side, split(qkv_local), split(fc1_local)
     )
@@ -1441,9 +1678,7 @@
         [qv_bias[:, 0], jnp.zeros_like(qv_bias[:, 0]), qv_bias[:, 1]], axis=1
     ).astype(SINGLE)
     bias_rows = jnp.pad(bias_rows, ((0, 0), (0, 0), (0, lwp - lw))).reshape(2, 3 * lwp)
-    attn_in, qkv_rows, proj_line = project_qkv(
-        n, img, x_all, mods, qkv_full, bias_rows, proj_turned
-    )
+    attn_in, qkv_rows = project_qkv(n, img, x_all, mods, qkv_full, bias_rows)
     mixture, lse, e_near, mix_loc, proj_full = attend(
         n, dp, qkv_rows, mask_row, e_loc, split(proj_line)
     )
@@ -1470,20 +1705,23 @@
     grad_middle, grad_attn, sums, grad_mix = middle_back(
         n, img, mlp_in_part, running, middle, attn_out, e_loc, proj_full, mods, lwp
     )
-    grad_q, grad_k, grad_v, q_bias_part, v_bias_part, mlp_sum, proj_part = attend_back(
-        n, img, qkv_rows, mixture, grad_mix, lse, mask_col, mlp_out_part, grad_attn, mix_loc
-    )
-    proj_part, fc_sum = lax.optimization_barrier((proj_part, fc_sum))
-    proj_half = lax.psum_scatter(proj_part, "dp", scatter_dimension=0, tiled=True)
-    attn_in_part, mod_one = attn_in_back(n, img, grad_q, grad_k, grad_v, x_all, qkv_full)
-    qkv_plan = [(0, c, t, 0) for t in range(2) for c in range(3)]
-    (qkv_part,) = weight_grads(
-        n, img, (attn_in,), (grad_q, grad_k, grad_v), qkv_plan, lwp, "qkv_grad"
-    )
-    qkv_part, fc_sum = lax.optimization_barrier((qkv_part, fc_sum))
-    qkv_sum = lax.psum_scatter(qkv_part, "dp", scatter_dimension=0, tiled=True)
+    grad_q, grad_k, grad_v, q_bias_part, v_bias_part, proj_rest, out_running = attend_back(
+        n, dp, img, qkv_rows, mixture, grad_mix, lse, mask_col, mlp_out_part, grad_attn, mix_loc
+    )
+    attn_in_part, mod_one, qkv_part, mlp_sum, proj_own = attn_in_back(
+        n,
+        img,
+        grad_q,
+        grad_k,
+        grad_v,
+        x_all,
+        attn_in,
+        qkv_full,
+        mlp_out_part,
+        out_running,
+        proj_rest,
+    )
     fc1_sum, fc2_sum = fc_sum[:, : 2 * units], fc_sum[:, 2 * units :]
-    proj_own = sum_proj(n, proj_half)
 
     upstream_sum = sums[:, 4]
     gate_two = gate_two_part + fc2_shift * upstream_sum
@@ -1503,27 +1741,22 @@
     extra = jnp.concatenate(
         [jnp.stack([q_bias, v_bias], axis=1).reshape(-1), fc1_bias_part.reshape(-1)]
     )
-    grad_attn_in, every, cond_sum = end(
-        n, dp, cut, attn_in_part, packed[:, None], extra[None], ada_flat
+    grad_attn_in, qkv_sum, every, cond_sum = end(
+        n,
+        dp,
+        cut,
+        attn_in_part,
+        qkv_part.reshape(dp, 2, depth // 2, 6 * lwp),
+        packed[:, None],
+        extra[None],
+        ada_flat,
     )
     every = every[:, 0]
     total = jnp.sum(every, axis=0)
 
-    def by_row(vectors):
-        return jnp.concatenate(
-            [
-                jnp.broadcast_to(vectors[0:1], (img, width)),
-                jnp.broadcast_to(vectors[1:2], (pad, width)),
-            ]
-        )
-
-    block_out = (
-        (middle + by_row(mods[:, 5]) * (mlp_sum + by_row(fc2_shift))) * live_loc
-    ).astype(HALF)
-    normed, inv_std = layer_norm(x_loc.astype(SINGLE))
-    input_grad = (
-        grad_middle + norm_back(normed, inv_std, grad_attn_in * (1.0 + by_row(mods[:, 1])))
-    ) * live_loc
+    image_out, text_out, image_grad, text_grad = rows_out(
+        img, slots, grad_attn_in, grad_middle, x_loc, middle, mlp_sum, mods, fc2_shift, live_loc
+    )
 
     mod_half = every[:, :cut].astype(HALF).reshape(dp, 2, mod_cols)
     ada_grad = jnp.einsum("nd,ntc->dtc", act_slice, mod_half, preferred_element_type=SINGLE)
@@ -1538,14 +1771,14 @@
     def streams(flat, last):
         return flat.astype(SINGLE).reshape(depth, 2, last)
 
-    qkv_grad = qkv_sum.astype(SINGLE).reshape(depth, 2, 3, lwp)[..., :lw]
+    qkv_grad = qkv_sum.reshape(depth, 2, 3, lwp)[..., :lw]
     fc2_grad = streams(fc2_sum, units).transpose(2, 1, 0)
     proj_grad = proj_own.reshape(depth, 2, lwp)[..., :share].transpose(2, 1, 0)
     return (
-        block_out[None, :img],
-        block_out[None, img : img + slots],
-        input_grad[None, :img],
-        input_grad[None, img : img + slots],
+        image_out,
+        text_out,
+        image_grad,
+        text_grad,
         cond_grad,
         ada_grad,
         ada_bias_grad,

time: 752 us -> 712 us (0.947)
  Pallas kernels: 670 us -> 638 us
    pallas_call x5, Pallas kernels: 265 us -> 249 us  [the longest x1 92.9 us: start(): pl.pallas_call(functools.partial(start_kernel, n, dp), in_specs=[inner] *...]
    pallas_call x2 -> x1, Pallas kernels: 74.6 us -> 61.8 us  [weight_grads(): pl.pallas_call(functools.partial(grads_kernel, n, img, plan, rounds), gri...]
    unnamed x66 -> x43, local copies, waits for them, and re-layouts: 18.9 us -> 15.3 us
  transfers between devices with their start and end apart: 3 -> 2, of which waited for: 1 -> 0; matrix products, arithmetic and copies ran while one was open for 4% -> 6% of each run, Pallas kernels for 34% -> 54%
where the time goes in v3:
time: 712 us; the launch traced here: 709 us
  Pallas kernels  638 us (90%)
  local copies, waits for them, and re-layouts  44.4 us (6%)
  between operations  15.4 us (2%)
  other arithmetic  9.9 us (1%)
    pallas_call x1, Pallas kernels, start(): pl.pallas_call(functools.partial(start_kernel, n, dp), in_specs=[inner] *...  92.9 us
    pallas_call x1, Pallas kernels, middle_rows(): pl.pallas_call(functools.partial(middle_kernel, n, img), in_specs=[inner]...  81.6 us
    pallas_call x1, Pallas kernels, end(): pl.pallas_call(functools.partial(end_kernel, n, dp, cut), in_specs=[anywh...  79.2 us
    pallas_call x1, Pallas kernels, attend_back(): pl.pallas_call(functools.partial(attn_back_kernel, n, img, pairs), grid=(...  77.3 us
    pallas_call x1, Pallas kernels, feed_forward(): pl.pallas_call(functools.partial(mlp_kernel, n, img, tile), grid=(n,), in...  65.5 us
    pallas_call x1, Pallas kernels, weight_grads(): pl.pallas_call(functools.partial(grads_kernel, n, img, plan, rounds), gri...  61.8 us
    pallas_call x1, Pallas kernels, attn_in_back(): pl.pallas_call(functools.partial(attn_in_kernel, n, img), grid=(n + 6,),...  56.2 us
    pallas_call x1, Pallas kernels, middle_back(): pl.pallas_call(functools.partial(middle_back_kernel, n, img), in_specs=[a...  54.8 us
  transfers between devices with their start and end apart: 2, of which 0 were waited for; matrix products, arithmetic and copies ran while one was open for 6% of the time, Pallas kernels for 54%

profile of v3, /device:TPU:0, one launch (start us, length us, event | category | flops | bytes accessed | tf_op | source)
XLA Modules:
  0.0 708.7 jit_solution(11208863534472704748)
XLA Ops:
  7.2 1.3 copy.91
  8.5 0.9 all_gather_reshape.3
  12.9 2.9 copy.114
  17.2 2.0 reshape_reshape.9.qkv_ref
  19.1 1.7 reshape_reshape.10.fc1_ref
  20.8 1.0 fusion.2.x_ref
  21.9 92.9 %start.1 = (bf16[4,336,1536]{2,1,0:T(8,128)(2,1)}, f32[4,1,6272]{2,1,0:T(1,128)}, f32[8,1,256]{2,1,0:T(1,128)}, bf16[8,2,96,2304]{3,2,1,0:T(8,128)(2,1)}, bf16[8,2,96,3072]{3,2,1,0:T(8,128)(2,1)}) custom-call(bf16[336,1536]{1,0:T(8,128)(2,1)} %fusion.2.x_ref, f32[8,1,256]{2,1,0:T(1,128)} %pad_convert_fusion.act_ref, bf16[192,4608]{1,0:T(8,128)(2,1)} %bitcast.87, ...), custom_call_target="tpu_custom_call" | custom-call | flops 1000000 | bytes 104857600 | tf_op jit(solution)/shard_map/start/pallas_call | solution.py:653
  114.8 0.9 copy.129
  118.1 1.2 copy.93
  119.3 1.7 reshape_reshape.11.fc2_ref
  122.4 1.0 fusion.3.e_ref.e_loc
  123.4 13.2 %project_qkv.1 = (bf16[4,336,1536]{2,1,0:T(8,128)(2,1)}, bf16[4,336,1152]{2,1,0:T(8,128)(2,1)}) custom-call(bf16[4,336,1536]{2,1,0:T(8,128)(2,1)} %get-tuple-element.64.x_ref, f32[2,8,1536]{2,1,0:T(8,128)} %pad.27.clone.mod_ref, bf16[1536,2304]{1,0:T(8,128)(2,1)} %bitcast.119, f32[2,1152]{1,0:T(2,128)} %bitcast.114), custom_call_target="tpu_custom_call" | custom-call | flops 4756340736 | bytes 31457280 | tf_op jit(solution)/shard_map/project_qkv/pallas_call | solution.py:698
  136.5 48.7 %attend.1 = (bf16[4,336,384]{2,1,0:T(8,128)(2,1)}, f32[4,336,384]{2,1,0:T(8,128)}, bf16[2,336,1536]{2,1,0:T(8,128)(2,1)}, bf16[336,1536]{1,0:T(8,128)(2,1)}, bf16[8,2,384,768]{3,2,1,0:T(8,128)(2,1)}) custom-call(bf16[4,336,1152]{2,1,0:T(8,128)(2,1)} %get-tuple-element.67.q_ref.k_ref.v_ref, bf16[4,336,1152]{2,1,0:T(8,128)(2,1)} %get-tuple-element.67.q_ref.k_ref.v_ref, ...), custom_call_target="tpu_custom_call" | custom-call | flops 11098128384 | bytes 20971520 | tf_op jit(solution)/shard_map/attend/pallas_call | solution.py:809
  185.2 81.6 %middle_rows.1 = (f32[336,1536]{1,0:T(8,128)}, f32[336,1536]{1,0:T(8,128)}, bf16[4,336,1536]{2,1,0:T(8,128)(2,1)}, bf16[8,2,96,3072]{3,2,1,0:T(8,128)(2,1)}) custom-call(bf16[336,1536]{1,0:T(8,128)(2,1)} %get-tuple-element.69.mix_ref.r_ref, bf16[336,1536]{1,0:T(8,128)(2,1)} %fusion.2.x_ref, bf16[8,4,192,768]{3,2,1,0:T(8,128)(2,1)} %bitcast.85, ...), custom_call_target="tpu_custom_call" | custom-call | flops 1585446912 | bytes 104857600 | tf_op jit(solution)/shard_map/middle_rows/pallas_call | solution.py:1043
  266.9 65.5 %feed_forward.1 = (bf16[4,336,1536]{2,1,0:T(8,128)(2,1)}, bf16[4,336,1536]{2,1,0:T(8,128)(2,1)}, bf16[4,336,1536]{2,1,0:T(8,128)(2,1)}, bf16[4,336,1536]{2,1,0:T...) custom-call(bf16[4,336,1536]{2,1,0:T(8,128)(2,1)} %get-tuple-element.71.b_ref.refs_0_, ...), custom_call_target="tpu_custom_call" | custom-call | flops 19025362944 | bytes 52428800 | tf_op jit(solution)/shard_map/feed_forward/pallas_call | solution.py:1151
  332.3 61.8 %fc_grads.1 = (bf16[1536,6144]{1,0:T(8,128)(2,1)}, bf16[2,336,1536]{2,1,0:T(8,128)(2,1)}) custom-call(bf16[4,336,1536]{2,1,0:T(8,128)(2,1)} %get-tuple-element.71.b_ref.refs_0_, bf16[4,336,1536]{2,1,0:T(8,128)(2,1)} %get-tuple-element.76.refs_1_, bf16[4,336,1536]{2,1,0:T(8,128)(2,1)} %get-tuple-element.77.refs_2_, ...), custom_call_target="tpu_custom_call" | custom-call | flops 12683575296 | bytes 62914560 | tf_op jit(solution)/shard_map/fc_grads/pallas_call | solution.py:1248
  395.6 54.8 %middle_back.1 = (f32[336,1536]{1,0:T(8,128)}, bf16[336,1536]{1,0:T(8,128)(2,1)}, f32[2,8,1536]{2,1,0:T(8,128)}, bf16[4,336,384]{2,1,0:T(8,128)(2,1)}) custom-call(bf16[4,336,1536]{2,1,0:T(8,128)(2,1)} %get-tuple-element.75.refs_4_.part_ref, bf16[2,336,1536]{2,1,0:T(8,128)(2,1)} %get-tuple-element.79.prev_ref, f32[336,1536]{1,0:T(8,128)} %get-tuple-element.80.m_ref, ...), custom_call_target="tpu_custom_call" | custom-call | flops 1585446912 | bytes 62914560 | tf_op jit(solution)/shard_map/middle_back/pallas_call | solution.py:1329
  450.3 1.0 copy.98
  451.3 0.9 slice.114
  452.2 1.1 broadcast_in_dim.47.mask_ref
  453.3 77.3 %attend_back.1 = (bf16[4,336,384]{2,1,0:T(8,128)(2,1)}, bf16[4,336,384]{2,1,0:T(8,128)(2,1)}, bf16[4,336,384]{2,1,0:T(8,128)(2,1)}, f32[3,2,128]{2,1,0:T(2,128)}...) custom-call(bf16[4,336,1152]{2,1,0:T(8,128)(2,1)} %get-tuple-element.67.q_ref.k_ref.v_ref, ...), custom_call_target="tpu_custom_call" | custom-call | flops 27745320960 | bytes 31457280 | tf_op jit(solution)/shard_map/attend_back/pallas_call | solution.py:958
  532.1 56.2 %attn_in_back.1 = (bf16[4,336,1536]{2,1,0:T(8,128)(2,1)}, f32[2,2,1536]{2,1,0:T(2,128)}, bf16[1536,2304]{1,0:T(8,128)(2,1)}, f32[336,1536]{1,0:T(8,128)}, f32[192,768]{1,0:T(8,128)}) custom-call(bf16[4,336,384]{2,1,0:T(8,128)(2,1)} %get-tuple-element.86.dq_ref, bf16[4,336,384]{2,1,0:T(8,128)(2,1)} %get-tuple-element.87.dk_ref, ...), custom_call_target="tpu_custom_call" | custom-call | flops 9512681472 | bytes 31457280 | tf_op jit(solution)/shard_map/attn_in_back/pallas_call | solution.py:1429
  589.9 79.2 %end.1 = (f32[336,1536]{1,0:T(8,128)}, f32[2,96,2304]{2,1,0:T(8,128)}, f32[8,1,10752]{2,1,0:T(1,128)}, f32[8,1,256]{2,1,0:T(1,128)}) custom-call(bf16[4,336,1536]{2,1,0:T(8,128)(2,1)} %get-tuple-element.92.parts, bf16[8,2,96,2304]{3,2,1,0:T(8,128)(2,1)} %bitcast.90, f32[4,1,6144]{2,1,0:T(1,128)} %broadcast_in_dim.48.packed, ...), custom_call_target="tpu_custom_call" | custom-call | flops 1000000 | bytes 104857600 | tf_op jit(solution)/shard_map/end/pallas_call | solution.py:1529
  669.1 1.5 fusion.14
  671.4 4.5 copy.106
  675.9 3.0 reshape.353
  678.9 2.1 copy.107
  681.0 7.1 %rows_out.1 = (bf16[1,256,1536]{2,1,0:T(8,128)(2,1)}, bf16[1,77,1536]{2,1,0:T(8,128)(2,1)}, f32[1,256,1536]{2,1,0:T(8,128)}, f32[1,77,1536]{2,1,0:T(8,128)}) custom-call(f32[336,1536]{1,0:T(8,128)} %get-tuple-element.100.da_ref, f32[336,1536]{1,0:T(8,128)} %get-tuple-element.101.dm_ref, bf16[336,1536]{1,0:T(8,128)(2,1)} %fusion.2.x_ref, ...), custom_call_target="tpu_custom_call" | custom-call | flops 1000000 | bytes 14680064 | tf_op jit(solution)/shard_map/rows_out/pallas_call | solution.py:1571
  688.1 2.3 copy.105
  695.0 2.0 slice_convert_fusion
  697.0 1.6 copy.126
  698.6 3.0 reshape.366
  (101 shorter events, 17.6 us)
Async XLA Ops:
  7.2 129.4 %all-gather.2.cloned.1.call-start = ((), (), s32[]{:S(2)}) async-start(), calls=%async_computation.1 | async-start | bytes 1474560 | tf_op jit(solution)/shard_map/all_gather | solution.py:1651
  9.4 6.4 copy-start.9
  9.4 7.2 %copy-start.2 = (bf16[192,2,3,384]{3,1,2,0:T(2,128)(2,1)S(1)}, bf16[192,2,3,384]{3,1,2,0:T(2,128)(2,1)}, u32[]{:S(2)}) copy-start(bf16[192,2,3,384]{3,1,2,0:T(2,128)(2,1)} %param.22) | copy-start | bytes 2654212
  9.4 685.6 %reduce-scatter.2.cloned.1.call-start = ((), (), s32[]{:S(2)}) async-start(), calls=%async_computation.2 | async-start | bytes 21233664 | tf_op jit(solution)/shard_map/reduce_scatter | solution.py:1703
  16.5 2.6 copy-start
  17.2 3.7 copy-start.3
  17.2 3.6 copy-start.7
  21.9 93.8 %copy-start.11 = (bf16[2,2,384]{2,1,0:T(2,128)(2,1)S(1)}, bf16[2,2,384]{2,1,0:T(2,128)(2,1)}, u32[]{:S(2)}) copy-start(bf16[2,2,384]{2,1,0:T(2,128)(2,1)} %param.23) | copy-start | bytes 9220
  21.9 96.2 %copy-start.1 = (bf16[1536,2,192]{0,2,1:T(8,128)(2,1)S(1)}, bf16[1536,2,192]{0,2,1:T(8,128)(2,1)}, u32[]{:S(2)}) copy-start(bf16[1536,2,192]{0,2,1:T(8,128)(2,1)} %param.28) | copy-start | bytes 3538948
  118.1 2.9 copy-start.15
  118.1 4.2 copy-start.6
  119.3 3.1 copy-start.4
  394.2 0.7 copy-start.13
  394.2 137.8 %copy-start.8 = (f32[1,2,4,384]{3,1,2,0:T(2,128)}, f32[1,2,4,384]{3,1,2,0:T(2,128)S(1)}, u32[]{:S(2)}) copy-start(f32[1,2,4,384]{3,1,2,0:T(2,128)S(1)} %copy.117) | copy-start | bytes 36868
  453.3 78.0 %copy-start.10 = (f32[2,1536]{1,0:T(2,128)S(1)}, f32[2,1536]{1,0:T(2,128)}, u32[]{:S(2)}) copy-start(f32[2,1536]{1,0:T(2,128)} %get-tuple-element.99) | copy-start | bytes 36868
  453.3 78.7 %copy-start.12 = (f32[2,1536]{1,0:T(2,128)S(1)}, f32[2,1536]{1,0:T(2,128)}, u32[]{:S(2)}) copy-start(f32[2,1536]{1,0:T(2,128)} %get-tuple-element.96) | copy-start | bytes 36868
  681.0 12.4 %copy-start.14 = (f32[8,1,256]{2,1,0:T(1,128)S(1)}, f32[8,1,256]{2,1,0:T(1,128)}, u32[]{:S(2)}) copy-start(f32[8,1,256]{2,1,0:T(1,128)} %get-tuple-element.107) | copy-start | bytes 24580
  681.0 12.5 %copy-start.5 = (f32[192,768]{1,0:T(8,128)S(1)}, f32[192,768]{1,0:T(8,128)}, u32[]{:S(2)}) copy-start(f32[192,768]{1,0:T(8,128)} %get-tuple-element.111) | copy-start | bytes 1769476
Sparse Core Ops, SparseCore 0:
  10.2 40.0 all-gather.1
  394.3 148.0 reduce-scatter.1

commit v4 on v3

--- a/solution.py
+++ b/solution.py
@@ -594,16 +594,23 @@
 
 
 def start_kernel(
-    n, dp, x_ref, act_ref, ada_ref, side_ref, qkv_ref, fc1_ref, x_all, side_all, acts, qkv_all, fc1_all,
-    part, parts, row, a_send, a_recv, p_send, p_recv, s_send, s_recv, *sems,
+    n, dp, x_ref, cond_ref, ada_ref, ada_bias, proj_bias, fc2_bias, length_ref, qkv_ref, fc1_ref,
+    x_all, side_all, acts, mods, shifts, qkv_all, fc1_all,
+    act_ref, part, parts, row, a_send, a_recv, p_send, p_recv, s_send, s_recv, *sems,
 ):
     me, my = lax.axis_index("seq"), lax.axis_index("dp")
-    depth, cols = ada_ref.shape
+    depth, _, cols = ada_ref.shape
+    width = x_ref.shape[1]
     greet(n, "all", "all")
     gather = LineGather(n, x_ref, x_all, *sems[:3])
     qkv = GroupGather(qkv_ref, qkv_all, *sems[3:8])
     fc1 = GroupGather(fc1_ref, fc1_all, *sems[8:13])
     gather.begin()
+    cond = cond_ref[...].astype(SINGLE)
+    act = (cond / (1.0 + jnp.exp(-cond))).astype(HALF).astype(SINGLE)
+    act_ref[...] = jnp.zeros_like(act_ref)
+    for k in range(dp):
+        act_ref[k, :, :depth] = act[:, k * depth : (k + 1) * depth]
     others = range(1, dp)
     act_go = [to_group(my, dp, k, act_ref, acts, a_send, a_recv) for k in others]
     for copy in act_go:
@@ -612,19 +619,27 @@
     acts[my] = act_ref[my]
     for copy in act_go:
         copy.wait_recv()
-    product = nn_dot(acts[:, 0, :depth].astype(HALF), ada_ref[...])
-    for k in range(dp):
-        part[k] = product[k : k + 1]
+    rows = acts[:, 0, :depth].astype(HALF)
+    for t in range(2):
+        product = nn_dot(rows, ada_ref[:, t, :])
+        for k in range(dp):
+            part[k, :, t * cols : (t + 1) * cols] = product[k : k + 1]
     part_go = [to_group(my, dp, k, part, parts, p_send, p_recv) for k in others]
     for copy in part_go:
         copy.start()
     parts[my] = part[my]
+    place = 0
+    for ref in (ada_bias, proj_bias, fc2_bias):
+        for t in range(2):
+            size = ref.shape[1]
+            row[:, place : place + size] = ref[t : t + 1].astype(SINGLE)
+            place += size
+    row[:, place:] = jnp.full((1, LANES), length_ref[0, 0].astype(SINGLE))
     for copy in part_go:
         copy.wait_recv()
     qkv.begin()
     fc1.begin()
-    row[...] = side_ref[...]
-    row[:, :cols] += jnp.sum(parts[...], axis=0)
+    row[:, : 2 * cols] += jnp.sum(parts[...], axis=0)
     row_go = [to_line(me, n, k, row, side_all, s_send, s_recv) for k in range(1, n)]
     for copy in row_go:
         copy.start()
@@ -637,6 +652,19 @@
             fc1.arrive(hop)
     for copy in row_go:
         copy.wait()
+    mods[...] = jnp.zeros_like(mods)
+    piece = math.gcd(cols, width)
+    share = proj_bias.shape[1]
+    for z in range(n):
+        for t in range(2):
+            for start in range(0, cols, piece):
+                to, at = divmod(z * cols + start, width)
+                mods[t, to : to + 1, at : at + piece] = side_all[
+                    z, :, t * cols + start : t * cols + start + piece
+                ]
+        for k in range(4):
+            start = 2 * cols + k * share
+            shifts[k : k + 1, z * share : (z + 1) * share] = side_all[z, :, start : start + share]
     for copy in act_go + part_go:
         copy.wait_send()
     gather.keep().wait()
@@ -645,26 +673,31 @@
     fc1.finish()
 
 
-def start(n, dp, x_loc, act_parts, ada, side, qkv, fc1):
+def start(n, dp, x_loc, cond, ada, ada_bias, proj_bias, fc2_bias, length, qkv, fc1):
     rows, width = x_loc.shape
-    cols = ada.shape[1]
+    depth, _, cols = ada.shape
+    span = 2 * cols + 4 * proj_bias.shape[1] + LANES
     anywhere = pl.BlockSpec(memory_space=pl.ANY)
     inner = pl.BlockSpec(memory_space=pltpu.VMEM)
+    scalar = pl.BlockSpec(memory_space=pltpu.SMEM)
     return pl.pallas_call(
         functools.partial(start_kernel, n, dp),
-        in_specs=[inner] * 6,
-        out_specs=[anywhere, inner, inner, anywhere, anywhere],
+        in_specs=[inner] * 6 + [scalar, inner, inner],
+        out_specs=[anywhere, inner, inner, inner, inner, anywhere, anywhere],
         out_shape=[
             jax.ShapeDtypeStruct((n, rows, width), HALF),
-            jax.ShapeDtypeStruct((n,) + side.shape, SINGLE),
-            jax.ShapeDtypeStruct(act_parts.shape, SINGLE),
+            jax.ShapeDtypeStruct((n, 1, span), SINGLE),
+            jax.ShapeDtypeStruct((dp, 1, up(depth, LANES)), SINGLE),
+            jax.ShapeDtypeStruct((2, 8, width), SINGLE),
+            jax.ShapeDtypeStruct((4, width), SINGLE),
             jax.ShapeDtypeStruct((dp,) + qkv.shape, HALF),
             jax.ShapeDtypeStruct((dp,) + fc1.shape, HALF),
         ],
         scratch_shapes=[
-            pltpu.VMEM((dp, 1, cols), SINGLE),
-            pltpu.VMEM((dp, 1, cols), SINGLE),
-            pltpu.VMEM(side.shape, SINGLE),
+            pltpu.VMEM((dp, 1, up(depth, LANES)), SINGLE),
+            pltpu.VMEM((dp, 1, 2 * cols), SINGLE),
+            pltpu.VMEM((dp, 1, 2 * cols), SINGLE),
+            pltpu.VMEM((1, span), SINGLE),
             pltpu.SemaphoreType.DMA((dp - 1,)),
             pltpu.SemaphoreType.DMA((dp - 1,)),
             pltpu.SemaphoreType.DMA((dp - 1,)),
@@ -678,7 +711,7 @@
         compiler_params=remote(1),
         cost_estimate=cost(10**6, 100 * MEGA),
         name="start",
-    )(x_loc, act_parts, ada, side, qkv, fc1)
+    )(x_loc, cond, ada, ada_bias, proj_bias, fc2_bias, length, qkv, fc1)
 
 
 def qkv_kernel(img, x_ref, mod_ref, w_ref, b_ref, a_ref, o_ref):
@@ -841,8 +874,8 @@
 
 def attn_back_kernel(
     lines, img, pairs, q_ref, k_ref, v_ref, o_ref, g_ref, lse_ref, mask_ref, y_ref, l_ref, r_ref,
-    dq_ref, dk_ref, dv_ref, qb_ref, vb_ref, p_rest, tail,
-    acc_ref, lse_row, delta_row, turned, p_part, *scratch,
+    dq_ref, dk_ref, dv_ref, qb_ref, vb_ref, p_ref, tail,
+    acc_ref, lse_row, delta_row, turned, *scratch,
 ):
     linear = pl.program_id(0)
     ahead = 2 * lines
@@ -851,15 +884,13 @@
     step = lax.rem(lax.max(linear - ahead, 0), lines)
     n, rows, _ = q_ref.shape
     total = n * rows
-    line = LineSum(lines, at_rows(y_ref), None, *scratch[:6], stop=lines - 2, tail=tail)
-    group = GroupSum(p_part, scratch[6], None, *scratch[7:], None)
+    line = LineSum(lines, at_rows(y_ref), None, *scratch, stop=lines - 2, tail=tail)
 
     def begin():
-        greet(lines, "near", "paths")
+        greet(lines, "near")
         line.round(0)
 
     at_step(linear, 0, begin)
-    tile = r_ref.shape[1]
     for t, sl in ((0, slice(0, img)), (1, slice(img, rows))):
 
         @pl.when(linear == 0)
@@ -868,11 +899,7 @@
 
         @pl.when(both(linear < ahead, lax.rem(linear, 2) == t))
         def _():
-            column = pl.ds(pl.multiple_of(linear * tile, LANES), tile)
-            product = nn_dot(turned[:, sl], r_ref[sl]).astype(HALF)
-            p_part[:, :, :, column] = product.reshape(p_part.shape[:3] + (tile,))
-
-    at_step(linear, ahead, group.begin)
+            p_ref[...] = nn_dot(turned[:, sl], r_ref[sl]).astype(HALF).reshape(p_ref.shape)
 
     @pl.when(linear >= ahead)
     def _():
@@ -922,14 +949,7 @@
     for hop in range(1, lines - 2):
         at_step(linear, min(last, ahead + 5 * hop), functools.partial(line.round, hop))
 
-    for number in range(group.phases - 1):
-        at_step(linear, min(last, ahead + 2 + 4 * number), functools.partial(group.step, number))
-
-    def finish():
-        line.close()
-        group.close(p_rest)
-
-    at_step(linear, last, finish)
+    at_step(linear, last, line.close)
 
 
 def attend_back(n, dp, img, qkv, mixture, grad_mix, lse, mask_col, out_parts, grad_attn, mix_loc):
@@ -940,7 +960,7 @@
     ahead = 2 * n
     steps = pairs * n
     width = out_parts.shape[2]
-    depth = width // dp // 2
+    depth = width // dp
 
     def place(k):
         return lax.rem(lax.max(k - ahead, 0), n)
@@ -976,13 +996,13 @@
             block(0),
             bias,
             bias,
-            whole((2, 2, depth, 2 * n * lw), True),
+            pl.BlockSpec((dp, 1, depth, lw), lambda k: (0, lax.min(k, ahead - 1), 0, 0)),
             anywhere,
         ],
         out_shape=[jax.ShapeDtypeStruct((n, rows, lw), HALF)] * 3
         + [jax.ShapeDtypeStruct((pairs, 2, LANES), SINGLE)] * 2
         + [
-            jax.ShapeDtypeStruct((2, 2, depth, 2 * n * lw), HALF),
+            jax.ShapeDtypeStruct((dp, 2 * n, depth, lw), HALF),
             jax.ShapeDtypeStruct((2, rows, width), HALF),
         ],
         scratch_shapes=[
@@ -990,10 +1010,8 @@
             pltpu.VMEM((2, total), SINGLE),
             pltpu.VMEM((2, total), SINGLE),
             pltpu.VMEM((width, rows), HALF),
-            pltpu.VMEM((dp, 2, depth, 2 * n * lw), HALF),
         ]
-        + LineSum.scratch(n, rows, width, stop=n - 2)
-        + GroupSum.scratch_inner(dp, depth, 2 * n * lw),
+        + LineSum.scratch(n, rows, width, stop=n - 2),
         compiler_params=remote(3, 62),
         cost_estimate=cost(2 * 5 * 4 * pairs * total * total * LANES, 30 * MEGA, 2 * pairs * total * total),
         name="attend_back",
@@ -1001,9 +1019,8 @@
 
 
 def proj_columns(w_ref, z, t):
-    dp, n, depth, cols = w_ref.shape
-    half = cols // 2
-    return w_ref[:, z, :, t * half : (t + 1) * half].reshape(dp * depth, half)
+    dp, _, _, depth, heads = w_ref.shape
+    return w_ref[:, z, t].reshape(dp * depth, heads)
 
 
 def middle_kernel(
@@ -1013,7 +1030,7 @@
     fc2 = GroupGather(fc2_ref, fc2_all, *sems[3:])
     fc2.begin()
     lw = mix_ref.shape[1] // n
-    heads = w_ref.shape[3] // 2
+    heads = w_ref.shape[4]
     for t, sl in ((0, slice(0, img)), (1, slice(img, x_ref.shape[0]))):
         attn = b_ref[t : t + 1]
         for z in range(n):
@@ -1117,7 +1134,7 @@
             hidden, slope = gelu_both(pre)
             hidden = hidden.astype(HALF)
             g_ref[0, sl, here] = hidden
-            w2 = w2_ref[:, cols]
+            w2 = w2_ref[:, t, :, here].reshape(-1, tile)
             out = nt_dot(hidden, w2)
             dz = nn_dot(grad, w2) * slope
             sum_ref[t : t + 1, here] += jnp.sum(dz, axis=0, keepdims=True)
@@ -1139,7 +1156,7 @@
 def feed_forward(n, img, mlp_in, e_loc, e_near, mods, w1, b1, w2):
     rows, width = mlp_in.shape[1:]
     units = w1.shape[1] // 2
-    tile = min(512, units)
+    tile = min(768, units)
     while units % tile:
         tile -= LANES
 
@@ -1208,9 +1225,9 @@
         at_step(step, 0, begin)
     else:
         o_ref, turned = rest
-    tile = o_ref.shape[1]
+    tile = 512 if o_ref.shape[3] % 512 == 0 else 2 * LANES
     before = None
-    for k, (left, right, stream, column) in enumerate(plan):
+    for k, (left, right, stream) in enumerate(plan):
 
         @pl.when(step == k)
         def _():
@@ -1220,8 +1237,12 @@
             size = count * (sl.stop - sl.start)
             if before != (left, stream):
                 turned[:, :size] = l_ref[:, sl].reshape(size, l_ref.shape[2]).T
-            values = r_ref[:, sl, column : column + tile].reshape(size, tile)
-            o_ref[...] = nn_dot(turned[:, :size], values).astype(HALF)
+            for column in range(0, o_ref.shape[3], tile):
+                values = r_ref[:, sl, column : column + tile].reshape(size, tile)
+                product = nn_dot(turned[:, :size], values).astype(HALF)
+                o_ref[:, 0, :, column : column + tile] = product.reshape(
+                    o_ref.shape[0], o_ref.shape[2], tile
+                )
 
         before = (left, stream)
     if rounds:
@@ -1230,32 +1251,27 @@
         at_step(step, len(plan) - 1, line.close)
 
 
-def weight_grads(n, img, lefts, rights, plan, tile, name, rounds=(), parts=None, collective=None):
+def weight_grads(n, dp, img, lefts, rights, plan, rounds, parts, collective, name):
     rows, depth = lefts[0].shape[1:]
-    in_specs = [whole(a.shape, True) for a in (*lefts, *rights)]
-    out_specs = [pl.BlockSpec((depth, tile), lambda k: (0, k))]
-    out_shape = [jax.ShapeDtypeStruct((depth, len(plan) * tile), HALF)]
+    wide = rights[0].shape[2]
+    anywhere = pl.BlockSpec(memory_space=pl.ANY)
+    block = (dp, 1, depth // dp, wide)
     longest = max(up(n * img, LANES), up(n * (rows - img), LANES))
-    scratch = [pltpu.VMEM((depth, longest), HALF)]
-    arrays = (*lefts, *rights)
-    if rounds:
-        anywhere = pl.BlockSpec(memory_space=pl.ANY)
-        in_specs.append(anywhere)
-        out_specs.append(anywhere)
-        out_shape.append(jax.ShapeDtypeStruct((2,) + parts.shape[1:], HALF))
-        scratch += LineSum.scratch(n, *parts.shape[1:], stop=n - 2)
-        arrays += (parts,)
     return pl.pallas_call(
         functools.partial(grads_kernel, n, img, plan, rounds),
         grid=(len(plan),),
-        in_specs=in_specs,
-        out_specs=out_specs,
-        out_shape=out_shape,
-        scratch_shapes=scratch,
-        compiler_params=remote(collective, 60) if rounds else params(60),
-        cost_estimate=cost(2 * n * rows * depth * len(plan) * tile // 2, 60 * MEGA),
+        in_specs=[whole(a.shape, True) for a in (*lefts, *rights)] + [anywhere],
+        out_specs=[pl.BlockSpec(block, lambda k: (0, k, 0, 0)), anywhere],
+        out_shape=[
+            jax.ShapeDtypeStruct((dp, len(plan), depth // dp, wide), HALF),
+            jax.ShapeDtypeStruct((2,) + parts.shape[1:], HALF),
+        ],
+        scratch_shapes=[pltpu.VMEM((depth, longest), HALF)]
+        + LineSum.scratch(n, *parts.shape[1:], stop=n - 2),
+        compiler_params=remote(collective, 60),
+        cost_estimate=cost(2 * n * rows * depth * len(plan) * wide // 2, 60 * MEGA),
         name=name,
-    )(*arrays)
+    )(*lefts, *rights, parts)
 
 
 def middle_back_kernel(
@@ -1264,7 +1280,7 @@
 ):
     me = lax.axis_index("seq")
     rows, width = m_ref.shape
-    heads = w_ref.shape[3] // 2
+    heads = w_ref.shape[4]
     streams = ((0, slice(0, img)), (1, slice(img, rows)))
     greet(n, "all")
     line = LineSum(n, at_rows(part_ref), db_ref, *line_scratch, first=n - 2, prev=prev_ref)
@@ -1352,19 +1368,12 @@
 
 def attn_in_kernel(
     n, img, dq_ref, dk_ref, dv_ref, x_ref, a_ref, w_ref, y_ref, prev_ref, p_ref,
-    da_ref, sum_ref, g_ref, y_sum, p_sum, turned, p_own, *scratch,
+    da_ref, sum_ref, g_ref, y_sum, p_rest, turned, *scratch,
 ):
     step = pl.program_id(0)
     count, rows, lw = dq_ref.shape
     line = LineSum(n, at_rows(y_ref), y_sum, *scratch[:6], first=n - 2, prev=prev_ref)
-    wide = p_sum.shape[1]
-    proj = LineSum(
-        n,
-        lambda owner: p_own.at[:, pl.ds(pl.multiple_of(owner * wide, LANES), wide)],
-        p_sum,
-        *scratch[6:12],
-    )
-    group = GroupLast(p_ref, *scratch[12:])
+    group = GroupSum(p_ref, *scratch[6:])
     streams = ((0, slice(0, img)), (1, slice(img, rows)))
 
     def begin():
@@ -1399,22 +1408,12 @@
                     turned[:, :size] = a_ref[:, sl].reshape(size, a_ref.shape[2]).T
                 g_ref[...] = nn_dot(turned[:, :size], ref[:, sl].reshape(size, lw)).astype(HALF)
 
-    half_rows = p_ref.shape[2]
-
-    def store(half, value):
-        p_own[half * half_rows : (half + 1) * half_rows] = value.astype(HALF)
-
-    def hand_on():
-        group.finish(store)
-        proj.round(0)
-
-    at_step(step, n - 1, hand_on)
-    for hop in range(1, n - 1):
-        at_step(step, min(n + 5, n - 1 + 3 * hop), functools.partial(proj.round, hop))
+    for number in range(group.phases - 1):
+        at_step(step, min(n + 5, 1 + 5 * number), functools.partial(group.step, number))
 
     def finish():
         line.finish()
-        proj.finish()
+        group.close(p_rest)
 
     at_step(step, n + 5, finish)
 
@@ -1424,35 +1423,30 @@
     width = x_all.shape[2]
     anywhere = pl.BlockSpec(memory_space=pl.ANY)
     row = pl.BlockSpec((1, rows, width), lambda k: (lax.min(k, n - 1), 0, 0))
-    tall, wide = 2 * proj.shape[2], proj.shape[3] // n
     longest = max(up(n * img, LANES), up(n * (rows - img), LANES))
     return pl.pallas_call(
         functools.partial(attn_in_kernel, n, img),
         grid=(n + 6,),
         in_specs=[whole(dq.shape, True)] * 3
         + [row, whole(attn_in.shape, True), whole(weight.shape, True)]
-        + [anywhere, anywhere, whole(proj.shape, True)],
+        + [anywhere] * 3,
         out_specs=[
             row,
             whole((2, 2, width)),
             pl.BlockSpec((width, lw), lambda k: (0, lax.max(k - n, 0))),
             whole((rows, width), True),
-            whole((tall, wide), True),
+            whole((2, 2) + proj.shape[2:], True),
         ],
         out_shape=[
             jax.ShapeDtypeStruct((n, rows, width), HALF),
             jax.ShapeDtypeStruct((2, 2, width), SINGLE),
             jax.ShapeDtypeStruct((width, 6 * lw), HALF),
             jax.ShapeDtypeStruct((rows, width), SINGLE),
-            jax.ShapeDtypeStruct((tall, wide), SINGLE),
+            jax.ShapeDtypeStruct((2, 2) + proj.shape[2:], HALF),
         ],
-        scratch_shapes=[
-            pltpu.VMEM((width, longest), HALF),
-            pltpu.VMEM((tall, n * wide), HALF),
-        ]
+        scratch_shapes=[pltpu.VMEM((width, longest), HALF)]
         + LineSum.scratch(n, rows, width, first=n - 2)
-        + LineSum.scratch(n, tall, wide)
-        + GroupLast.scratch(*proj.shape[2:]),
+        + GroupSum.scratch(proj.shape[0], *proj.shape[2:]),
         compiler_params=remote(10, 62),
         cost_estimate=cost(12 * n * rows * width * lw, 30 * MEGA),
         name="attn_in_back",
@@ -1460,8 +1454,8 @@
 
 
 def end_kernel(
-    n, dp, cut, parts, qkv_part, packed, extra, ada_ref,
-    sum_ref, qkv_sum, every, cond_ref,
+    n, dp, cut, parts, qkv_part, p_rest, packed, extra, ada_ref,
+    sum_ref, qkv_sum, p_own, every, cond_ref,
     z_got, row, c_part, c_got, c_all, z_send, z_recv, e_send, e_recv, c_send, c_recv, a_send, a_recv,
     *scratch,
 ):
@@ -1470,12 +1464,14 @@
     span = packed.shape[2]
     greet(n, "all", "all")
     line = LineSum(n, at_rows(parts), sum_ref, *scratch[:6])
-    group = GroupSum(qkv_part, *scratch[6:])
+    group = GroupSum(qkv_part, *scratch[6:15])
+    proj = GroupLast(p_rest, *scratch[15:])
     mates, others = range(1, n), range(1, dp)
     z_go = [to_line(me, n, k, packed, z_got, z_send, z_recv) for k in mates]
     for copy in z_go:
         copy.start()
     group.begin()
+    proj.begin()
     line.round(0)
     z_got[me] = packed[me]
     for copy in z_go:
@@ -1489,7 +1485,9 @@
     group.step(0)
     for copy in e_go:
         copy.wait_recv()
-    product = nt_dot(every[:, 0, :cut].astype(HALF), ada_ref[...])
+    cols = cut // 2
+    product = nt_dot(every[:, 0, :cols].astype(HALF), ada_ref[:, 0, :])
+    product = product + nt_dot(every[:, 0, cols:cut].astype(HALF), ada_ref[:, 1, :])
     c_part[...] = jnp.zeros_like(c_part)
     for k in range(dp):
         c_part[k, :, :depth] = product[k : k + 1]
@@ -1514,12 +1512,17 @@
         copy.wait_recv()
     cond_ref[...] = jnp.sum(c_all[...], axis=0)
     group.finish(qkv_sum)
+
+    def store(half, value):
+        p_own[half] = value.astype(HALF)
+
+    proj.finish(store)
     line.finish()
     for copy in z_go + e_go + c_go + a_go:
         copy.wait_send()
 
 
-def end(n, dp, cut, parts, qkv_part, packed, extra, ada):
+def end(n, dp, cut, parts, qkv_part, proj_rest, packed, extra, ada):
     rows, width = parts.shape[1:]
     depth = up(ada.shape[0], LANES)
     span = packed.shape[2] + extra.shape[1]
@@ -1528,11 +1531,12 @@
     sems = [n - 1, n - 1, dp - 1, dp - 1, dp - 1, dp - 1, n - 1, n - 1]
     return pl.pallas_call(
         functools.partial(end_kernel, n, dp, cut),
-        in_specs=[anywhere, anywhere, inner, inner, inner],
-        out_specs=[inner] * 4,
+        in_specs=[anywhere, anywhere, inner, inner, inner, inner],
+        out_specs=[inner] * 5,
         out_shape=[
             jax.ShapeDtypeStruct((rows, width), SINGLE),
             jax.ShapeDtypeStruct(qkv_part.shape[1:], SINGLE),
+            jax.ShapeDtypeStruct(proj_rest.shape[1:], HALF),
             jax.ShapeDtypeStruct((dp, 1, span), SINGLE),
             jax.ShapeDtypeStruct((dp, 1, depth), SINGLE),
         ],
@@ -1545,11 +1549,12 @@
         ]
         + [pltpu.SemaphoreType.DMA((k,)) for k in sems]
         + LineSum.scratch(n, rows, width)
-        + GroupSum.scratch(dp, *qkv_part.shape[2:]),
+        + GroupSum.scratch(dp, *qkv_part.shape[2:])
+        + GroupLast.scratch(*proj_rest.shape[2:]),
         compiler_params=remote(7, 60),
         cost_estimate=cost(10**6, 100 * MEGA),
         name="end",
-    )(parts, qkv_part, packed, extra, ada)
+    )(parts, qkv_part, proj_rest, packed, extra, ada)
 
 
 def rows_kernel(img, slots, da_ref, dm_ref, x_ref, m_ref, y_ref, mod_ref, shift_ref, live_ref, io_ref, to_ref, ig_ref, tg_ref):
@@ -1628,42 +1633,30 @@
 
     qkv_local = jnp.pad(qkv_weight, ((0, 0), (0, 0), (0, 0), (0, lwp - lw))).reshape(depth, 6 * lwp)
     share = proj_weight.shape[0]
-    proj_turned = proj_weight.transpose(2, 1, 0).reshape(depth, 2 * share)
     fc1_local = fc1_weight.reshape(depth, 2 * units)
-    fc2_turned = fc2_weight.transpose(2, 1, 0).reshape(depth, 2 * units)
 
     cond_float = conditioning.astype(SINGLE)
-    cond_act = jax.nn.silu(cond_float).astype(HALF)
-    act_parts = jnp.pad(
-        cond_act.astype(SINGLE).reshape(dp, 1, depth), ((0, 0), (0, 0), (0, up(depth, LANES) - depth))
-    )
-    ada_flat = ada_weight.reshape(depth, 2 * mod_cols)
     bias_cols = proj_bias.shape[1]
     cut = 2 * mod_cols
-    side = jnp.concatenate(
-        [
-            ada_bias.astype(SINGLE).reshape(-1),
-            proj_bias.astype(SINGLE).reshape(-1),
-            fc2_bias.astype(SINGLE).reshape(-1),
-            jnp.full((LANES,), length.astype(SINGLE)),
-        ]
-    )[None]
-    proj_line = lax.all_gather(proj_turned, "seq", axis=0, tiled=False)
-    x_all, side_all, acts, qkv_full, fc1_full = start(
-        n, dp, x_loc, act_parts, ada_flat, side, split(qkv_local), split(fc1_local)
+    proj_line = lax.all_gather(proj_weight.transpose(1, 2, 0), "seq", axis=0, tiled=False)
+    x_all, side_all, acts, mods, shifts, qkv_full, fc1_full = start(
+        n,
+        dp,
+        x_loc,
+        conditioning,
+        ada_weight,
+        ada_bias,
+        proj_bias,
+        fc2_bias,
+        text_lengths,
+        split(qkv_local),
+        split(fc1_local),
     )
     qkv_full = qkv_full.reshape(width, 6 * lwp)
     fc1_full = fc1_full.reshape(width, 2 * units)
     act_slice = acts[:, 0, :depth].astype(HALF)
-    side_all = side_all[:, 0]
-
-    def columns(begin, cols):
-        return side_all[:, begin : begin + 2 * cols].reshape(n, 2, cols).transpose(1, 0, 2)
-
-    mods = jnp.pad(columns(0, mod_cols).reshape(2, 6, width), ((0, 0), (0, 2), (0, 0)))
-    proj_shift = columns(cut, bias_cols).reshape(2, width)
-    fc2_shift = columns(cut + 2 * bias_cols, bias_cols).reshape(2, width)
-    lengths_all = side_all[:, cut + 4 * bias_cols]
+    proj_shift, fc2_shift = shifts[:2], shifts[2:]
+    lengths_all = side_all[:, 0, cut + 4 * bias_cols]
 
     slot = jnp.arange(rows, dtype=SINGLE)[None, :] - img
     live = jnp.logical_or(slot < 0, jnp.logical_and(slot < lengths_all[:, None], slot < slots))
@@ -1680,35 +1673,34 @@
     bias_rows = jnp.pad(bias_rows, ((0, 0), (0, 0), (0, lwp - lw))).reshape(2, 3 * lwp)
     attn_in, qkv_rows = project_qkv(n, img, x_all, mods, qkv_full, bias_rows)
     mixture, lse, e_near, mix_loc, proj_full = attend(
-        n, dp, qkv_rows, mask_row, e_loc, split(proj_line)
-    )
-    proj_full = proj_full.reshape(dp, n, depth, 2 * share)
+        n, dp, qkv_rows, mask_row, e_loc, proj_line.reshape(2, -1, share)
+    )
+    proj_full = proj_full.reshape(dp, n, 2, depth, share)
 
     attn_out, middle, mlp_in, fc2_full = middle_rows(
-        n, dp, img, mix_loc, x_loc, proj_full, proj_shift, mods, split(fc2_turned)
-    )
-    fc2_full = fc2_full.reshape(width, 2 * units)
+        n, dp, img, mix_loc, x_loc, proj_full, proj_shift, mods, fc2_weight.transpose(1, 2, 0)
+    )
     hidden, grad_pre, grad_mlp, mlp_in_part, mlp_out_part, fc1_bias_part, gate_two_part = (
         feed_forward(
             n, img, mlp_in, e_loc, e_near, mods, fc1_full, fc1_bias.astype(SINGLE), fc2_full
         )
     )
-    tile = units // 4 if units % (4 * LANES) == 0 else units // 2
-    tiles = units // tile
-    fc_plan = [(w, w, t, k * tile) for w in range(2) for t in range(2) for k in range(tiles)]
-    fc_rounds = [(k + 1) * 4 * tiles * 2 // (3 * (n - 2)) for k in range(n - 3)]
+    fc_plan = [(w, w, t) for w in range(2) for t in range(2)]
+    fc_rounds = [(k + 1) * 4 // (n - 2) for k in range(n - 3)]
     fc_part, running = weight_grads(
-        n, img, (mlp_in, grad_mlp), (grad_pre, hidden), fc_plan, tile, "fc_grads", fc_rounds, mlp_in_part, 6
-    )
-    fc_sum = lax.psum_scatter(fc_part, "dp", scatter_dimension=0, tiled=True)
+        n, dp, img, (mlp_in, grad_mlp), (grad_pre, hidden), fc_plan, fc_rounds, mlp_in_part, 6, "fc_grads"
+    )
+    fc_sum = lax.psum_scatter(
+        fc_part.reshape(dp * 4 * depth, units), "dp", scatter_dimension=0, tiled=True
+    ).reshape(4, depth, units)
 
     grad_middle, grad_attn, sums, grad_mix = middle_back(
         n, img, mlp_in_part, running, middle, attn_out, e_loc, proj_full, mods, lwp
     )
-    grad_q, grad_k, grad_v, q_bias_part, v_bias_part, proj_rest, out_running = attend_back(
+    grad_q, grad_k, grad_v, q_bias_part, v_bias_part, proj_part, out_running = attend_back(
         n, dp, img, qkv_rows, mixture, grad_mix, lse, mask_col, mlp_out_part, grad_attn, mix_loc
     )
-    attn_in_part, mod_one, qkv_part, mlp_sum, proj_own = attn_in_back(
+    attn_in_part, mod_one, qkv_part, mlp_sum, proj_rest = attn_in_back(
         n,
         img,
         grad_q,
@@ -1719,9 +1711,9 @@
         qkv_full,
         mlp_out_part,
         out_running,
-        proj_rest,
-    )
-    fc1_sum, fc2_sum = fc_sum[:, : 2 * units], fc_sum[:, 2 * units :]
+        proj_part.reshape(dp, 2, n * depth, lwp),
+    )
+    fc_own = fc_sum.astype(SINGLE)
 
     upstream_sum = sums[:, 4]
     gate_two = gate_two_part + fc2_shift * upstream_sum
@@ -1741,16 +1733,21 @@
     extra = jnp.concatenate(
         [jnp.stack([q_bias, v_bias], axis=1).reshape(-1), fc1_bias_part.reshape(-1)]
     )
-    grad_attn_in, qkv_sum, every, cond_sum = end(
+    grad_attn_in, qkv_sum, proj_own, every, cond_sum = end(
         n,
         dp,
         cut,
         attn_in_part,
         qkv_part.reshape(dp, 2, depth // 2, 6 * lwp),
+        proj_rest,
         packed[:, None],
         extra[None],
-        ada_flat,
-    )
+        ada_weight,
+    )
+    proj_own, fc_sum = lax.optimization_barrier((proj_own, fc_sum))
+    proj_sum = lax.psum_scatter(
+        proj_own.reshape(n * 2 * depth, lwp), "seq", scatter_dimension=0, tiled=True
+    ).reshape(2, depth, lwp)
     every = every[:, 0]
     total = jnp.sum(every, axis=0)
 
@@ -1768,12 +1765,10 @@
     fc1_bias_grad = total[after + 4 * lw :].reshape(2, units)
     cond_grad = cond_sum[:, 0, :depth].reshape(1, width) * silu_slope(cond_float)
 
-    def streams(flat, last):
-        return flat.astype(SINGLE).reshape(depth, 2, last)
-
     qkv_grad = qkv_sum.reshape(depth, 2, 3, lwp)[..., :lw]
-    fc2_grad = streams(fc2_sum, units).transpose(2, 1, 0)
-    proj_grad = proj_own.reshape(depth, 2, lwp)[..., :share].transpose(2, 1, 0)
+    fc1_grad = fc_own[:2].transpose(1, 0, 2)
+    fc2_grad = fc_own[2:].transpose(2, 0, 1)
+    proj_grad = proj_sum.astype(SINGLE)[..., :share].transpose(2, 0, 1)
     return (
         image_out,
         text_out,
@@ -1786,7 +1781,7 @@
         qv_bias_grad,
         proj_grad,
         proj_bias_grad,
-        streams(fc1_sum, units),
+        fc1_grad,
         fc1_bias_grad,
         fc2_grad,
         fc2_bias_grad,

time: 712 us -> 685 us (0.962)
  Pallas kernels: 638 us -> 614 us
  local copies, waits for them, and re-layouts: 44.4 us -> 33.8 us
    pallas_call x1, Pallas kernels: 77.3 us -> 60.9 us  [attend_back(): pl.pallas_call(functools.partial(attn_back_kernel, n, img, pairs), grid=(...]
    pallas_call x1, Pallas kernels: 61.8 us -> 50.2 us  [weight_grads(): pl.pallas_call(functools.partial(grads_kernel, n, img, plan, rounds), gri...]
    unnamed x43 -> x33, local copies, waits for them, and re-layouts: 15.3 us -> 14.2 us
  transfers between devices with their start and end apart: 2 -> 3, of which waited for: 0 -> 0; matrix products, arithmetic and copies ran while one was open for 6% -> 6% of each run, Pallas kernels for 54% -> 55%
where the time goes in v4:
time: 685 us; the launch traced here: 676 us
  Pallas kernels  614 us (90%)
  local copies, waits for them, and re-layouts  33.8 us (5%)
  between operations  15 us (2%)
  other arithmetic  11.6 us (2%)
    pallas_call x1, Pallas kernels, start(): pl.pallas_call(functools.partial(start_kernel, n, dp), in_specs=[inner] *...  97.5 us
    pallas_call x1, Pallas kernels, end(): pl.pallas_call(functools.partial(end_kernel, n, dp, cut), in_specs=[anywh...  85.8 us
    pallas_call x1, Pallas kernels, middle_rows(): pl.pallas_call(functools.partial(middle_kernel, n, img), in_specs=[inner]...  82.4 us
    pallas_call x1, Pallas kernels, feed_forward(): pl.pallas_call(functools.partial(mlp_kernel, n, img, tile), grid=(n,), in...  62.9 us
    pallas_call x1, Pallas kernels, attend_back(): pl.pallas_call(functools.partial(attn_back_kernel, n, img, pairs), grid=(...  60.9 us
    pallas_call x1, Pallas kernels, middle_back(): pl.pallas_call(functools.partial(middle_back_kernel, n, img), in_specs=[a...  55.7 us
    pallas_call x1, Pallas kernels, weight_grads(): pl.pallas_call(functools.partial(grads_kernel, n, img, plan, rounds), gri...  50.2 us
    pallas_call x1, Pallas kernels, attn_in_back(): pl.pallas_call(functools.partial(attn_in_kernel, n, img), grid=(n + 6,),...  49.3 us
  transfers between devices with their start and end apart: 3, of which 0 were waited for; matrix products, arithmetic and copies ran while one was open for 6% of the time, Pallas kernels for 55%

profile of v4, /device:TPU:0, one launch (start us, length us, event | category | flops | bytes accessed | tf_op | source)
XLA Modules:
  0.0 675.7 jit_solution(11207326340988226281)
XLA Ops:
  8.0 0.8 fusion.17
  8.7 2.3 fusion.2.x_ref
  12.6 2.0 reshape_reshape.6.qkv_ref
  14.5 1.7 reshape_reshape.7.fc1_ref
  16.8 97.5 %start.1 = (bf16[4,336,1536]{2,1,0:T(8,128)(2,1)}, f32[4,1,6272]{2,1,0:T(1,128)}, f32[8,1,256]{2,1,0:T(1,128)}, f32[2,8,1536]{2,1,0:T(8,128)}, f32[4,1536]{1,0:T...) custom-call(bf16[336,1536]{1,0:T(8,128)(2,1)} %fusion.2.x_ref, bf16[1,1536]{1,0:T(2,128)(2,1)} %cond_ref.1, ...), custom_call_target="tpu_custom_call" | custom-call | flops 1000000 | bytes 104857600 | tf_op jit(solution)/shard_map/start/pallas_call | solution.py:683
  114.3 0.8 slice_reduce_fusion.1
  115.9 1.3 slice.108.b_ref
  117.9 1.0 fusion.3.e_ref.e_loc
  118.9 13.2 %project_qkv.1 = (bf16[4,336,1536]{2,1,0:T(8,128)(2,1)}, bf16[4,336,1152]{2,1,0:T(8,128)(2,1)}) custom-call(bf16[4,336,1536]{2,1,0:T(8,128)(2,1)} %get-tuple-element.68.x_ref, f32[2,8,1536]{2,1,0:T(8,128)} %get-tuple-element.69.mod_ref, bf16[1536,2304]{1,0:T(8,128)(2,1)} %bitcast.83, f32[2,1152]{1,0:T(2,128)} %bitcast.79), custom_call_target="tpu_custom_call" | custom-call | flops 4756340736 | bytes 31457280 | tf_op jit(solution)/shard_map/project_qkv/pallas_call | solution.py:731
  132.1 48.6 %attend.1 = (bf16[4,336,384]{2,1,0:T(8,128)(2,1)}, f32[4,336,384]{2,1,0:T(8,128)}, bf16[2,336,1536]{2,1,0:T(8,128)(2,1)}, bf16[336,1536]{1,0:T(8,128)(2,1)}, bf16[8,2,768,384]{3,2,1,0:T(8,128)(2,1)}) custom-call(bf16[4,336,1152]{2,1,0:T(8,128)(2,1)} %get-tuple-element.71.q_ref.k_ref.v_ref, bf16[4,336,1152]{2,1,0:T(8,128)(2,1)} %get-tuple-element.71.q_ref.k_ref.v_ref, ...), custom_call_target="tpu_custom_call" | custom-call | flops 11098128384 | bytes 20971520 | tf_op jit(solution)/shard_map/attend/pallas_call | solution.py:842
  180.8 82.4 %middle_rows.1 = (f32[336,1536]{1,0:T(8,128)}, f32[336,1536]{1,0:T(8,128)}, bf16[4,336,1536]{2,1,0:T(8,128)(2,1)}, bf16[8,2,192,1536]{3,2,1,0:T(8,128)(2,1)}) custom-call(bf16[336,1536]{1,0:T(8,128)(2,1)} %get-tuple-element.74.mix_ref.r_ref, bf16[336,1536]{1,0:T(8,128)(2,1)} %fusion.2.x_ref, bf16[8,4,2,192,384]{4,3,2,1,0:T(8,128)(2,1)} %bitcast.63, ...), custom_call_target="tpu_custom_call" | custom-call | flops 1585446912 | bytes 104857600 | tf_op jit(solution)/shard_map/middle_rows/pallas_call | solution.py:1060
  263.1 62.9 %feed_forward.1 = (bf16[4,336,1536]{2,1,0:T(8,128)(2,1)}, bf16[4,336,1536]{2,1,0:T(8,128)(2,1)}, bf16[4,336,1536]{2,1,0:T(8,128)(2,1)}, bf16[4,336,1536]{2,1,0:T...) custom-call(bf16[4,336,1536]{2,1,0:T(8,128)(2,1)} %get-tuple-element.77.b_ref.refs_0_, ...), custom_call_target="tpu_custom_call" | custom-call | flops 19025362944 | bytes 52428800 | tf_op jit(solution)/shard_map/feed_forward/pallas_call | solution.py:1168
  326.0 50.2 %fc_grads.1 = (bf16[8,4,192,1536]{3,2,1,0:T(8,128)(2,1)}, bf16[2,336,1536]{2,1,0:T(8,128)(2,1)}) custom-call(bf16[4,336,1536]{2,1,0:T(8,128)(2,1)} %get-tuple-element.77.b_ref.refs_0_, bf16[4,336,1536]{2,1,0:T(8,128)(2,1)} %get-tuple-element.82.refs_1_, bf16[4,336,1536]{2,1,0:T(8,128)(2,1)} %get-tuple-element.83.refs_2_, ...), custom_call_target="tpu_custom_call" | custom-call | flops 12683575296 | bytes 62914560 | tf_op jit(solution)/shard_map/fc_grads/pallas_call | solution.py:1260
  376.3 0.8 copy-done.1
  377.2 55.7 %middle_back.1 = (f32[336,1536]{1,0:T(8,128)}, bf16[336,1536]{1,0:T(8,128)(2,1)}, f32[2,8,1536]{2,1,0:T(8,128)}, bf16[4,336,384]{2,1,0:T(8,128)(2,1)}) custom-call(bf16[4,336,1536]{2,1,0:T(8,128)(2,1)} %get-tuple-element.81.refs_4_.part_ref, bf16[2,336,1536]{2,1,0:T(8,128)(2,1)} %get-tuple-element.85.prev_ref, f32[336,1536]{1,0:T(8,128)} %get-tuple-element.86.m_ref, ...), custom_call_target="tpu_custom_call" | custom-call | flops 1585446912 | bytes 62914560 | tf_op jit(solution)/shard_map/middle_back/pallas_call | solution.py:1345
  432.9 1.0 copy.61
  433.9 0.9 slice.109
  434.8 1.1 broadcast_in_dim.39.mask_ref
  435.9 60.9 %attend_back.1 = (bf16[4,336,384]{2,1,0:T(8,128)(2,1)}, bf16[4,336,384]{2,1,0:T(8,128)(2,1)}, bf16[4,336,384]{2,1,0:T(8,128)(2,1)}, f32[3,2,128]{2,1,0:T(2,128)}...) custom-call(bf16[4,336,1152]{2,1,0:T(8,128)(2,1)} %get-tuple-element.71.q_ref.k_ref.v_ref, ...), custom_call_target="tpu_custom_call" | custom-call | flops 27745320960 | bytes 31457280 | tf_op jit(solution)/shard_map/attend_back/pallas_call | solution.py:978
  498.8 49.3 %attn_in_back.1 = (bf16[4,336,1536]{2,1,0:T(8,128)(2,1)}, f32[2,2,1536]{2,1,0:T(2,128)}, bf16[1536,2304]{1,0:T(8,128)(2,1)}, f32[336,1536]{1,0:T(8,128)}, bf16[2,2,768,384]{3,2,1,0:T(8,128)(2,1)}) custom-call(bf16[4,336,384]{2,1,0:T(8,128)(2,1)} %get-tuple-element.92.dq_ref, bf16[4,336,384]{2,1,0:T(8,128)(2,1)} %get-tuple-element.93.dk_ref, ...), custom_call_target="tpu_custom_call" | custom-call | flops 9512681472 | bytes 31457280 | tf_op jit(solution)/shard_map/attn_in_back/pallas_call | solution.py:1427
  548.2 0.8 pad_maximum_fusion
  549.1 0.7 broadcast_in_dim.40.packed
  549.8 85.8 %end.1 = (f32[336,1536]{1,0:T(8,128)}, f32[2,96,2304]{2,1,0:T(8,128)}, bf16[2,768,384]{2,1,0:T(8,128)(2,1)}, f32[8,1,10752]{2,1,0:T(1,128)}, f32[8,1,256]{2,1,0:T(1,128)}) custom-call(bf16[4,336,1536]{2,1,0:T(8,128)(2,1)} %get-tuple-element.98.parts, bf16[8,2,96,2304]{3,2,1,0:T(8,128)(2,1)} %bitcast.66, bf16[2,2,768,384]{3,2,1,0:T(8,128)(2,1)} %get-tuple-element.100.p_rest, ...), custom_call_target="tpu_custom_call" | custom-call | flops 1000000 | bytes 104857600 | tf_op jit(solution)/shard_map/end/pallas_call | solution.py:1532
  636.4 1.5 fusion.14
  638.7 4.5 copy.67
  643.2 2.9 reshape.297
  646.1 2.1 copy.68
  648.2 7.3 %rows_out.1 = (bf16[1,256,1536]{2,1,0:T(8,128)(2,1)}, bf16[1,77,1536]{2,1,0:T(8,128)(2,1)}, f32[1,256,1536]{2,1,0:T(8,128)}, f32[1,77,1536]{2,1,0:T(8,128)}) custom-call(f32[336,1536]{1,0:T(8,128)} %get-tuple-element.107.da_ref, f32[336,1536]{1,0:T(8,128)} %get-tuple-element.108.dm_ref, bf16[336,1536]{1,0:T(8,128)(2,1)} %fusion.2.x_ref, ...), custom_call_target="tpu_custom_call" | custom-call | flops 1000000 | bytes 14680064 | tf_op jit(solution)/shard_map/rows_out/pallas_call | solution.py:1576
  655.5 2.3 copy.66
  662.2 1.7 slice_bitcast_fusion
  663.9 3.2 copy.69
  667.1 1.8 convert_bitcast_fusion
  (78 shorter events, 11.7 us)
Async XLA Ops:
  7.2 4.8 copy-start.3
  7.2 124.9 %all-gather.3.cloned.1.call-start = ((), (), s32[]{:S(2)}) async-start(), calls=%async_computation.4 | async-start | bytes 1474560 | tf_op jit(solution)/shard_map/all_gather | solution.py:1641
  7.9 627.7 %reduce-scatter.3.cloned.1.call-start = ((), (), s32[]{:S(2)}) async-start(), calls=%async_computation.2 | async-start | bytes 21233664 | tf_op jit(solution)/shard_map/reduce_scatter | solution.py:1693
  11.0 3.5 copy-start.2
  16.8 100.4 %copy-start.12 = (bf16[2,1536]{1,0:T(2,128)(2,1)S(1)}, bf16[2,1536]{1,0:T(2,128)(2,1)}, u32[]{:S(2)}) copy-start(bf16[2,1536]{1,0:T(2,128)(2,1)} %param.27) | copy-start | bytes 18436
  16.8 101.0 %copy-start.5 = (bf16[1,77,1536]{2,1,0:T(8,128)(2,1)S(1)}, bf16[1,77,1536]{2,1,0:T(8,128)(2,1)}, u32[]{:S(2)}) copy-start(bf16[1,77,1536]{2,1,0:T(8,128)(2,1)} %param.31) | copy-start | bytes 709636
  16.8 101.1 %copy-start.4 = (bf16[1,256,1536]{2,1,0:T(8,128)(2,1)S(1)}, bf16[1,256,1536]{2,1,0:T(8,128)(2,1)}, u32[]{:S(2)}) copy-start(bf16[1,256,1536]{2,1,0:T(8,128)(2,1)} %param.30) | copy-start | bytes 2359300
  376.2 0.9 copy-start.1
  376.3 290.9 %reduce-scatter.5.cloned.1.call-start = ((), (), s32[]{:S(2)}) async-start(), calls=%async_computation.3 | async-start | bytes 1474560 | tf_op jit(solution)/shard_map/reduce_scatter | solution.py:1748
  435.9 61.6 %copy-start.8 = (f32[2,1536]{1,0:T(2,128)S(1)}, f32[2,1536]{1,0:T(2,128)}, u32[]{:S(2)}) copy-start(f32[2,1536]{1,0:T(2,128)} %get-tuple-element.106) | copy-start | bytes 36868
  435.9 62.3 %copy-start.7 = (f32[4,1536]{1,0:T(4,128)S(1)}, f32[4,1536]{1,0:T(4,128)}, u32[]{:S(2)}) copy-start(f32[4,1536]{1,0:T(4,128)} %get-tuple-element.76) | copy-start | bytes 73732
  435.9 62.3 %copy-start.9 = (f32[2,1536]{1,0:T(2,128)S(1)}, f32[2,1536]{1,0:T(2,128)}, u32[]{:S(2)}) copy-start(f32[2,1536]{1,0:T(2,128)} %get-tuple-element.103) | copy-start | bytes 36868
  549.8 85.9 %copy-start.10 = (f32[8,1,256]{2,1,0:T(1,128)S(1)}, f32[8,1,256]{2,1,0:T(1,128)}, u32[]{:S(2)}) copy-start(f32[8,1,256]{2,1,0:T(1,128)} %get-tuple-element.115) | copy-start | bytes 24580
  648.2 12.6 %copy-start.11 = (f32[8,1,256]{2,1,0:T(1,128)S(1)}, f32[8,1,256]{2,1,0:T(1,128)}, u32[]{:S(2)}) copy-start(f32[8,1,256]{2,1,0:T(1,128)} %get-tuple-element.114) | copy-start | bytes 24580
  648.2 12.7 %copy-start.6 = (bf16[1,1536]{1,0:T(2,128)(2,1)S(1)}, bf16[1,1536]{1,0:T(2,128)(2,1)}, u32[]{:S(2)}) copy-start(bf16[1,1536]{1,0:T(2,128)(2,1)} %cond_ref.1) | copy-start | bytes 9220
  648.2 13.3 %copy-start = (bf16[768,1536]{1,0:T(8,128)(2,1)S(1)}, bf16[768,1536]{1,0:T(8,128)(2,1)}, u32[]{:S(2)}) copy-start(bf16[768,1536]{1,0:T(8,128)(2,1)} %reduce-scatter.3.cloned.1.call-done) | copy-start | bytes 7077892
Sparse Core Ops, SparseCore 0:
  9.6 44.3 all-gather.2
  376.4 130.5 reduce-scatter.2
  635.8 28.1 reduce-scatter.4

commit v5 on v4

--- a/solution.py
+++ b/solution.py
@@ -245,11 +245,6 @@
             pltpu.VMEM((2, half - 1, rows, width), HALF),
         ] + [pltpu.SemaphoreType.DMA((2, half)) for _ in range(5)]
 
-    @staticmethod
-    def scratch_inner(dp, rows, width):
-        full = GroupSum.scratch(dp, rows, width)
-        return full[:1] + full[2:8]
-
     def span(self, half, count):
         mask = 0
         for k in range(self.phases):
@@ -323,18 +318,11 @@
             for index in range(2**phase):
                 self.copy(half, phase, index).wait_recv()
 
-    def finish(self, out):
+    def finish(self, store):
         self.took(0)
         for half in range(2):
-            out[half] = self.value(half, 0, 0).astype(out.dtype)
+            store(half, self.value(half, 0, 0))
         self.sent(0)
-
-    def close(self, rest):
-        self.took(1)
-        for half in range(2):
-            for count in range(2):
-                rest[half, count] = self.value(half, count, 1).astype(rest.dtype)
-        self.sent(1)
 
     def sent(self, first):
         for half, count in self.every():
@@ -343,36 +331,6 @@
             for half in range(2):
                 for index in range(2**phase):
                     self.copy(half, phase, index).wait_send()
-
-
-class GroupLast:
-    def __init__(self, rest, came, send, recv):
-        self.rest, self.came, self.send, self.recv = rest, came, send, recv
-        masks = masks_of(lax.axis_size("dp"))
-        self.partners = [flip(lax.axis_index("dp"), mask) for mask in (masks[0], masks[-1])]
-
-    @staticmethod
-    def scratch(rows, width):
-        return [pltpu.VMEM((2, rows, width), HALF)] + [pltpu.SemaphoreType.DMA((2,))] * 2
-
-    def copy(self, half):
-        return pltpu.make_async_remote_copy(
-            src_ref=self.rest.at[half, 1],
-            dst_ref=self.came.at[half],
-            send_sem=self.send.at[half],
-            recv_sem=self.recv.at[half],
-            device_id={"dp": self.partners[half]},
-            device_id_type=MESH,
-        )
-
-    def begin(self):
-        for half in range(2):
-            self.copy(half).start()
-
-    def finish(self, store):
-        for half in range(2):
-            self.copy(half).wait()
-            store(half, self.rest[half, 0].astype(SINGLE) + self.came[half].astype(SINGLE))
 
 
 class LineGather:
@@ -775,20 +733,19 @@
     keys = k_ref[...].reshape(n * rows, LANES)
     values = v_ref[...].reshape(n * rows, LANES)
     first = halves(queries.shape)
-    outs, logs = [], []
-    for head in range(2):
-        own = first if head == 0 else jnp.logical_not(first)
-        scores = nt_dot(jnp.where(own, queries, HALF(0)), keys) + mask_ref[...]
-        maxima = jnp.max(scores, axis=-1, keepdims=True)
-        raised = jnp.exp(scores - maxima)
-        totals = jnp.sum(raised, axis=-1, keepdims=True)
-        weights = (raised * (1.0 / totals)).astype(HALF)
-        outs.append(nn_dot(weights, values))
-        logs.append(maxima + jnp.log(totals))
-    mixed = jnp.where(first, outs[0], outs[1]).astype(HALF)
+    zero = HALF(0)
+    pair_rows = jnp.concatenate([jnp.where(first, queries, zero), jnp.where(first, zero, queries)])
+    scores = nt_dot(pair_rows, keys) + mask_ref[...]
+    maxima = jnp.max(scores, axis=-1, keepdims=True)
+    raised = jnp.exp(scores - maxima)
+    totals = jnp.sum(raised, axis=-1, keepdims=True)
+    weights = (raised * (1.0 / totals)).astype(HALF)
+    outs = nn_dot(weights, values)
+    logs = maxima + jnp.log(totals)
+    mixed = jnp.where(first, outs[:rows], outs[rows:]).astype(HALF)
     o_ref[0] = mixed
     o_buf[pair, block] = mixed
-    lse_ref[0] = jnp.where(first, logs[0], logs[1])
+    lse_ref[0] = jnp.where(first, logs[:rows], logs[rows:])
     static_pairs = o_buf.shape[0]
 
     def columns(sender, which):
@@ -922,19 +879,25 @@
         keys, values = k_ref[0], v_ref[0]
         first = halves(keys.shape)
         mask = mask_ref[0][:, 0:1]
-        dks, dvs = [], []
-        for head in range(2):
-            own = first if head == 0 else jnp.logical_not(first)
-            key_own = jnp.where(own, keys, HALF(0))
-            scores = nt_dot(key_own, queries)
-            probs = jnp.exp((scores - lse_row[head : head + 1]) + mask)
-            grad_prob = nt_dot(jnp.where(own, values, HALF(0)), grads)
-            grad_score = (probs * (grad_prob - delta_row[head : head + 1])).astype(HALF)
-            dvs.append(nn_dot(probs.astype(HALF), grads))
-            dks.append(nn_dot(grad_score, queries))
-            acc_ref[...] += tn_dot(grad_score, key_own)
-        dk_ref[0] = jnp.where(first, dks[0], dks[1]).astype(HALF)
-        dv = jnp.where(first, dvs[0], dvs[1])
+        zero = HALF(0)
+
+        def pair(value):
+            return jnp.concatenate([jnp.where(first, value, zero), jnp.where(first, zero, value)])
+
+        def by_head(row):
+            return row[...].reshape(2, 1, total)
+
+        key_pair = pair(keys)
+        scores = nt_dot(key_pair, queries).reshape(2, rows, total)
+        probs = jnp.exp((scores - by_head(lse_row)) + mask)
+        grad_prob = nt_dot(pair(values), grads).reshape(2, rows, total)
+        grad_score = (probs * (grad_prob - by_head(delta_row))).astype(HALF)
+        grad_score = grad_score.reshape(2 * rows, total)
+        dvs = nn_dot(probs.astype(HALF).reshape(2 * rows, total), grads)
+        dks = nn_dot(grad_score, queries)
+        acc_ref[...] += tn_dot(grad_score, key_pair)
+        dk_ref[0] = jnp.where(first, dks[:rows], dks[rows:]).astype(HALF)
+        dv = jnp.where(first, dvs[:rows], dvs[rows:])
         dv_ref[0] = dv.astype(HALF)
         vb_ref[0, 0:1] += jnp.sum(dv[:img], axis=0, keepdims=True)
         vb_ref[0, 1:2] += jnp.sum(dv[img:], axis=0, keepdims=True)
@@ -1367,18 +1330,16 @@
 
 
 def attn_in_kernel(
-    n, img, dq_ref, dk_ref, dv_ref, x_ref, a_ref, w_ref, y_ref, prev_ref, p_ref,
-    da_ref, sum_ref, g_ref, y_sum, p_rest, turned, *scratch,
+    n, img, dq_ref, dk_ref, dv_ref, x_ref, a_ref, w_ref, y_ref, prev_ref,
+    da_ref, sum_ref, g_ref, y_sum, turned, *scratch,
 ):
     step = pl.program_id(0)
     count, rows, lw = dq_ref.shape
-    line = LineSum(n, at_rows(y_ref), y_sum, *scratch[:6], first=n - 2, prev=prev_ref)
-    group = GroupSum(p_ref, *scratch[6:])
+    line = LineSum(n, at_rows(y_ref), y_sum, *scratch, first=n - 2, prev=prev_ref)
     streams = ((0, slice(0, img)), (1, slice(img, rows)))
 
     def begin():
-        greet(n, "near", "paths")
-        group.begin()
+        greet(n, "near")
         line.round(n - 2)
         sum_ref[...] = jnp.zeros_like(sum_ref)
 
@@ -1408,17 +1369,10 @@
                     turned[:, :size] = a_ref[:, sl].reshape(size, a_ref.shape[2]).T
                 g_ref[...] = nn_dot(turned[:, :size], ref[:, sl].reshape(size, lw)).astype(HALF)
 
-    for number in range(group.phases - 1):
-        at_step(step, min(n + 5, 1 + 5 * number), functools.partial(group.step, number))
-
-    def finish():
-        line.finish()
-        group.close(p_rest)
-
-    at_step(step, n + 5, finish)
-
-
-def attn_in_back(n, img, dq, dk, dv, x_all, attn_in, weight, out_parts, running, proj):
+    at_step(step, n + 5, line.finish)
+
+
+def attn_in_back(n, img, dq, dk, dv, x_all, attn_in, weight, out_parts, running):
     _, rows, lw = dq.shape
     width = x_all.shape[2]
     anywhere = pl.BlockSpec(memory_space=pl.ANY)
@@ -1429,33 +1383,30 @@
         grid=(n + 6,),
         in_specs=[whole(dq.shape, True)] * 3
         + [row, whole(attn_in.shape, True), whole(weight.shape, True)]
-        + [anywhere] * 3,
+        + [anywhere] * 2,
         out_specs=[
             row,
             whole((2, 2, width)),
             pl.BlockSpec((width, lw), lambda k: (0, lax.max(k - n, 0))),
             whole((rows, width), True),
-            whole((2, 2) + proj.shape[2:], True),
         ],
         out_shape=[
             jax.ShapeDtypeStruct((n, rows, width), HALF),
             jax.ShapeDtypeStruct((2, 2, width), SINGLE),
             jax.ShapeDtypeStruct((width, 6 * lw), HALF),
             jax.ShapeDtypeStruct((rows, width), SINGLE),
-            jax.ShapeDtypeStruct((2, 2) + proj.shape[2:], HALF),
         ],
         scratch_shapes=[pltpu.VMEM((width, longest), HALF)]
-        + LineSum.scratch(n, rows, width, first=n - 2)
-        + GroupSum.scratch(proj.shape[0], *proj.shape[2:]),
+        + LineSum.scratch(n, rows, width, first=n - 2),
         compiler_params=remote(10, 62),
         cost_estimate=cost(12 * n * rows * width * lw, 30 * MEGA),
         name="attn_in_back",
-    )(dq, dk, dv, x_all, attn_in, weight, out_parts, running, proj)
+    )(dq, dk, dv, x_all, attn_in, weight, out_parts, running)
 
 
 def end_kernel(
-    n, dp, cut, parts, qkv_part, p_rest, packed, extra, ada_ref,
-    sum_ref, qkv_sum, p_own, every, cond_ref,
+    n, dp, cut, parts, qkv_part, p_ref, packed, extra, ada_ref, acts,
+    sum_ref, qkv_sum, p_own, every, cond_ref, ada_grad,
     z_got, row, c_part, c_got, c_all, z_send, z_recv, e_send, e_recv, c_send, c_recv, a_send, a_recv,
     *scratch,
 ):
@@ -1465,14 +1416,14 @@
     greet(n, "all", "all")
     line = LineSum(n, at_rows(parts), sum_ref, *scratch[:6])
     group = GroupSum(qkv_part, *scratch[6:15])
-    proj = GroupLast(p_rest, *scratch[15:])
+    proj = GroupSum(p_ref, *scratch[15:])
     mates, others = range(1, n), range(1, dp)
     z_go = [to_line(me, n, k, packed, z_got, z_send, z_recv) for k in mates]
     for copy in z_go:
         copy.start()
+    line.round(0)
+    proj.begin()
     group.begin()
-    proj.begin()
-    line.round(0)
     z_got[me] = packed[me]
     for copy in z_go:
         copy.wait_recv()
@@ -1482,12 +1433,13 @@
     for copy in e_go:
         copy.start()
     every[my] = row[...]
+    proj.step(0)
     group.step(0)
     for copy in e_go:
         copy.wait_recv()
     cols = cut // 2
-    product = nt_dot(every[:, 0, :cols].astype(HALF), ada_ref[:, 0, :])
-    product = product + nt_dot(every[:, 0, cols:cut].astype(HALF), ada_ref[:, 1, :])
+    halves_of = [every[:, 0, t * cols : (t + 1) * cols].astype(HALF) for t in range(2)]
+    product = nt_dot(halves_of[0], ada_ref[:, 0, :]) + nt_dot(halves_of[1], ada_ref[:, 1, :])
     c_part[...] = jnp.zeros_like(c_part)
     for k in range(dp):
         c_part[k, :, :depth] = product[k : k + 1]
@@ -1495,34 +1447,41 @@
     for copy in c_go:
         copy.start()
     c_got[my] = c_part[my]
-    a_go = [to_line(me, n, k, c_got, c_all, a_send, a_recv) for k in mates]
+    act_rows = acts[:, 0, :depth].astype(HALF)
+    for t in range(2):
+        ada_grad[:, t, :] = tn_dot(act_rows, halves_of[t])
     for hop in range(1, n - 1):
         line.round(hop)
-        if hop == 1:
-            for copy in c_go:
-                copy.wait_recv()
-            for copy in a_go:
-                copy.start()
-            c_all[me] = c_got[...]
-        if hop < group.phases:
-            group.step(hop)
-    for number in range(max(n - 1, 1), group.phases):
+    for number in range(1, group.phases):
+        proj.step(number)
         group.step(number)
+    for copy in c_go:
+        copy.wait_recv()
+    a_go = [to_line(me, n, k, c_got, c_all, a_send, a_recv) for k in mates]
+    for copy in a_go:
+        copy.start()
+    c_all[me] = c_got[...]
     for copy in a_go:
         copy.wait_recv()
     cond_ref[...] = jnp.sum(c_all[...], axis=0)
-    group.finish(qkv_sum)
-
-    def store(half, value):
+    rows, _, _, wide = qkv_sum.shape
+
+    def store_proj(half, value):
         p_own[half] = value.astype(HALF)
 
-    proj.finish(store)
+    def store_qkv(half, value):
+        own = slice(half * rows // 2, (half + 1) * rows // 2)
+        for k in range(6):
+            qkv_sum[own, k % 3, k // 3, :] = value[:, k * wide : (k + 1) * wide]
+
+    proj.finish(store_proj)
+    group.finish(store_qkv)
     line.finish()
     for copy in z_go + e_go + c_go + a_go:
         copy.wait_send()
 
 
-def end(n, dp, cut, parts, qkv_part, proj_rest, packed, extra, ada):
+def end(n, dp, cut, parts, qkv_part, proj_part, packed, extra, ada, acts):
     rows, width = parts.shape[1:]
     depth = up(ada.shape[0], LANES)
     span = packed.shape[2] + extra.shape[1]
@@ -1531,14 +1490,15 @@
     sems = [n - 1, n - 1, dp - 1, dp - 1, dp - 1, dp - 1, n - 1, n - 1]
     return pl.pallas_call(
         functools.partial(end_kernel, n, dp, cut),
-        in_specs=[anywhere, anywhere, inner, inner, inner, inner],
-        out_specs=[inner] * 5,
+        in_specs=[anywhere, anywhere, anywhere, inner, inner, inner, inner],
+        out_specs=[inner] * 6,
         out_shape=[
             jax.ShapeDtypeStruct((rows, width), SINGLE),
-            jax.ShapeDtypeStruct(qkv_part.shape[1:], SINGLE),
-            jax.ShapeDtypeStruct(proj_rest.shape[1:], HALF),
+            jax.ShapeDtypeStruct((ada.shape[0], 3, 2, qkv_part.shape[3] // 6), SINGLE),
+            jax.ShapeDtypeStruct(proj_part.shape[1:], HALF),
             jax.ShapeDtypeStruct((dp, 1, span), SINGLE),
             jax.ShapeDtypeStruct((dp, 1, depth), SINGLE),
+            jax.ShapeDtypeStruct(ada.shape, SINGLE),
         ],
         scratch_shapes=[
             pltpu.VMEM(packed.shape, SINGLE),
@@ -1550,11 +1510,11 @@
         + [pltpu.SemaphoreType.DMA((k,)) for k in sems]
         + LineSum.scratch(n, rows, width)
         + GroupSum.scratch(dp, *qkv_part.shape[2:])
-        + GroupLast.scratch(*proj_rest.shape[2:]),
-        compiler_params=remote(7, 60),
+        + GroupSum.scratch(dp, *proj_part.shape[2:]),
+        compiler_params=remote(7, 62),
         cost_estimate=cost(10**6, 100 * MEGA),
         name="end",
-    )(parts, qkv_part, proj_rest, packed, extra, ada)
+    )(parts, qkv_part, proj_part, packed, extra, ada, acts)
 
 
 def rows_kernel(img, slots, da_ref, dm_ref, x_ref, m_ref, y_ref, mod_ref, shift_ref, live_ref, io_ref, to_ref, ig_ref, tg_ref):
@@ -1654,7 +1614,6 @@
     )
     qkv_full = qkv_full.reshape(width, 6 * lwp)
     fc1_full = fc1_full.reshape(width, 2 * units)
-    act_slice = acts[:, 0, :depth].astype(HALF)
     proj_shift, fc2_shift = shifts[:2], shifts[2:]
     lengths_all = side_all[:, 0, cut + 4 * bias_cols]
 
@@ -1700,7 +1659,7 @@
     grad_q, grad_k, grad_v, q_bias_part, v_bias_part, proj_part, out_running = attend_back(
         n, dp, img, qkv_rows, mixture, grad_mix, lse, mask_col, mlp_out_part, grad_attn, mix_loc
     )
-    attn_in_part, mod_one, qkv_part, mlp_sum, proj_rest = attn_in_back(
+    attn_in_part, mod_one, qkv_part, mlp_sum = attn_in_back(
         n,
         img,
         grad_q,
@@ -1711,7 +1670,6 @@
         qkv_full,
         mlp_out_part,
         out_running,
-        proj_part.reshape(dp, 2, n * depth, lwp),
     )
     fc_own = fc_sum.astype(SINGLE)
 
@@ -1733,16 +1691,17 @@
     extra = jnp.concatenate(
         [jnp.stack([q_bias, v_bias], axis=1).reshape(-1), fc1_bias_part.reshape(-1)]
     )
-    grad_attn_in, qkv_sum, proj_own, every, cond_sum = end(
+    grad_attn_in, qkv_sum, proj_own, every, cond_sum, ada_grad = end(
         n,
         dp,
         cut,
         attn_in_part,
         qkv_part.reshape(dp, 2, depth // 2, 6 * lwp),
-        proj_rest,
+        proj_part.reshape(dp, 2, n * depth, lwp),
         packed[:, None],
         extra[None],
         ada_weight,
+        acts,
     )
     proj_own, fc_sum = lax.optimization_barrier((proj_own, fc_sum))
     proj_sum = lax.psum_scatter(
@@ -1755,8 +1714,6 @@
         img, slots, grad_attn_in, grad_middle, x_loc, middle, mlp_sum, mods, fc2_shift, live_loc
     )
 
-    mod_half = every[:, :cut].astype(HALF).reshape(dp, 2, mod_cols)
-    ada_grad = jnp.einsum("nd,ntc->dtc", act_slice, mod_half, preferred_element_type=SINGLE)
     ada_bias_grad = total[:cut].reshape(2, mod_cols)
     proj_bias_grad = total[cut : cut + 2 * bias_cols].reshape(2, bias_cols)
     fc2_bias_grad = total[cut + 2 * bias_cols : cut + 4 * bias_cols].reshape(2, bias_cols)
@@ -1765,7 +1722,7 @@
     fc1_bias_grad = total[after + 4 * lw :].reshape(2, units)
     cond_grad = cond_sum[:, 0, :depth].reshape(1, width) * silu_slope(cond_float)
 
-    qkv_grad = qkv_sum.reshape(depth, 2, 3, lwp)[..., :lw]
+    qkv_grad = qkv_sum[..., :lw].transpose(0, 2, 1, 3)
     fc1_grad = fc_own[:2].transpose(1, 0, 2)
     fc2_grad = fc_own[2:].transpose(2, 0, 1)
     proj_grad = proj_sum.astype(SINGLE)[..., :share].transpose(2, 0, 1)

time: 685 us -> 678 us (0.990)
  waiting for transfers between devices: 0.74 us -> 10.6 us
    pallas_call x1, Pallas kernels: 49.3 us -> 34.7 us  [attn_in_back(): pl.pallas_call(functools.partial(attn_in_kernel, n, img), grid=(n + 6,),...]
    reduce_scatter x1, waiting for transfers between devices: 0.01 us -> 9.87 us  [body(): lax.psum_scatter(proj_own.reshape(n * 2 * depth, lwp), 'seq', scatter_dim...]
    pallas_call x1, Pallas kernels: 50.2 us -> 59.5 us  [weight_grads(): pl.pallas_call(functools.partial(grads_kernel, n, img, plan, rounds), gri...]
    unnamed x33 -> x34, local copies, waits for them, and re-layouts: 14.2 us -> 11.5 us
  transfers between devices with their start and end apart: 3 -> 3, of which waited for: 0 -> 1; matrix products, arithmetic and copies ran while one was open for 6% -> 5% of each run, Pallas kernels for 55% -> 53%
where the time goes in v5:
time: 678 us; the launch traced here: 673 us
  Pallas kernels  608 us (90%)
  local copies, waits for them, and re-layouts  28.2 us (4%)
  between operations  14.9 us (2%)
  other arithmetic  11.3 us (2%)
  waiting for transfers between devices  10.6 us (2%)
    pallas_call x1, Pallas kernels, start(): pl.pallas_call(functools.partial(start_kernel, n, dp), in_specs=[inner] *...  97.5 us
    pallas_call x1, Pallas kernels, end(): pl.pallas_call(functools.partial(end_kernel, n, dp, cut), in_specs=[anywh...  89.8 us
    pallas_call x1, Pallas kernels, middle_rows(): pl.pallas_call(functools.partial(middle_kernel, n, img), in_specs=[inner]...  82.4 us
    pallas_call x1, Pallas kernels, feed_forward(): pl.pallas_call(functools.partial(mlp_kernel, n, img, tile), grid=(n,), in...  63.5 us
    pallas_call x1, Pallas kernels, weight_grads(): pl.pallas_call(functools.partial(grads_kernel, n, img, plan, rounds), gri...  59.5 us
    pallas_call x1, Pallas kernels, attend_back(): pl.pallas_call(functools.partial(attn_back_kernel, n, img, pairs), grid=(...  55.8 us
    pallas_call x1, Pallas kernels, middle_back(): pl.pallas_call(functools.partial(middle_back_kernel, n, img), in_specs=[a...  55.6 us
    pallas_call x1, Pallas kernels, attend(): pl.pallas_call(functools.partial(attn_kernel, n), grid=(pairs, n), in_spe...  48.7 us
  transfers between devices with their start and end apart: 3, of which 1 were waited for; matrix products, arithmetic and copies ran while one was open for 5% of the time, Pallas kernels for 53%

profile of v5, /device:TPU:0, one launch (start us, length us, event | category | flops | bytes accessed | tf_op | source)
XLA Modules:
  0.0 673.2 jit_solution(443970308810083144)
XLA Ops:
  8.0 0.8 fusion.13
  8.7 2.3 fusion.2.x_ref
  12.5 2.0 reshape_reshape.6.qkv_ref
  14.4 1.7 reshape_reshape.7.fc1_ref
  16.7 97.5 %start.1 = (bf16[4,336,1536]{2,1,0:T(8,128)(2,1)}, f32[4,1,6272]{2,1,0:T(1,128)}, f32[8,1,256]{2,1,0:T(1,128)}, f32[2,8,1536]{2,1,0:T(8,128)}, f32[4,1536]{1,0:T...) custom-call(bf16[336,1536]{1,0:T(8,128)(2,1)} %fusion.2.x_ref, bf16[1,1536]{1,0:T(2,128)(2,1)} %cond_ref.1, ...), custom_call_target="tpu_custom_call" | custom-call | flops 1000000 | bytes 104857600 | tf_op jit(solution)/shard_map/start/pallas_call | solution.py:641
  114.3 0.8 slice_reduce_fusion.1
  115.9 1.3 slice.100.b_ref
  117.9 1.0 fusion.3.e_ref.e_loc
  118.9 13.2 %project_qkv.1 = (bf16[4,336,1536]{2,1,0:T(8,128)(2,1)}, bf16[4,336,1152]{2,1,0:T(8,128)(2,1)}) custom-call(bf16[4,336,1536]{2,1,0:T(8,128)(2,1)} %get-tuple-element.68.x_ref, f32[2,8,1536]{2,1,0:T(8,128)} %get-tuple-element.69.mod_ref, bf16[1536,2304]{1,0:T(8,128)(2,1)} %bitcast.76, f32[2,1152]{1,0:T(2,128)} %bitcast.72), custom_call_target="tpu_custom_call" | custom-call | flops 4756340736 | bytes 31457280 | tf_op jit(solution)/shard_map/project_qkv/pallas_call | solution.py:689
  132.1 48.7 %attend.1 = (bf16[4,336,384]{2,1,0:T(8,128)(2,1)}, f32[4,336,384]{2,1,0:T(8,128)}, bf16[2,336,1536]{2,1,0:T(8,128)(2,1)}, bf16[336,1536]{1,0:T(8,128)(2,1)}, bf16[8,2,768,384]{3,2,1,0:T(8,128)(2,1)}) custom-call(bf16[4,336,1152]{2,1,0:T(8,128)(2,1)} %get-tuple-element.71.q_ref.k_ref.v_ref, bf16[4,336,1152]{2,1,0:T(8,128)(2,1)} %get-tuple-element.71.q_ref.k_ref.v_ref, ...), custom_call_target="tpu_custom_call" | custom-call | flops 11098128384 | bytes 20971520 | tf_op jit(solution)/shard_map/attend/pallas_call | solution.py:799
  180.8 82.4 %middle_rows.1 = (f32[336,1536]{1,0:T(8,128)}, f32[336,1536]{1,0:T(8,128)}, bf16[4,336,1536]{2,1,0:T(8,128)(2,1)}, bf16[8,2,192,1536]{3,2,1,0:T(8,128)(2,1)}) custom-call(bf16[336,1536]{1,0:T(8,128)(2,1)} %get-tuple-element.74.mix_ref.r_ref, bf16[336,1536]{1,0:T(8,128)(2,1)} %fusion.2.x_ref, bf16[8,4,2,192,384]{4,3,2,1,0:T(8,128)(2,1)} %bitcast.56, ...), custom_call_target="tpu_custom_call" | custom-call | flops 1585446912 | bytes 104857600 | tf_op jit(solution)/shard_map/middle_rows/pallas_call | solution.py:1023
  263.2 63.5 %feed_forward.1 = (bf16[4,336,1536]{2,1,0:T(8,128)(2,1)}, bf16[4,336,1536]{2,1,0:T(8,128)(2,1)}, bf16[4,336,1536]{2,1,0:T(8,128)(2,1)}, bf16[4,336,1536]{2,1,0:T...) custom-call(bf16[4,336,1536]{2,1,0:T(8,128)(2,1)} %get-tuple-element.77.b_ref.refs_0_, ...), custom_call_target="tpu_custom_call" | custom-call | flops 19025362944 | bytes 52428800 | tf_op jit(solution)/shard_map/feed_forward/pallas_call | solution.py:1131
  326.7 59.5 %fc_grads.1 = (bf16[8,4,192,1536]{3,2,1,0:T(8,128)(2,1)}, bf16[2,336,1536]{2,1,0:T(8,128)(2,1)}) custom-call(bf16[4,336,1536]{2,1,0:T(8,128)(2,1)} %get-tuple-element.77.b_ref.refs_0_, bf16[4,336,1536]{2,1,0:T(8,128)(2,1)} %get-tuple-element.82.refs_1_, bf16[4,336,1536]{2,1,0:T(8,128)(2,1)} %get-tuple-element.83.refs_2_, ...), custom_call_target="tpu_custom_call" | custom-call | flops 12683575296 | bytes 62914560 | tf_op jit(solution)/shard_map/fc_grads/pallas_call | solution.py:1223
  386.4 0.8 copy-done.3
  387.3 55.6 %middle_back.1 = (f32[336,1536]{1,0:T(8,128)}, bf16[336,1536]{1,0:T(8,128)(2,1)}, f32[2,8,1536]{2,1,0:T(8,128)}, bf16[4,336,384]{2,1,0:T(8,128)(2,1)}) custom-call(bf16[4,336,1536]{2,1,0:T(8,128)(2,1)} %get-tuple-element.81.refs_4_.part_ref, bf16[2,336,1536]{2,1,0:T(8,128)(2,1)} %get-tuple-element.85.prev_ref, f32[336,1536]{1,0:T(8,128)} %get-tuple-element.86.m_ref, ...), custom_call_target="tpu_custom_call" | custom-call | flops 1585446912 | bytes 62914560 | tf_op jit(solution)/shard_map/middle_back/pallas_call | solution.py:1308
  442.9 1.0 copy.55
  443.9 0.9 slice.101
  444.8 1.1 broadcast_in_dim.39.mask_ref
  445.9 55.8 %attend_back.1 = (bf16[4,336,384]{2,1,0:T(8,128)(2,1)}, bf16[4,336,384]{2,1,0:T(8,128)(2,1)}, bf16[4,336,384]{2,1,0:T(8,128)(2,1)}, f32[3,2,128]{2,1,0:T(2,128)}...) custom-call(bf16[4,336,1152]{2,1,0:T(8,128)(2,1)} %get-tuple-element.71.q_ref.k_ref.v_ref, ...), custom_call_target="tpu_custom_call" | custom-call | flops 27745320960 | bytes 31457280 | tf_op jit(solution)/shard_map/attend_back/pallas_call | solution.py:941
  503.7 34.7 %attn_in_back.1 = (bf16[4,336,1536]{2,1,0:T(8,128)(2,1)}, f32[2,2,1536]{2,1,0:T(2,128)}, bf16[1536,2304]{1,0:T(8,128)(2,1)}, f32[336,1536]{1,0:T(8,128)}) custom-call(bf16[4,336,384]{2,1,0:T(8,128)(2,1)} %get-tuple-element.92.dq_ref, bf16[4,336,384]{2,1,0:T(8,128)(2,1)} %get-tuple-element.93.dk_ref, bf16[4,336,384]{2,1,0:T(8,128)(2,1)} %get-tuple-element.94.dv_ref, ...), custom_call_target="tpu_custom_call" | custom-call | flops 9512681472 | bytes 31457280 | tf_op jit(solution)/shard_map/attn_in_back/pallas_call | solution.py:1381
  538.4 0.8 pad_maximum_fusion
  540.1 89.8 %end.1 = (f32[336,1536]{1,0:T(8,128)}, f32[192,3,2,384]{3,2,1,0:T(2,128)}, bf16[2,768,384]{2,1,0:T(8,128)(2,1)}, f32[8,1,10752]{2,1,0:T(1,128)}, f32[8,1,256]{2,1,0:T(1,128)}, /*index=5*/f32[192,2,2304]{2,1,0:T(2,128)}) custom-call(bf16[4,336,1536]{2,1,0:T(8,128)(2,1)} %get-tuple-element.97.parts, bf16[8,2,96,2304]{3,2,1,0:T(8,128)(2,1)} %bitcast.60, ...), custom_call_target="tpu_custom_call" | custom-call | flops 1000000 | bytes 104857600 | tf_op jit(solution)/shard_map/end/pallas_call | solution.py:1491
  630.6 1.2 reduce_sum.9
  631.9 7.2 %rows_out.1 = (bf16[1,256,1536]{2,1,0:T(8,128)(2,1)}, bf16[1,77,1536]{2,1,0:T(8,128)(2,1)}, f32[1,256,1536]{2,1,0:T(8,128)}, f32[1,77,1536]{2,1,0:T(8,128)}) custom-call(f32[336,1536]{1,0:T(8,128)} %get-tuple-element.107.da_ref, f32[336,1536]{1,0:T(8,128)} %get-tuple-element.108.dm_ref, bf16[336,1536]{1,0:T(8,128)(2,1)} %fusion.2.x_ref, ...), custom_call_target="tpu_custom_call" | custom-call | flops 1000000 | bytes 14680064 | tf_op jit(solution)/shard_map/rows_out/pallas_call | solution.py:1536
  639.1 2.3 copy.60
  645.8 1.7 slice_bitcast_fusion
  647.5 3.2 copy.61
  650.8 9.9 %reduce-scatter.5.cloned.1.call-done = bf16[384,384]{1,0:T(8,128)(2,1)} async-done(((bf16[1536,384]{1,0:T(8,128)(2,1)}), bf16[384,384]{1,0:T(8,128)(2,1)}) %reduce-scatter.5.cloned.1.call-update) | async-done | bytes 294928 | tf_op jit(solution)/shard_map/reduce_scatter | solution.py:1707
  660.6 1.8 convert_bitcast_fusion
  662.5 1.8 copy.66
  664.3 0.9 copy-done.2
  665.2 1.2 copy.67
  (75 shorter events, 11.7 us)
Async XLA Ops:
  7.2 4.7 copy-start.5
  7.2 124.9 %all-gather.3.cloned.1.call-start = ((), (), s32[]{:S(2)}) async-start(), calls=%async_computation.4 | async-start | bytes 1474560 | tf_op jit(solution)/shard_map/all_gather | solution.py:1601
  7.9 622.0 %reduce-scatter.3.cloned.1.call-start = ((), (), s32[]{:S(2)}) async-start(), calls=%async_computation.2 | async-start | bytes 21233664 | tf_op jit(solution)/shard_map/reduce_scatter | solution.py:1652
  11.9 2.6 copy-start.4
  16.7 100.5 %copy-start.13 = (bf16[2,1536]{1,0:T(2,128)(2,1)S(1)}, bf16[2,1536]{1,0:T(2,128)(2,1)}, u32[]{:S(2)}) copy-start(bf16[2,1536]{1,0:T(2,128)(2,1)} %param.27) | copy-start | bytes 18436
  16.7 101.1 %copy-start.7 = (bf16[1,77,1536]{2,1,0:T(8,128)(2,1)S(1)}, bf16[1,77,1536]{2,1,0:T(8,128)(2,1)}, u32[]{:S(2)}) copy-start(bf16[1,77,1536]{2,1,0:T(8,128)(2,1)} %param.31) | copy-start | bytes 709636
  16.7 101.2 %copy-start.6 = (bf16[1,256,1536]{2,1,0:T(8,128)(2,1)S(1)}, bf16[1,256,1536]{2,1,0:T(8,128)(2,1)}, u32[]{:S(2)}) copy-start(bf16[1,256,1536]{2,1,0:T(8,128)(2,1)} %param.30) | copy-start | bytes 2359300
  386.3 0.9 copy-start.3
  386.3 274.3 %reduce-scatter.5.cloned.1.call-start = ((), (), s32[]{:S(2)}) async-start(), calls=%async_computation.3 | async-start | bytes 1474560 | tf_op jit(solution)/shard_map/reduce_scatter | solution.py:1707
  445.9 56.6 %copy-start.10 = (f32[2,1536]{1,0:T(2,128)S(1)}, f32[2,1536]{1,0:T(2,128)}, u32[]{:S(2)}) copy-start(f32[2,1536]{1,0:T(2,128)} %get-tuple-element.105) | copy-start | bytes 36868
  445.9 57.2 %copy-start.9 = (f32[4,1536]{1,0:T(4,128)S(1)}, f32[4,1536]{1,0:T(4,128)}, u32[]{:S(2)}) copy-start(f32[4,1536]{1,0:T(4,128)} %get-tuple-element.76) | copy-start | bytes 73732
  445.9 57.2 %copy-start.11 = (f32[2,1536]{1,0:T(2,128)S(1)}, f32[2,1536]{1,0:T(2,128)}, u32[]{:S(2)}) copy-start(f32[2,1536]{1,0:T(2,128)} %get-tuple-element.102) | copy-start | bytes 36868
  631.9 12.5 %copy-start.12 = (f32[8,1,256]{2,1,0:T(1,128)S(1)}, f32[8,1,256]{2,1,0:T(1,128)}, u32[]{:S(2)}) copy-start(f32[8,1,256]{2,1,0:T(1,128)} %get-tuple-element.114) | copy-start | bytes 24580
  631.9 12.7 %copy-start.8 = (bf16[1,1536]{1,0:T(2,128)(2,1)S(1)}, bf16[1,1536]{1,0:T(2,128)(2,1)}, u32[]{:S(2)}) copy-start(bf16[1,1536]{1,0:T(2,128)(2,1)} %cond_ref.1) | copy-start | bytes 9220
  631.9 13.3 %copy-start.1 = (bf16[768,1536]{1,0:T(8,128)(2,1)S(1)}, bf16[768,1536]{1,0:T(8,128)(2,1)}, u32[]{:S(2)}) copy-start(bf16[768,1536]{1,0:T(8,128)(2,1)} %reduce-scatter.3.cloned.1.call-done) | copy-start | bytes 7077892
  647.5 14.9 %copy-start = (f32[192,2,2304]{2,1,0:T(2,128)S(1)}, f32[192,2,2304]{2,1,0:T(2,128)}, u32[]{:S(2)}) copy-start(f32[192,2,2304]{2,1,0:T(2,128)} %get-tuple-element.213) | copy-start | bytes 10616836
  662.5 2.8 copy-start.2
Sparse Core Ops, SparseCore 0:
  9.6 44.4 all-gather.2
  386.4 129.5 reduce-scatter.2
  630.0 30.5 reduce-scatter.4

commit v6 on v5

--- a/solution.py
+++ b/solution.py
@@ -1046,14 +1046,27 @@
     return me + lax.select(count <= 2 * low, near, far)
 
 
-def mlp_kernel(n, img, tile, b_ref, e_loc, e_near, mod_ref, w1_ref, b1_ref, w2_ref,
-    g_ref, dz_ref, dy_ref, db_ref, y_ref, sum_ref, gate_ref, acc_ref, out_ref, e_all, near_sem, *sems):
+def mlp_kernel(n, img, tile, b_ref, e_loc, e_near, mod_ref, w1_far, b1_ref, w2_far,
+    g_ref, dz_ref, dy_ref, db_ref, y_ref, sum_ref, gate_ref, acc_ref, out_ref, e_all, near_sem,
+    w1_ref, w2_ref, w_sem, *sems):
     step = pl.program_id(0)
     me = lax.axis_index("seq")
     owner = by_distance(me, n, step)
     e_ref = e_all.at[pl.ds(owner, 1)]
     gather = LineGather(n, e_near, e_all, *sems, first=1)
     own = pltpu.make_async_copy(e_loc, e_all.at[me], near_sem.at[2])
+    wide = g_ref.shape[2]
+
+    def weights(t):
+        cols = pl.ds(t * wide, wide)
+        return (
+            pltpu.make_async_copy(w1_far.at[:, cols], w1_ref.at[:, cols], w_sem.at[t, 0]),
+            pltpu.make_async_copy(w2_far.at[:, t], w2_ref.at[:, t], w_sem.at[t, 1]),
+        )
+
+    def weights_in(t):
+        for copy in weights(t):
+            copy.wait()
 
     def nears(action):
         for way, sign in ((0, 1), (1, -1)):
@@ -1070,6 +1083,9 @@
         gather.begin()
         own.start()
         nears(lambda copy: copy.start())
+        for t in range(2):
+            for copy in weights(t):
+                copy.start()
         own.wait()
         nears(lambda copy: copy.wait())
 
@@ -1085,6 +1101,7 @@
         gate_ref[...] = jnp.zeros_like(gate_ref)
 
     for t, sl in ((0, slice(0, img)), (1, slice(img, b_ref.shape[1]))):
+        at_step(step, 0, functools.partial(weights_in, t))
         rows = b_ref[0, sl]
         grad = (mod_ref[t, 5:6] * e_ref[0, sl].astype(SINGLE)).astype(HALF)
         dy_ref[0, sl] = grad
@@ -1136,9 +1153,9 @@
             pl.BlockSpec(memory_space=pl.ANY),
             pl.BlockSpec(memory_space=pl.ANY),
             whole(mods.shape),
-            whole(w1.shape, True),
+            pl.BlockSpec(memory_space=pl.ANY),
             whole(b1.shape),
-            whole(w2.shape, True),
+            pl.BlockSpec(memory_space=pl.ANY),
         ],
         out_specs=[
             owned(units),
@@ -1163,6 +1180,9 @@
             pltpu.VMEM((rows, width), SINGLE),
             pltpu.VMEM((n, rows, width), HALF),
             pltpu.SemaphoreType.DMA((3,)),
+            pltpu.VMEM(w1.shape, HALF),
+            pltpu.VMEM(w2.shape, HALF),
+            pltpu.SemaphoreType.DMA((2, 2)),
         ]
         + LineGather.scratch(n),
         compiler_params=remote(9, 60),
@@ -1174,20 +1194,26 @@
 def grads_kernel(n, img, plan, rounds, *refs):
     lefts = max(p[0] for p in plan) + 1
     rights = max(p[1] for p in plan) + 1
-    l_refs, r_refs = refs[:lefts], refs[lefts : lefts + rights]
-    rest = refs[lefts + rights :]
+    count = lefts + rights
+    far, rest = refs[:count], refs[count:]
+    held, loaded, rest = rest[-count - 1 : -1], rest[-1], rest[: -count - 1]
+    l_refs, r_refs = held[:lefts], held[lefts:]
+    copies = [pltpu.make_async_copy(far[k], held[k], loaded.at[k]) for k in range(count)]
     step = pl.program_id(0)
-    if rounds:
-        parts, o_ref, tail, turned = rest[:4]
-        line = LineSum(n, at_rows(parts), None, *rest[4:], stop=n - 2, tail=tail)
-
-        def begin():
-            greet(n, "near")
-            line.round(0)
-
-        at_step(step, 0, begin)
-    else:
-        o_ref, turned = rest
+    parts, o_ref, tail, turned = rest[:4]
+    line = LineSum(n, at_rows(parts), None, *rest[4:], stop=n - 2, tail=tail)
+
+    def begin():
+        greet(n, "near")
+        line.round(0)
+        for left, right, stream in plan:
+            if stream == 0:
+                copies[left].start()
+                copies[lefts + right].start()
+
+    at_step(step, 0, begin)
+    for hop, when in enumerate(rounds):
+        at_step(step, when, functools.partial(line.round, hop + 1))
     tile = 512 if o_ref.shape[3] % 512 == 0 else 2 * LANES
     before = None
     for k, (left, right, stream) in enumerate(plan):
@@ -1195,6 +1221,9 @@
         @pl.when(step == k)
         def _():
             l_ref, r_ref = l_refs[left], r_refs[right]
+            if stream == 0:
+                copies[left].wait()
+                copies[lefts + right].wait()
             count, rows, _ = l_ref.shape
             sl = slice(0, img) if stream == 0 else slice(img, rows)
             size = count * (sl.stop - sl.start)
@@ -1208,10 +1237,7 @@
                 )
 
         before = (left, stream)
-    if rounds:
-        for hop, when in enumerate(rounds):
-            at_step(step, when, functools.partial(line.round, hop + 1))
-        at_step(step, len(plan) - 1, line.close)
+    at_step(step, len(plan) - 1, line.close)
 
 
 def weight_grads(n, dp, img, lefts, rights, plan, rounds, parts, collective, name):
@@ -1223,14 +1249,16 @@
     return pl.pallas_call(
         functools.partial(grads_kernel, n, img, plan, rounds),
         grid=(len(plan),),
-        in_specs=[whole(a.shape, True) for a in (*lefts, *rights)] + [anywhere],
+        in_specs=[anywhere] * (len(lefts) + len(rights) + 1),
         out_specs=[pl.BlockSpec(block, lambda k: (0, k, 0, 0)), anywhere],
         out_shape=[
             jax.ShapeDtypeStruct((dp, len(plan), depth // dp, wide), HALF),
             jax.ShapeDtypeStruct((2,) + parts.shape[1:], HALF),
         ],
         scratch_shapes=[pltpu.VMEM((depth, longest), HALF)]
-        + LineSum.scratch(n, *parts.shape[1:], stop=n - 2),
+        + LineSum.scratch(n, *parts.shape[1:], stop=n - 2)
+        + [pltpu.VMEM(a.shape, HALF) for a in (*lefts, *rights)]
+        + [pltpu.SemaphoreType.DMA((len(lefts) + len(rights),))],
         compiler_params=remote(collective, 60),
         cost_estimate=cost(2 * n * rows * depth * len(plan) * wide // 2, 60 * MEGA),
         name=name,

time: 678 us -> 675 us (level)
  transfers between devices with their start and end apart: 3 -> 3, of which waited for: 1 -> 1; matrix products, arithmetic and copies ran while one was open for 5% -> 5% of each run, Pallas kernels for 53% -> 54%
where the time goes in v6:
time: 675 us; the launch traced here: 670 us
  Pallas kernels  605 us (90%)
  local copies, waits for them, and re-layouts  28.2 us (4%)
  between operations  14.9 us (2%)
  other arithmetic  11.3 us (2%)
  waiting for transfers between devices  10.6 us (2%)
    pallas_call x1, Pallas kernels, start(): pl.pallas_call(functools.partial(start_kernel, n, dp), in_specs=[inner] *...  97.5 us
    pallas_call x1, Pallas kernels, end(): pl.pallas_call(functools.partial(end_kernel, n, dp, cut), in_specs=[anywh...  94.7 us
    pallas_call x1, Pallas kernels, middle_rows(): pl.pallas_call(functools.partial(middle_kernel, n, img), in_specs=[inner]...  82.4 us
    pallas_call x1, Pallas kernels, feed_forward(): pl.pallas_call(functools.partial(mlp_kernel, n, img, tile), grid=(n,), in...  61.7 us
    pallas_call x1, Pallas kernels, middle_back(): pl.pallas_call(functools.partial(middle_back_kernel, n, img), in_specs=[a...  55.6 us
    pallas_call x1, Pallas kernels, attend_back(): pl.pallas_call(functools.partial(attn_back_kernel, n, img, pairs), grid=(...  55.2 us
    pallas_call x1, Pallas kernels, weight_grads(): pl.pallas_call(functools.partial(grads_kernel, n, img, plan, rounds), gri...  53.2 us
    pallas_call x1, Pallas kernels, attend(): pl.pallas_call(functools.partial(attn_kernel, n), grid=(pairs, n), in_spe...  48.7 us
  transfers between devices with their start and end apart: 3, of which 1 were waited for; matrix products, arithmetic and copies ran while one was open for 5% of the time, Pallas kernels for 54%

profile of v6, /device:TPU:0, one launch (start us, length us, event | category | flops | bytes accessed | tf_op | source)
XLA Modules:
  0.0 670.1 jit_solution(17960868705960523868)
XLA Ops:
  8.0 0.8 fusion.13
  8.7 2.3 fusion.2.x_ref
  12.5 2.0 reshape_reshape.6.qkv_ref
  14.4 1.7 reshape_reshape.7.fc1_ref
  16.7 97.5 %start.1 = (bf16[4,336,1536]{2,1,0:T(8,128)(2,1)}, f32[4,1,6272]{2,1,0:T(1,128)}, f32[8,1,256]{2,1,0:T(1,128)}, f32[2,8,1536]{2,1,0:T(8,128)}, f32[4,1536]{1,0:T...) custom-call(bf16[336,1536]{1,0:T(8,128)(2,1)} %fusion.2.x_ref, bf16[1,1536]{1,0:T(2,128)(2,1)} %cond_ref.1, ...), custom_call_target="tpu_custom_call" | custom-call | flops 1000000 | bytes 104857600 | tf_op jit(solution)/shard_map/start/pallas_call | solution.py:641
  114.3 0.8 slice_reduce_fusion.1
  115.9 1.3 slice.100.b_ref
  117.9 1.0 fusion.3.e_ref.e_loc
  118.9 13.2 %project_qkv.1 = (bf16[4,336,1536]{2,1,0:T(8,128)(2,1)}, bf16[4,336,1152]{2,1,0:T(8,128)(2,1)}) custom-call(bf16[4,336,1536]{2,1,0:T(8,128)(2,1)} %get-tuple-element.68.x_ref, f32[2,8,1536]{2,1,0:T(8,128)} %get-tuple-element.69.mod_ref, bf16[1536,2304]{1,0:T(8,128)(2,1)} %bitcast.76, f32[2,1152]{1,0:T(2,128)} %bitcast.72), custom_call_target="tpu_custom_call" | custom-call | flops 4756340736 | bytes 31457280 | tf_op jit(solution)/shard_map/project_qkv/pallas_call | solution.py:689
  132.1 48.7 %attend.1 = (bf16[4,336,384]{2,1,0:T(8,128)(2,1)}, f32[4,336,384]{2,1,0:T(8,128)}, bf16[2,336,1536]{2,1,0:T(8,128)(2,1)}, bf16[336,1536]{1,0:T(8,128)(2,1)}, bf16[8,2,768,384]{3,2,1,0:T(8,128)(2,1)}) custom-call(bf16[4,336,1152]{2,1,0:T(8,128)(2,1)} %get-tuple-element.71.q_ref.k_ref.v_ref, bf16[4,336,1152]{2,1,0:T(8,128)(2,1)} %get-tuple-element.71.q_ref.k_ref.v_ref, ...), custom_call_target="tpu_custom_call" | custom-call | flops 11098128384 | bytes 20971520 | tf_op jit(solution)/shard_map/attend/pallas_call | solution.py:799
  180.8 82.4 %middle_rows.1 = (f32[336,1536]{1,0:T(8,128)}, f32[336,1536]{1,0:T(8,128)}, bf16[4,336,1536]{2,1,0:T(8,128)(2,1)}, bf16[8,2,192,1536]{3,2,1,0:T(8,128)(2,1)}) custom-call(bf16[336,1536]{1,0:T(8,128)(2,1)} %get-tuple-element.74.mix_ref.r_ref, bf16[336,1536]{1,0:T(8,128)(2,1)} %fusion.2.x_ref, bf16[8,4,2,192,384]{4,3,2,1,0:T(8,128)(2,1)} %bitcast.56, ...), custom_call_target="tpu_custom_call" | custom-call | flops 1585446912 | bytes 104857600 | tf_op jit(solution)/shard_map/middle_rows/pallas_call | solution.py:1023
  263.2 61.7 %feed_forward.1 = (bf16[4,336,1536]{2,1,0:T(8,128)(2,1)}, bf16[4,336,1536]{2,1,0:T(8,128)(2,1)}, bf16[4,336,1536]{2,1,0:T(8,128)(2,1)}, bf16[4,336,1536]{2,1,0:T...) custom-call(bf16[4,336,1536]{2,1,0:T(8,128)(2,1)} %get-tuple-element.77.b_ref.refs_0_, ...), custom_call_target="tpu_custom_call" | custom-call | flops 19025362944 | bytes 52428800 | tf_op jit(solution)/shard_map/feed_forward/pallas_call | solution.py:1148
  324.9 53.2 %fc_grads.1 = (bf16[8,4,192,1536]{3,2,1,0:T(8,128)(2,1)}, bf16[2,336,1536]{2,1,0:T(8,128)(2,1)}) custom-call(bf16[4,336,1536]{2,1,0:T(8,128)(2,1)} %get-tuple-element.77.b_ref.refs_0_, bf16[4,336,1536]{2,1,0:T(8,128)(2,1)} %get-tuple-element.82.refs_1_, bf16[4,336,1536]{2,1,0:T(8,128)(2,1)} %get-tuple-element.83.refs_2_, ...), custom_call_target="tpu_custom_call" | custom-call | flops 12683575296 | bytes 62914560 | tf_op jit(solution)/shard_map/fc_grads/pallas_call | solution.py:1249
  378.2 0.8 copy-done.3
  379.1 55.6 %middle_back.1 = (f32[336,1536]{1,0:T(8,128)}, bf16[336,1536]{1,0:T(8,128)(2,1)}, f32[2,8,1536]{2,1,0:T(8,128)}, bf16[4,336,384]{2,1,0:T(8,128)(2,1)}) custom-call(bf16[4,336,1536]{2,1,0:T(8,128)(2,1)} %get-tuple-element.81.refs_4_.part_ref, bf16[2,336,1536]{2,1,0:T(8,128)(2,1)} %get-tuple-element.85.prev_ref, f32[336,1536]{1,0:T(8,128)} %get-tuple-element.86.m_ref, ...), custom_call_target="tpu_custom_call" | custom-call | flops 1585446912 | bytes 62914560 | tf_op jit(solution)/shard_map/middle_back/pallas_call | solution.py:1336
  434.6 1.0 copy.55
  435.6 0.9 slice.101
  436.5 1.1 broadcast_in_dim.39.mask_ref
  437.6 55.2 %attend_back.1 = (bf16[4,336,384]{2,1,0:T(8,128)(2,1)}, bf16[4,336,384]{2,1,0:T(8,128)(2,1)}, bf16[4,336,384]{2,1,0:T(8,128)(2,1)}, f32[3,2,128]{2,1,0:T(2,128)}...) custom-call(bf16[4,336,1152]{2,1,0:T(8,128)(2,1)} %get-tuple-element.71.q_ref.k_ref.v_ref, ...), custom_call_target="tpu_custom_call" | custom-call | flops 27745320960 | bytes 31457280 | tf_op jit(solution)/shard_map/attend_back/pallas_call | solution.py:941
  494.8 35.6 %attn_in_back.1 = (bf16[4,336,1536]{2,1,0:T(8,128)(2,1)}, f32[2,2,1536]{2,1,0:T(2,128)}, bf16[1536,2304]{1,0:T(8,128)(2,1)}, f32[336,1536]{1,0:T(8,128)}) custom-call(bf16[4,336,384]{2,1,0:T(8,128)(2,1)} %get-tuple-element.92.dq_ref, bf16[4,336,384]{2,1,0:T(8,128)(2,1)} %get-tuple-element.93.dk_ref, bf16[4,336,384]{2,1,0:T(8,128)(2,1)} %get-tuple-element.94.dv_ref, ...), custom_call_target="tpu_custom_call" | custom-call | flops 9512681472 | bytes 31457280 | tf_op jit(solution)/shard_map/attn_in_back/pallas_call | solution.py:1409
  530.4 0.8 pad_maximum_fusion
  532.1 94.7 %end.1 = (f32[336,1536]{1,0:T(8,128)}, f32[192,3,2,384]{3,2,1,0:T(2,128)}, bf16[2,768,384]{2,1,0:T(8,128)(2,1)}, f32[8,1,10752]{2,1,0:T(1,128)}, f32[8,1,256]{2,1,0:T(1,128)}, /*index=5*/f32[192,2,2304]{2,1,0:T(2,128)}) custom-call(bf16[4,336,1536]{2,1,0:T(8,128)(2,1)} %get-tuple-element.97.parts, bf16[8,2,96,2304]{3,2,1,0:T(8,128)(2,1)} %bitcast.60, ...), custom_call_target="tpu_custom_call" | custom-call | flops 1000000 | bytes 104857600 | tf_op jit(solution)/shard_map/end/pallas_call | solution.py:1519
  627.6 1.2 reduce_sum.9
  628.9 7.2 %rows_out.1 = (bf16[1,256,1536]{2,1,0:T(8,128)(2,1)}, bf16[1,77,1536]{2,1,0:T(8,128)(2,1)}, f32[1,256,1536]{2,1,0:T(8,128)}, f32[1,77,1536]{2,1,0:T(8,128)}) custom-call(f32[336,1536]{1,0:T(8,128)} %get-tuple-element.107.da_ref, f32[336,1536]{1,0:T(8,128)} %get-tuple-element.108.dm_ref, bf16[336,1536]{1,0:T(8,128)(2,1)} %fusion.2.x_ref, ...), custom_call_target="tpu_custom_call" | custom-call | flops 1000000 | bytes 14680064 | tf_op jit(solution)/shard_map/rows_out/pallas_call | solution.py:1564
  636.1 2.3 copy.60
  642.8 1.7 slice_bitcast_fusion
  644.5 3.2 copy.61
  647.7 9.9 %reduce-scatter.5.cloned.1.call-done = bf16[384,384]{1,0:T(8,128)(2,1)} async-done(((bf16[1536,384]{1,0:T(8,128)(2,1)}), bf16[384,384]{1,0:T(8,128)(2,1)}) %reduce-scatter.5.cloned.1.call-update) | async-done | bytes 294928 | tf_op jit(solution)/shard_map/reduce_scatter | solution.py:1735
  657.6 1.8 convert_bitcast_fusion
  659.4 1.8 copy.66
  661.2 0.9 copy-done.2
  662.2 1.2 copy.67
  (75 shorter events, 11.7 us)
Async XLA Ops:
  7.2 4.7 copy-start.5
  7.2 124.9 %all-gather.3.cloned.1.call-start = ((), (), s32[]{:S(2)}) async-start(), calls=%async_computation.4 | async-start | bytes 1474560 | tf_op jit(solution)/shard_map/all_gather | solution.py:1629
  7.9 618.9 %reduce-scatter.3.cloned.1.call-start = ((), (), s32[]{:S(2)}) async-start(), calls=%async_computation.2 | async-start | bytes 21233664 | tf_op jit(solution)/shard_map/reduce_scatter | solution.py:1680
  11.9 2.6 copy-start.4
  16.7 100.5 %copy-start.13 = (bf16[2,1536]{1,0:T(2,128)(2,1)S(1)}, bf16[2,1536]{1,0:T(2,128)(2,1)}, u32[]{:S(2)}) copy-start(bf16[2,1536]{1,0:T(2,128)(2,1)} %param.27) | copy-start | bytes 18436
  16.7 101.1 %copy-start.7 = (bf16[1,77,1536]{2,1,0:T(8,128)(2,1)S(1)}, bf16[1,77,1536]{2,1,0:T(8,128)(2,1)}, u32[]{:S(2)}) copy-start(bf16[1,77,1536]{2,1,0:T(8,128)(2,1)} %param.31) | copy-start | bytes 709636
  16.7 101.2 %copy-start.6 = (bf16[1,256,1536]{2,1,0:T(8,128)(2,1)S(1)}, bf16[1,256,1536]{2,1,0:T(8,128)(2,1)}, u32[]{:S(2)}) copy-start(bf16[1,256,1536]{2,1,0:T(8,128)(2,1)} %param.30) | copy-start | bytes 2359300
  378.1 0.9 copy-start.3
  378.1 279.5 %reduce-scatter.5.cloned.1.call-start = ((), (), s32[]{:S(2)}) async-start(), calls=%async_computation.3 | async-start | bytes 1474560 | tf_op jit(solution)/shard_map/reduce_scatter | solution.py:1735
  437.6 55.9 %copy-start.10 = (f32[2,1536]{1,0:T(2,128)S(1)}, f32[2,1536]{1,0:T(2,128)}, u32[]{:S(2)}) copy-start(f32[2,1536]{1,0:T(2,128)} %get-tuple-element.105) | copy-start | bytes 36868
  437.6 56.6 %copy-start.9 = (f32[4,1536]{1,0:T(4,128)S(1)}, f32[4,1536]{1,0:T(4,128)}, u32[]{:S(2)}) copy-start(f32[4,1536]{1,0:T(4,128)} %get-tuple-element.76) | copy-start | bytes 73732
  437.6 56.6 %copy-start.11 = (f32[2,1536]{1,0:T(2,128)S(1)}, f32[2,1536]{1,0:T(2,128)}, u32[]{:S(2)}) copy-start(f32[2,1536]{1,0:T(2,128)} %get-tuple-element.102) | copy-start | bytes 36868
  628.8 12.5 %copy-start.12 = (f32[8,1,256]{2,1,0:T(1,128)S(1)}, f32[8,1,256]{2,1,0:T(1,128)}, u32[]{:S(2)}) copy-start(f32[8,1,256]{2,1,0:T(1,128)} %get-tuple-element.114) | copy-start | bytes 24580
  628.8 12.7 %copy-start.8 = (bf16[1,1536]{1,0:T(2,128)(2,1)S(1)}, bf16[1,1536]{1,0:T(2,128)(2,1)}, u32[]{:S(2)}) copy-start(bf16[1,1536]{1,0:T(2,128)(2,1)} %cond_ref.1) | copy-start | bytes 9220
  628.9 13.3 %copy-start.1 = (bf16[768,1536]{1,0:T(8,128)(2,1)S(1)}, bf16[768,1536]{1,0:T(8,128)(2,1)}, u32[]{:S(2)}) copy-start(bf16[768,1536]{1,0:T(8,128)(2,1)} %reduce-scatter.3.cloned.1.call-done) | copy-start | bytes 7077892
  644.5 14.9 %copy-start = (f32[192,2,2304]{2,1,0:T(2,128)S(1)}, f32[192,2,2304]{2,1,0:T(2,128)}, u32[]{:S(2)}) copy-start(f32[192,2,2304]{2,1,0:T(2,128)} %get-tuple-element.213) | copy-start | bytes 10616836
  659.4 2.8 copy-start.2
Sparse Core Ops, SparseCore 0:
  9.6 44.4 all-gather.2
  378.3 130.9 reduce-scatter.2
  627.0 30.5 reduce-scatter.4

commit v7 on v6

--- a/solution.py
+++ b/solution.py
@@ -1266,8 +1266,8 @@
 
 
 def middle_back_kernel(
-    n, img, part_ref, prev_ref, m_ref, y_ref, e_ref, w_ref, mod_ref, dm_ref, dy_ref, sum_ref, all_ref,
-    db_ref, mix, send, recv, local, *line_scratch,
+    n, img, part_ref, prev_ref, m_ref, y_ref, e_ref, w_far, mod_ref, dm_ref, dy_ref, sum_ref, all_ref,
+    db_ref, mix, send, recv, local, w_ref, w_sem, *line_scratch,
 ):
     me = lax.axis_index("seq")
     rows, width = m_ref.shape
@@ -1276,6 +1276,8 @@
     greet(n, "all")
     line = LineSum(n, at_rows(part_ref), db_ref, *line_scratch, first=n - 2, prev=prev_ref)
     line.round(n - 2)
+    weights = pltpu.make_async_copy(w_far, w_ref, w_sem)
+    weights.start()
     if mix.shape[2] > heads:
         mix[...] = jnp.zeros_like(mix)
     line.finish()
@@ -1308,6 +1310,7 @@
         )
 
     keep = pltpu.make_async_copy(mix.at[me], all_ref.at[me], local)
+    weights.wait()
     for peer in range(n):
         for t, sl in streams:
             mix[peer, sl, :heads] = nn_dot(dy_ref[sl], proj_columns(w_ref, peer, t)).astype(HALF)
@@ -1335,7 +1338,7 @@
     anywhere = pl.BlockSpec(memory_space=pl.ANY)
     return pl.pallas_call(
         functools.partial(middle_back_kernel, n, img),
-        in_specs=[anywhere, anywhere] + [inner] * 5,
+        in_specs=[anywhere, anywhere] + [inner] * 3 + [anywhere, inner],
         out_specs=[inner, inner, inner, anywhere],
         out_shape=[
             jax.ShapeDtypeStruct((rows, width), SINGLE),
@@ -1348,6 +1351,8 @@
             pltpu.VMEM((n, rows, lwp), HALF),
             pltpu.SemaphoreType.DMA((n,)),
             pltpu.SemaphoreType.DMA((n,)),
+            pltpu.SemaphoreType.DMA,
+            pltpu.VMEM(weight.shape, HALF),
             pltpu.SemaphoreType.DMA,
         ]
         + LineSum.scratch(n, rows, width, first=n - 2),

time: 675 us -> 668 us (0.990)
  Pallas kernels: 605 us -> 597 us
    pallas_call x1, Pallas kernels: 94.7 us -> 86.4 us  [end(): pl.pallas_call(functools.partial(end_kernel, n, dp, cut), in_specs=[anywh...]
  transfers between devices with their start and end apart: 3 -> 3, of which waited for: 1 -> 1; matrix products, arithmetic and copies ran while one was open for 5% -> 5% of each run, Pallas kernels for 54% -> 53%
where the time goes in v7:
time: 668 us; the launch traced here: 663 us
  Pallas kernels  597 us (89%)
  local copies, waits for them, and re-layouts  28.2 us (4%)
  between operations  14.9 us (2%)
  other arithmetic  11.3 us (2%)
  waiting for transfers between devices  10.6 us (2%)
    pallas_call x1, Pallas kernels, start(): pl.pallas_call(functools.partial(start_kernel, n, dp), in_specs=[inner] *...  97.5 us
    pallas_call x1, Pallas kernels, end(): pl.pallas_call(functools.partial(end_kernel, n, dp, cut), in_specs=[anywh...  86.4 us
    pallas_call x1, Pallas kernels, middle_rows(): pl.pallas_call(functools.partial(middle_kernel, n, img), in_specs=[inner]...  82.4 us
    pallas_call x1, Pallas kernels, feed_forward(): pl.pallas_call(functools.partial(mlp_kernel, n, img, tile), grid=(n,), in...  61.7 us
    pallas_call x1, Pallas kernels, attend_back(): pl.pallas_call(functools.partial(attn_back_kernel, n, img, pairs), grid=(...  58.7 us
    pallas_call x1, Pallas kernels, weight_grads(): pl.pallas_call(functools.partial(grads_kernel, n, img, plan, rounds), gri...  53.2 us
    pallas_call x1, Pallas kernels, middle_back(): pl.pallas_call(functools.partial(middle_back_kernel, n, img), in_specs=[a...  51.3 us
    pallas_call x1, Pallas kernels, attend(): pl.pallas_call(functools.partial(attn_kernel, n), grid=(pairs, n), in_spe...  48.7 us
  transfers between devices with their start and end apart: 3, of which 1 were waited for; matrix products, arithmetic and copies ran while one was open for 5% of the time, Pallas kernels for 53%

profile of v7, /device:TPU:0, one launch (start us, length us, event | category | flops | bytes accessed | tf_op | source)
XLA Modules:
  0.0 662.6 jit_solution(13048105080541356250)
XLA Ops:
  8.0 0.8 fusion.13
  8.7 2.3 fusion.2.x_ref
  12.5 2.0 reshape_reshape.6.qkv_ref
  14.4 1.7 reshape_reshape.7.fc1_ref
  16.7 97.5 %start.1 = (bf16[4,336,1536]{2,1,0:T(8,128)(2,1)}, f32[4,1,6272]{2,1,0:T(1,128)}, f32[8,1,256]{2,1,0:T(1,128)}, f32[2,8,1536]{2,1,0:T(8,128)}, f32[4,1536]{1,0:T...) custom-call(bf16[336,1536]{1,0:T(8,128)(2,1)} %fusion.2.x_ref, bf16[1,1536]{1,0:T(2,128)(2,1)} %cond_ref.1, ...), custom_call_target="tpu_custom_call" | custom-call | flops 1000000 | bytes 104857600 | tf_op jit(solution)/shard_map/start/pallas_call | solution.py:641
  114.3 0.8 slice_reduce_fusion.1
  115.9 1.3 slice.100.b_ref
  117.9 1.0 fusion.3.e_ref.e_loc
  118.9 13.2 %project_qkv.1 = (bf16[4,336,1536]{2,1,0:T(8,128)(2,1)}, bf16[4,336,1152]{2,1,0:T(8,128)(2,1)}) custom-call(bf16[4,336,1536]{2,1,0:T(8,128)(2,1)} %get-tuple-element.68.x_ref, f32[2,8,1536]{2,1,0:T(8,128)} %get-tuple-element.69.mod_ref, bf16[1536,2304]{1,0:T(8,128)(2,1)} %bitcast.76, f32[2,1152]{1,0:T(2,128)} %bitcast.72), custom_call_target="tpu_custom_call" | custom-call | flops 4756340736 | bytes 31457280 | tf_op jit(solution)/shard_map/project_qkv/pallas_call | solution.py:689
  132.1 48.7 %attend.1 = (bf16[4,336,384]{2,1,0:T(8,128)(2,1)}, f32[4,336,384]{2,1,0:T(8,128)}, bf16[2,336,1536]{2,1,0:T(8,128)(2,1)}, bf16[336,1536]{1,0:T(8,128)(2,1)}, bf16[8,2,768,384]{3,2,1,0:T(8,128)(2,1)}) custom-call(bf16[4,336,1152]{2,1,0:T(8,128)(2,1)} %get-tuple-element.71.q_ref.k_ref.v_ref, bf16[4,336,1152]{2,1,0:T(8,128)(2,1)} %get-tuple-element.71.q_ref.k_ref.v_ref, ...), custom_call_target="tpu_custom_call" | custom-call | flops 11098128384 | bytes 20971520 | tf_op jit(solution)/shard_map/attend/pallas_call | solution.py:799
  180.8 82.4 %middle_rows.1 = (f32[336,1536]{1,0:T(8,128)}, f32[336,1536]{1,0:T(8,128)}, bf16[4,336,1536]{2,1,0:T(8,128)(2,1)}, bf16[8,2,192,1536]{3,2,1,0:T(8,128)(2,1)}) custom-call(bf16[336,1536]{1,0:T(8,128)(2,1)} %get-tuple-element.74.mix_ref.r_ref, bf16[336,1536]{1,0:T(8,128)(2,1)} %fusion.2.x_ref, bf16[8,4,2,192,384]{4,3,2,1,0:T(8,128)(2,1)} %bitcast.56, ...), custom_call_target="tpu_custom_call" | custom-call | flops 1585446912 | bytes 104857600 | tf_op jit(solution)/shard_map/middle_rows/pallas_call | solution.py:1023
  263.2 61.7 %feed_forward.1 = (bf16[4,336,1536]{2,1,0:T(8,128)(2,1)}, bf16[4,336,1536]{2,1,0:T(8,128)(2,1)}, bf16[4,336,1536]{2,1,0:T(8,128)(2,1)}, bf16[4,336,1536]{2,1,0:T...) custom-call(bf16[4,336,1536]{2,1,0:T(8,128)(2,1)} %get-tuple-element.77.b_ref.refs_0_, ...), custom_call_target="tpu_custom_call" | custom-call | flops 19025362944 | bytes 52428800 | tf_op jit(solution)/shard_map/feed_forward/pallas_call | solution.py:1148
  324.9 53.2 %fc_grads.1 = (bf16[8,4,192,1536]{3,2,1,0:T(8,128)(2,1)}, bf16[2,336,1536]{2,1,0:T(8,128)(2,1)}) custom-call(bf16[4,336,1536]{2,1,0:T(8,128)(2,1)} %get-tuple-element.77.b_ref.refs_0_, bf16[4,336,1536]{2,1,0:T(8,128)(2,1)} %get-tuple-element.82.refs_1_, bf16[4,336,1536]{2,1,0:T(8,128)(2,1)} %get-tuple-element.83.refs_2_, ...), custom_call_target="tpu_custom_call" | custom-call | flops 12683575296 | bytes 62914560 | tf_op jit(solution)/shard_map/fc_grads/pallas_call | solution.py:1249
  378.2 0.8 copy-done.3
  379.1 51.3 %middle_back.1 = (f32[336,1536]{1,0:T(8,128)}, bf16[336,1536]{1,0:T(8,128)(2,1)}, f32[2,8,1536]{2,1,0:T(8,128)}, bf16[4,336,384]{2,1,0:T(8,128)(2,1)}) custom-call(bf16[4,336,1536]{2,1,0:T(8,128)(2,1)} %get-tuple-element.81.refs_4_.part_ref, bf16[2,336,1536]{2,1,0:T(8,128)(2,1)} %get-tuple-element.85.prev_ref, f32[336,1536]{1,0:T(8,128)} %get-tuple-element.86.m_ref, ...), custom_call_target="tpu_custom_call" | custom-call | flops 1585446912 | bytes 62914560 | tf_op jit(solution)/shard_map/middle_back/pallas_call | solution.py:1339
  430.4 1.0 copy.55
  431.4 0.9 slice.101
  432.3 1.1 broadcast_in_dim.39.mask_ref
  433.4 58.7 %attend_back.1 = (bf16[4,336,384]{2,1,0:T(8,128)(2,1)}, bf16[4,336,384]{2,1,0:T(8,128)(2,1)}, bf16[4,336,384]{2,1,0:T(8,128)(2,1)}, f32[3,2,128]{2,1,0:T(2,128)}...) custom-call(bf16[4,336,1152]{2,1,0:T(8,128)(2,1)} %get-tuple-element.71.q_ref.k_ref.v_ref, ...), custom_call_target="tpu_custom_call" | custom-call | flops 27745320960 | bytes 31457280 | tf_op jit(solution)/shard_map/attend_back/pallas_call | solution.py:941
  494.1 37.2 %attn_in_back.1 = (bf16[4,336,1536]{2,1,0:T(8,128)(2,1)}, f32[2,2,1536]{2,1,0:T(2,128)}, bf16[1536,2304]{1,0:T(8,128)(2,1)}, f32[336,1536]{1,0:T(8,128)}) custom-call(bf16[4,336,384]{2,1,0:T(8,128)(2,1)} %get-tuple-element.92.dq_ref, bf16[4,336,384]{2,1,0:T(8,128)(2,1)} %get-tuple-element.93.dk_ref, bf16[4,336,384]{2,1,0:T(8,128)(2,1)} %get-tuple-element.94.dv_ref, ...), custom_call_target="tpu_custom_call" | custom-call | flops 9512681472 | bytes 31457280 | tf_op jit(solution)/shard_map/attn_in_back/pallas_call | solution.py:1414
  531.3 0.8 pad_maximum_fusion
  532.9 86.4 %end.1 = (f32[336,1536]{1,0:T(8,128)}, f32[192,3,2,384]{3,2,1,0:T(2,128)}, bf16[2,768,384]{2,1,0:T(8,128)(2,1)}, f32[8,1,10752]{2,1,0:T(1,128)}, f32[8,1,256]{2,1,0:T(1,128)}, /*index=5*/f32[192,2,2304]{2,1,0:T(2,128)}) custom-call(bf16[4,336,1536]{2,1,0:T(8,128)(2,1)} %get-tuple-element.97.parts, bf16[8,2,96,2304]{3,2,1,0:T(8,128)(2,1)} %bitcast.60, ...), custom_call_target="tpu_custom_call" | custom-call | flops 1000000 | bytes 104857600 | tf_op jit(solution)/shard_map/end/pallas_call | solution.py:1524
  620.0 1.2 reduce_sum.9
  621.3 7.2 %rows_out.1 = (bf16[1,256,1536]{2,1,0:T(8,128)(2,1)}, bf16[1,77,1536]{2,1,0:T(8,128)(2,1)}, f32[1,256,1536]{2,1,0:T(8,128)}, f32[1,77,1536]{2,1,0:T(8,128)}) custom-call(f32[336,1536]{1,0:T(8,128)} %get-tuple-element.107.da_ref, f32[336,1536]{1,0:T(8,128)} %get-tuple-element.108.dm_ref, bf16[336,1536]{1,0:T(8,128)(2,1)} %fusion.2.x_ref, ...), custom_call_target="tpu_custom_call" | custom-call | flops 1000000 | bytes 14680064 | tf_op jit(solution)/shard_map/rows_out/pallas_call | solution.py:1569
  628.6 2.3 copy.60
  635.2 1.7 slice_bitcast_fusion
  637.0 3.2 copy.61
  640.2 9.9 %reduce-scatter.5.cloned.1.call-done = bf16[384,384]{1,0:T(8,128)(2,1)} async-done(((bf16[1536,384]{1,0:T(8,128)(2,1)}), bf16[384,384]{1,0:T(8,128)(2,1)}) %reduce-scatter.5.cloned.1.call-update) | async-done | bytes 294928 | tf_op jit(solution)/shard_map/reduce_scatter | solution.py:1740
  650.1 1.8 convert_bitcast_fusion
  651.9 1.8 copy.66
  653.7 0.9 copy-done.2
  654.7 1.2 copy.67
  (75 shorter events, 11.7 us)
Async XLA Ops:
  7.2 4.7 copy-start.5
  7.2 124.9 %all-gather.3.cloned.1.call-start = ((), (), s32[]{:S(2)}) async-start(), calls=%async_computation.4 | async-start | bytes 1474560 | tf_op jit(solution)/shard_map/all_gather | solution.py:1634
  7.9 611.4 %reduce-scatter.3.cloned.1.call-start = ((), (), s32[]{:S(2)}) async-start(), calls=%async_computation.2 | async-start | bytes 21233664 | tf_op jit(solution)/shard_map/reduce_scatter | solution.py:1685
  11.9 2.6 copy-start.4
  16.7 100.5 %copy-start.13 = (bf16[2,1536]{1,0:T(2,128)(2,1)S(1)}, bf16[2,1536]{1,0:T(2,128)(2,1)}, u32[]{:S(2)}) copy-start(bf16[2,1536]{1,0:T(2,128)(2,1)} %param.27) | copy-start | bytes 18436
  16.7 101.1 %copy-start.7 = (bf16[1,77,1536]{2,1,0:T(8,128)(2,1)S(1)}, bf16[1,77,1536]{2,1,0:T(8,128)(2,1)}, u32[]{:S(2)}) copy-start(bf16[1,77,1536]{2,1,0:T(8,128)(2,1)} %param.31) | copy-start | bytes 709636
  16.7 101.2 %copy-start.6 = (bf16[1,256,1536]{2,1,0:T(8,128)(2,1)S(1)}, bf16[1,256,1536]{2,1,0:T(8,128)(2,1)}, u32[]{:S(2)}) copy-start(bf16[1,256,1536]{2,1,0:T(8,128)(2,1)} %param.30) | copy-start | bytes 2359300
  378.1 0.9 copy-start.3
  378.1 271.9 %reduce-scatter.5.cloned.1.call-start = ((), (), s32[]{:S(2)}) async-start(), calls=%async_computation.3 | async-start | bytes 1474560 | tf_op jit(solution)/shard_map/reduce_scatter | solution.py:1740
  433.4 59.5 %copy-start.10 = (f32[2,1536]{1,0:T(2,128)S(1)}, f32[2,1536]{1,0:T(2,128)}, u32[]{:S(2)}) copy-start(f32[2,1536]{1,0:T(2,128)} %get-tuple-element.105) | copy-start | bytes 36868
  433.4 60.1 %copy-start.9 = (f32[4,1536]{1,0:T(4,128)S(1)}, f32[4,1536]{1,0:T(4,128)}, u32[]{:S(2)}) copy-start(f32[4,1536]{1,0:T(4,128)} %get-tuple-element.76) | copy-start | bytes 73732
  433.4 60.1 %copy-start.11 = (f32[2,1536]{1,0:T(2,128)S(1)}, f32[2,1536]{1,0:T(2,128)}, u32[]{:S(2)}) copy-start(f32[2,1536]{1,0:T(2,128)} %get-tuple-element.102) | copy-start | bytes 36868
  621.3 12.5 %copy-start.12 = (f32[8,1,256]{2,1,0:T(1,128)S(1)}, f32[8,1,256]{2,1,0:T(1,128)}, u32[]{:S(2)}) copy-start(f32[8,1,256]{2,1,0:T(1,128)} %get-tuple-element.114) | copy-start | bytes 24580
  621.3 12.7 %copy-start.8 = (bf16[1,1536]{1,0:T(2,128)(2,1)S(1)}, bf16[1,1536]{1,0:T(2,128)(2,1)}, u32[]{:S(2)}) copy-start(bf16[1,1536]{1,0:T(2,128)(2,1)} %cond_ref.1) | copy-start | bytes 9220
  621.3 13.3 %copy-start.1 = (bf16[768,1536]{1,0:T(8,128)(2,1)S(1)}, bf16[768,1536]{1,0:T(8,128)(2,1)}, u32[]{:S(2)}) copy-start(bf16[768,1536]{1,0:T(8,128)(2,1)} %reduce-scatter.3.cloned.1.call-done) | copy-start | bytes 7077892
  637.0 14.9 %copy-start = (f32[192,2,2304]{2,1,0:T(2,128)S(1)}, f32[192,2,2304]{2,1,0:T(2,128)}, u32[]{:S(2)}) copy-start(f32[192,2,2304]{2,1,0:T(2,128)} %get-tuple-element.213) | copy-start | bytes 10616836
  651.9 2.8 copy-start.2
Sparse Core Ops, SparseCore 0:
  9.6 44.4 all-gather.2
  378.3 130.9 reduce-scatter.2
  619.5 30.5 reduce-scatter.4
